TPU v7x, 32 devices: a whole 2x2x4 slice. The times are simulated.
32 devices in a mesh: ep: 8 (over y, x, core), hs: 4 (over z).
Axes of the slice: x: 2, y: 2, z: 4, core: 2. Of those that a mesh axis runs over, the one named last changes fastest.
Arguments:
- tokens: bfloat16 [4096, 1280], P('ep'), may hold values from -6 to 6
- attn_gain: float32 [1280], replicated, may hold values from 0.5 to 1.5
- attn_query: bfloat16 [1280, 1280], P(None, 'hs'), may hold values from -0.15625 to 0.15625
- attn_key: bfloat16 [1280, 1280], P(None, 'hs'), may hold values from -0.15625 to 0.15625
- attn_value: bfloat16 [1280, 1280], P(None, 'hs'), may hold values from -0.15625 to 0.15625
- attn_out: bfloat16 [1280, 1280], P(None, 'hs'), may hold values from -0.625 to 0.625
- ffn_gain: float32 [1280], replicated, may hold values from 0.5 to 1.5
- router: bfloat16 [1280, 64], replicated, may hold values from -0.078125 to 0.078125
- shared_gate: bfloat16 [1280, 1792], P(None, 'hs'), may hold values from -0.15625 to 0.15625
- shared_up: bfloat16 [1280, 1792], P(None, 'hs'), may hold values from -0.15625 to 0.15625
- shared_down: bfloat16 [1792, 1280], P('hs'), may hold values from -0.125 to 0.125
- expert_gate: bfloat16 [64, 1280, 896], P('ep', None, 'hs'), may hold values from -0.15625 to 0.15625
- expert_up: bfloat16 [64, 1280, 896], P('ep', None, 'hs'), may hold values from -0.15625 to 0.15625
- expert_down: bfloat16 [64, 896, 1280], P('ep', 'hs'), may hold values from -6 to 6
- routes: int32 [4096, 7], P('ep'), may hold values from 0 to 63, all different within a row; in each aligned block of 512 rows (0 to 511, 512 to 1023, ...) at most 112 rows name the same one
- documents: int32 [8, 512], P('ep'), may hold values from 0 to 3, never falling along the last dimension, each value on 1 to 256 neighbouring positions
- out_grad: bfloat16 [4096, 1280], P('ep', 'hs'), may hold values from -6 to 6
Outputs:
- output: bfloat16 [4096, 1280], P('ep', 'hs')
- grad_tokens: float32 [4096, 1280], P('ep', 'hs')
- grad_attn_gain: float32 [1280], replicated
- grad_attn_query: float32 [1280, 1280], P(None, 'hs')
- grad_attn_key: float32 [1280, 1280], P(None, 'hs')
- grad_attn_value: float32 [1280, 1280], P(None, 'hs')
- grad_attn_out: float32 [1280, 1280], P(None, 'hs')
- grad_ffn_gain: float32 [1280], replicated
- grad_router: float32 [1280, 64], replicated
- grad_shared_gate: float32 [1280, 1792], P(None, 'hs')
- grad_shared_up: float32 [1280, 1792], P(None, 'hs')
- grad_shared_down: float32 [1792, 1280], P('hs')
- grad_expert_gate: float32 [64, 1280, 896], P('ep', None, 'hs')
- grad_expert_up: float32 [64, 1280, 896], P('ep', None, 'hs')
- grad_expert_down: float32 [64, 896, 1280], P('ep', 'hs')
Inputs may be any that keep to these rules, and one draw needn't show every extreme that they name: `routes`: each row names 7 different experts and every expert is named by some row; the 512 rows of one sequence name any one expert at most 112 times, and in every draw the rows of some sequence name some expert exactly 112 times. `documents`: within each sequence the document number never falls; each document spans 1 to half of 512 positions.
All inputs are finite; a program needn't handle non-finite values.
Results may differ from a plain program's by a relative error of at most 0.02.
Values may be sent and summed in bfloat16 or wider, within the bound.
A program may use at most 448 MiB of HBM per device.

v0:
```python
import math

import jax
import jax.numpy as jnp
from jax import lax
from jax.sharding import PartitionSpec as P

HEADS = 10
HEAD_DIM = 128
CAP = 112


epsilon = 1e-06


def rms_norm(values, gain_vec):
    inverse_rms = lax.rsqrt(jnp.mean(values * values, axis=-1, keepdims=True) + epsilon)
    return values * inverse_rms * gain_vec


def rotary(head_values):
    half_dim = head_values.shape[-1] // 2
    frequency = 10000.0 ** (-jnp.arange(half_dim, dtype=jnp.float32) * 2.0 / head_values.shape[-1])
    angles = jnp.arange(head_values.shape[0], dtype=jnp.float32)[:, None] * frequency[None, :]
    cosine = jnp.cos(angles)[:, None, :]
    sine_table = jnp.sin(angles)[:, None, :]
    lower_half = head_values[..., :half_dim]
    upper_half = head_values[..., half_dim:]
    return jnp.concatenate(
        [
            lower_half * cosine - upper_half * sine_table,
            upper_half * cosine + lower_half * sine_table,
        ],
        axis=-1,
    )


def swiglu(gate_in, up_in):
    return jax.nn.silu(gate_in) * up_in


def product(left, right):
    return jnp.dot(left, right, preferred_element_type=jnp.float32)


def shards(
    tokens,
    attn_gain,
    attn_query,
    attn_key,
    attn_value,
    attn_out,
    ffn_gain,
    router,
    shared_gate,
    shared_up,
    shared_down,
    expert_gate,
    expert_up,
    expert_down,
    routes,
    documents,
    out_grad,
):
    tok_count = tokens.shape[0]
    model_width = tokens.shape[1]
    quarter = out_grad.shape[1]
    ep_count = lax.axis_size("ep")
    column_start = lax.axis_index("hs") * quarter
    local_experts = expert_gate.shape[0]
    experts_all = router.shape[1]
    topk = routes.shape[1]
    bf16 = jnp.bfloat16
    f32 = jnp.float32
    full_query, full_key, full_value, full_out = (
        lax.all_gather(attn_query, "hs", axis=1, tiled=True),
        lax.all_gather(attn_key, "hs", axis=1, tiled=True),
        lax.all_gather(attn_value, "hs", axis=1, tiled=True),
        lax.all_gather(attn_out, "hs", axis=1, tiled=True),
    )
    x_float = tokens.astype(f32)
    normed1 = rms_norm(x_float, attn_gain).astype(bf16)
    head_shape = (tok_count, HEADS, HEAD_DIM)
    query_pre = product(normed1, full_query).reshape(head_shape)
    key_pre = product(normed1, full_key).reshape(head_shape)
    values_low = product(normed1, full_value).astype(bf16).reshape(head_shape)
    queries_low = rotary(query_pre).astype(bf16)
    keys_low = rotary(key_pre).astype(bf16)
    score_scale = 1.0 / math.sqrt(HEAD_DIM)
    positions = jnp.arange(tok_count, dtype=jnp.int32)
    doc_row = documents[0]
    allowed = (positions[:, None] >= positions[None, :]) & (doc_row[:, None] == doc_row[None, :])
    scores = (
        jnp.einsum("qhd,khd->hqk", queries_low, keys_low, preferred_element_type=f32) * score_scale
    )
    scores = jnp.where(allowed[None], scores, -1e30)
    row_max = jnp.max(scores, axis=-1, keepdims=True)
    log_total = row_max + jnp.log(jnp.sum(jnp.exp(scores - row_max), axis=-1, keepdims=True))
    prob_values = jnp.exp(scores - log_total)
    probs_low = prob_values.astype(bf16)
    attended = jnp.einsum("hqk,khd->qhd", probs_low, values_low, preferred_element_type=f32)
    attended = attended.reshape(tok_count, model_width).astype(bf16)
    residual = x_float + product(attended, full_out)
    normed2 = rms_norm(residual, ffn_gain).astype(bf16)
    logits = product(normed2, router)
    gate_probs = jax.nn.softmax(logits, axis=-1)
    selector = (
        routes[:, :, None] == jnp.arange(experts_all, dtype=jnp.int32)[None, None, :]
    ).astype(f32)
    weight = jnp.sum(selector * gate_probs[:, None, :], axis=-1)
    sh_gate = product(normed2, shared_gate)
    sh_up = product(normed2, shared_up)
    sh_hidden = swiglu(sh_gate, sh_up).astype(bf16)
    shared_part = product(sh_hidden, shared_down)
    flat_routes = routes.reshape(tok_count * topk)
    onehot = (flat_routes[:, None] == jnp.arange(experts_all, dtype=jnp.int32)[None, :]).astype(
        jnp.int32
    )
    slot_index = jnp.sum((jnp.cumsum(onehot, axis=0) - onehot) * onehot, axis=1)
    dest_rows = flat_routes * CAP + slot_index
    send_rows = (
        jnp.zeros((experts_all * CAP, model_width), bf16)
        .at[dest_rows]
        .set(jnp.repeat(normed2, topk, axis=0))
        .reshape(experts_all, CAP, model_width)
    )
    gate_w, up_w, down_w = (expert_gate, expert_up, expert_down)
    slots_used = CAP
    received = lax.all_to_all(
        send_rows.reshape(ep_count, local_experts * slots_used, model_width),
        "ep",
        split_axis=0,
        concat_axis=0,
        tiled=True,
    ).reshape(ep_count, local_experts, slots_used, model_width)
    ex_gate = jnp.einsum("secd,edf->secf", received, gate_w, preferred_element_type=f32)
    ex_up = jnp.einsum("secd,edf->secf", received, up_w, preferred_element_type=f32)
    ex_hidden = swiglu(ex_gate, ex_up).astype(bf16)
    ex_part = jnp.einsum("secf,efd->secd", ex_hidden, down_w, preferred_element_type=f32)
    ex_quarter, shared_quarter = (
        lax.psum_scatter(
            ex_part.reshape(ep_count * local_experts * CAP, model_width),
            "hs",
            scatter_dimension=1,
            tiled=True,
        ),
        lax.psum_scatter(shared_part, "hs", scatter_dimension=1, tiled=True),
    )
    ex_send = ex_quarter.astype(bf16)
    send_width = ex_send.shape[-1]
    returned = lax.all_to_all(
        ex_send.reshape(ep_count, local_experts * slots_used, send_width),
        "ep",
        split_axis=0,
        concat_axis=0,
        tiled=True,
    )
    returned = returned.reshape(experts_all * CAP, quarter)
    picked = returned[dest_rows].reshape(tok_count, topk, quarter).astype(f32)
    routed_quarter = jnp.sum(weight[:, :, None] * picked, axis=1)
    residual_quarter = lax.dynamic_slice_in_dim(residual, column_start, quarter, 1)
    output = (residual_quarter + shared_quarter + routed_quarter).astype(bf16)
    grad_full = lax.all_gather(out_grad, "hs", axis=1, tiled=True)
    grad_float = grad_full.astype(f32)
    grad_rows = (
        (weight[:, :, None] * grad_float[:, None, :])
        .astype(bf16)
        .reshape(tok_count * topk, model_width)
    )
    send_grads = jnp.zeros((experts_all * CAP, model_width), bf16).at[dest_rows].set(grad_rows)
    send_grads = send_grads.reshape(experts_all, CAP, model_width)
    grad_received = lax.all_to_all(
        send_grads.reshape(ep_count, local_experts * slots_used, model_width),
        "ep",
        split_axis=0,
        concat_axis=0,
        tiled=True,
    ).reshape(ep_count, local_experts, slots_used, model_width)
    down_grad_part = jnp.einsum(
        "secf,secd->efd", ex_hidden, grad_received, preferred_element_type=f32
    )
    grad_ex_hidden = jnp.einsum("secd,efd->secf", grad_received, down_w, preferred_element_type=f32)
    ignored, pullback = jax.vjp(swiglu, ex_gate, ex_up)
    grad_ex_gate, grad_ex_up = pullback(grad_ex_hidden)
    grad_ex_gate = grad_ex_gate.astype(bf16)
    grad_ex_up = grad_ex_up.astype(bf16)
    gate_grad_part = jnp.einsum(
        "secd,secf->edf", received, grad_ex_gate, preferred_element_type=f32
    )
    up_grad_part = jnp.einsum("secd,secf->edf", received, grad_ex_up, preferred_element_type=f32)
    row_grads = jnp.einsum(
        "secf,edf->secd", grad_ex_gate, gate_w, preferred_element_type=f32
    ) + jnp.einsum("secf,edf->secd", grad_ex_up, up_w, preferred_element_type=f32)
    grad_expert_gate, grad_expert_up, grad_expert_down = (
        gate_grad_part,
        up_grad_part,
        down_grad_part,
    )
    grad_sh_hidden = jnp.einsum("td,fd->tf", grad_full, shared_down, preferred_element_type=f32)
    ignored, pullback = jax.vjp(swiglu, sh_gate, sh_up)
    grad_sh_gate, grad_sh_up = pullback(grad_sh_hidden)
    grad_sh_gate = grad_sh_gate.astype(bf16)
    grad_sh_up = grad_sh_up.astype(bf16)
    grad_shared_down = jnp.einsum("tf,td->fd", sh_hidden, grad_full, preferred_element_type=f32)
    grad_shared_gate = jnp.einsum("td,tf->df", normed2, grad_sh_gate, preferred_element_type=f32)
    grad_shared_up = jnp.einsum("td,tf->df", normed2, grad_sh_up, preferred_element_type=f32)
    normed_part = jnp.einsum(
        "tf,df->td", grad_sh_gate, shared_gate, preferred_element_type=f32
    ) + jnp.einsum("tf,df->td", grad_sh_up, shared_up, preferred_element_type=f32)
    own_grad = out_grad.astype(f32)
    weight_part = jnp.sum(own_grad[:, None, :] * picked, axis=2)
    back_rows = lax.all_to_all(
        row_grads.reshape(ep_count, local_experts * slots_used, model_width),
        "ep",
        split_axis=0,
        concat_axis=0,
        tiled=True,
    ).reshape(experts_all, slots_used, model_width)
    back_rows = back_rows.reshape(experts_all * CAP, model_width)
    routed_part = jnp.sum(back_rows[dest_rows].reshape(tok_count, topk, model_width), axis=1)
    normed_total, weight_grad = lax.psum((normed_part + routed_part, weight_part), "hs")
    grad_probs = jnp.sum(selector * weight_grad[:, :, None], axis=1)
    logit_grads = (
        gate_probs * (grad_probs - jnp.sum(grad_probs * gate_probs, axis=-1, keepdims=True))
    ).astype(bf16)
    grad_router = jnp.einsum("td,te->de", normed2, logit_grads, preferred_element_type=f32)
    normed_total = normed_total + jnp.einsum(
        "te,de->td", logit_grads, router, preferred_element_type=f32
    )
    ignored, pullback = jax.vjp(rms_norm, residual, ffn_gain)
    residual_norm_grad, grad_ffn_gain = pullback(normed_total)
    residual_grad = grad_float + residual_norm_grad
    residual_low = residual_grad.astype(bf16)
    residual_low_quarter = lax.dynamic_slice_in_dim(residual_low, column_start, quarter, 1)
    grad_out_part = jnp.einsum(
        "td,tc->dc", attended, residual_low_quarter, preferred_element_type=f32
    )
    attended_grad = jnp.einsum("tc,dc->td", residual_low, full_out, preferred_element_type=f32)
    attended_grad = attended_grad.astype(bf16).reshape(head_shape)
    prob_grads = jnp.einsum("qhd,khd->hqk", attended_grad, values_low, preferred_element_type=f32)
    value_grads = jnp.einsum(
        "hqk,qhd->khd", probs_low, attended_grad, preferred_element_type=f32
    ).astype(bf16)
    score_grads = (
        prob_values * (prob_grads - jnp.sum(prob_values * prob_grads, axis=-1, keepdims=True))
    ).astype(bf16)
    query_grads = (
        jnp.einsum("hqk,khd->qhd", score_grads, keys_low, preferred_element_type=f32) * score_scale
    )
    key_grads = (
        jnp.einsum("hqk,qhd->khd", score_grads, queries_low, preferred_element_type=f32)
        * score_scale
    )
    ignored, pullback = jax.vjp(rotary, query_pre)
    query_pre_grad = pullback(query_grads)[0].astype(bf16).reshape(tok_count, model_width)
    ignored, pullback = jax.vjp(rotary, key_pre)
    key_pre_grad = pullback(key_grads)[0].astype(bf16).reshape(tok_count, model_width)
    value_flat = value_grads.reshape(tok_count, model_width)
    normed1_grad = (
        jnp.einsum("tc,dc->td", query_pre_grad, full_query, preferred_element_type=f32)
        + jnp.einsum("tc,dc->td", key_pre_grad, full_key, preferred_element_type=f32)
        + jnp.einsum("tc,dc->td", value_flat, full_value, preferred_element_type=f32)
    )
    grad_query_part = jnp.einsum(
        "td,tc->dc",
        normed1,
        lax.dynamic_slice_in_dim(query_pre_grad, column_start, quarter, 1),
        preferred_element_type=f32,
    )
    grad_key_part = jnp.einsum(
        "td,tc->dc",
        normed1,
        lax.dynamic_slice_in_dim(key_pre_grad, column_start, quarter, 1),
        preferred_element_type=f32,
    )
    grad_value_part = jnp.einsum(
        "td,tc->dc",
        normed1,
        lax.dynamic_slice_in_dim(value_flat, column_start, quarter, 1),
        preferred_element_type=f32,
    )
    ignored, pullback = jax.vjp(rms_norm, x_float, attn_gain)
    tokens_norm_grad, grad_attn_gain = pullback(normed1_grad)
    tokens_grad = residual_grad + tokens_norm_grad
    summed = (
        lax.psum(grad_attn_gain.astype(jnp.bfloat16), "ep").astype(jnp.float32),
        lax.psum(grad_query_part.astype(jnp.bfloat16), "ep").astype(jnp.float32),
        lax.psum(grad_key_part.astype(jnp.bfloat16), "ep").astype(jnp.float32),
        lax.psum(grad_value_part.astype(jnp.bfloat16), "ep").astype(jnp.float32),
        lax.psum(grad_out_part.astype(jnp.bfloat16), "ep").astype(jnp.float32),
        lax.psum(grad_ffn_gain.astype(jnp.bfloat16), "ep").astype(jnp.float32),
        lax.psum(grad_router.astype(jnp.bfloat16), "ep").astype(jnp.float32),
        lax.psum(grad_shared_gate.astype(jnp.bfloat16), "ep").astype(jnp.float32),
        lax.psum(grad_shared_up.astype(jnp.bfloat16), "ep").astype(jnp.float32),
        lax.psum(grad_shared_down.astype(jnp.bfloat16), "ep").astype(jnp.float32),
    )
    grad_tokens = lax.dynamic_slice_in_dim(tokens_grad, column_start, quarter, 1)
    return (
        output,
        grad_tokens,
        summed[0],
        summed[1],
        summed[2],
        summed[3],
        summed[4],
        summed[5],
        summed[6],
        summed[7],
        summed[8],
        summed[9],
        grad_expert_gate,
        grad_expert_up,
        grad_expert_down,
    )


def solution(mesh):
    placed = (
        P("ep", None),
        P(),
        P(None, "hs"),
        P(None, "hs"),
        P(None, "hs"),
        P(None, "hs"),
        P(),
        P(),
        P(None, "hs"),
        P(None, "hs"),
        P("hs", None),
        P("ep", None, "hs"),
        P("ep", None, "hs"),
        P("ep", "hs", None),
        P("ep", None),
        P("ep", None),
        P("ep", "hs"),
    )
    return jax.shard_map(
        shards,
        mesh=mesh,
        in_specs=placed,
        out_specs=(
            P("ep", "hs"),
            P("ep", "hs"),
            P(),
            P(None, "hs"),
            P(None, "hs"),
            P(None, "hs"),
            P(None, "hs"),
            P(),
            P(),
            P(None, "hs"),
            P(None, "hs"),
            P("hs", None),
            P("ep", None, "hs"),
            P("ep", None, "hs"),
            P("ep", "hs", None),
        ),
        check_vma=False,
    )
```

profile of v0, /device:TPU:9, one launch (start us, length us, event | category | flops | bytes accessed | tf_op | source)
XLA Modules:
  0.0 1872.1 jit_solution(13965837612410693554)
XLA Ops:
  15.7 32.3 %reduce-window.6 = s32[64,28,128]{2,1,0:T(8,128)S(1)} reduce-window(s32[64,28,128]{2,1,0:T(8,128)} %fusion.38, s32[]{:T(128)} %constant.27.clone.1), window={size=1x1x128 pad=0_0x0_0x127_0}, to_apply=%region_8.9 | reduce-window | flops 29130752 | bytes 1835012 | tf_op jit(solution)/shard_map/reduce-window
  81.4 58.6 %all-gather.8.cloned.1.call-done = bf16[1280,1280]{0,1:T(8,128)(2,1)} async-done(((bf16[1280,320]{0,1:T(8,128)(2,1)}), bf16[1280,1280]{0,1:T(8,128)(2,1)}) %all-gather.8.cloned.1.call-update) | async-done | bytes 3276816 | tf_op jit(solution)/shard_map/all_gather | solution.py:76
  151.6 54.3 %all-gather.10.cloned.1.call-done = bf16[1280,1280]{0,1:T(8,128)(2,1)} async-done(((bf16[1280,320]{0,1:T(8,128)(2,1)}), bf16[1280,1280]{0,1:T(8,128)(2,1)}) %all-gather.10.cloned.1.call-update) | async-done | bytes 3276816 | tf_op jit(solution)/shard_map/all_gather | solution.py:77
  234.0 37.5 %all-gather.12.cloned.1.call-done = bf16[1280,1280]{0,1:T(8,128)(2,1)} async-done(((bf16[1280,320]{0,1:T(8,128)(2,1)}), bf16[1280,1280]{0,1:T(8,128)(2,1)}) %all-gather.12.cloned.1.call-update) | async-done | bytes 3276816 | tf_op jit(solution)/shard_map/all_gather | solution.py:79
  296.8 28.0 %scatter_custom_fusion = bf16[7168,1280]{1,0:T(8,128)(2,1)} fusion(s32[3584]{0:T(1024)S(1)} %fusion.56, bf16[3584,1280]{1,0:T(8,128)(2,1)} %reshape.318, bf16[]{:T(256)} %constant.55.clone.1), kind=kCustom, calls=%fused_computation.24 | custom fusion | bytes 18350592 | tf_op jit(solution)/shard_map/scatter | solution.py:124
  331.8 34.3 %all-gather.14.cloned.1.call-done = bf16[512,1280]{0,1:T(8,128)(2,1)} async-done(((bf16[512,320]{0,1:T(8,128)(2,1)}), bf16[512,1280]{0,1:T(8,128)(2,1)}) %all-gather.14.cloned.1.call-update) | async-done | bytes 1310736 | tf_op jit(solution)/shard_map/all_gather | solution.py:163
  377.1 19.4 %mul.595 = f32[3584,1280]{1,0:T(8,128)} reshape(f32[512,7,1280]{2,1,0:T(8,128)} %mul.594) | data formatting | bytes 36700160 | tf_op jit(solution)/shard_map/mul | solution.py:166
  398.3 29.3 %scatter_custom_fusion.1 = bf16[7168,1280]{1,0:T(8,128)(2,1)} fusion(s32[3584]{0:T(1024)S(1)} %fusion.56, f32[3584,1280]{1,0:T(8,128)} %mul.595, f32[3584]{0:T(1024)S(1)} %mul.592, bf16[]{:T(256)} %constant.55.clone.1), kind=kCustom, calls=%fused_computation.21 | custom fusion | flops 9175040 | bytes 36716544 | tf_op jit(solution)/shard_map/scatter | solution.py:170
  427.6 100.9 %all-to-all-done = bf16[8,896,1280]{2,1,0:T(8,128)(2,1)} async-done(((bf16[8,896,1280]{2,1,0:T(8,128)(2,1)}), bf16[8,896,1280]{2,1,0:T(8,128)(2,1)}, u32[]{:S(2)}, u32[]{:S(2)}) %all-to-all-start) | async-done | bytes 18350112 | tf_op jit(solution)/shard_map/all_to_all | solution.py:129
  560.7 174.6 %all-to-all-done.2 = bf16[8,896,1280]{2,1,0:T(8,128)(2,1)} async-done(((bf16[8,896,1280]{2,1,0:T(8,128)(2,1)}), bf16[8,896,1280]{2,1,0:T(8,128)(2,1)}, u32[]{:S(2)}, u32[]{:S(2)}) %all-to-all-start.2) | async-done | bytes 18350112 | tf_op jit(solution)/shard_map/all_to_all | solution.py:172
  735.3 19.8 %fusion.17 = (bf16[8,8,112,224]{3,2,0,1:T(8,128)(2,1)}, bf16[8,8,112,224]{3,2,0,1:T(8,128)(2,1)}, bf16[8,8,112,224]{3,2,0,1:T(8,128)(2,1)}) fusion(f32[8,8,112,224]{3,2,1,0:T(8,128)} %fusion.6, f32[8,8,112,224]{3,2,1,0:T(8,128)} %fusion.4, bf16[8,224,1280]{2,1,0:T(8,128)(2,1)} %param.30, bf16[8,8,112,1280]{3,2,1,0:T(8,128)(2,1)} %bitcast.24), kind=kOutput, calls=%fused_computation.32 | convolution fusion | flops 4136108032 | bytes 45416448 | tf_op jit(solution)/shard_map/secd,efd->secf/dot_general | solution.py:182
  755.1 20.5 %convolution_bitcast_fusion = f32[8,8,112,1280]{3,2,0,1:T(8,128)} fusion(bf16[8,8,112,224]{3,2,0,1:T(8,128)(2,1)} %get-tuple-element.111, bf16[8,224,1280]{2,1,0:T(8,128)(2,1)} %param.30), kind=kOutput, calls=%fused_computation.5 | convolution fusion | flops 4110417920 | bytes 44498944 | tf_op jit(solution)/shard_map/secf,efd->secd/dot_general | solution.py:139
  775.6 26.3 %copy.204 = f32[8,8,112,1280]{3,2,1,0:T(8,128)} copy(f32[8,8,112,1280]{3,2,0,1:T(8,128)} %convolution_bitcast_fusion) | data formatting | bytes 73400320 | tf_op jit(solution)/shard_map/secf,efd->secd/transpose | solution.py:139
  801.9 35.2 %copy.256 = f32[7168,1280]{0,1:T(8,128)} copy(f32[7168,1280]{1,0:T(8,128)} %bitcast.175) | data formatting | bytes 73400320
  837.2 21.3 %fusion.28 = f32[8,8,112,1280]{3,2,1,0:T(8,128)} fusion(bf16[8,8,112,224]{3,2,0,1:T(8,128)(2,1)} %get-tuple-element.110, bf16[8,1280,224]{1,2,0:T(8,128)(2,1)} %param.28), kind=kOutput, calls=%fused_computation.49 | convolution fusion | flops 4110417920 | bytes 44498944 | tf_op jit(solution)/shard_map/secf,edf->secd/dot_general | solution.py:191
  858.4 29.2 %add_bitcast_fusion = f32[8,8,112,1280]{3,2,0,1:T(8,128)} fusion(f32[8,8,112,1280]{3,2,1,0:T(8,128)} %fusion.28, bf16[8,8,112,224]{3,2,0,1:T(8,128)(2,1)} %get-tuple-element.109, bf16[8,1280,224]{1,2,0:T(8,128)(2,1)} %param.29), kind=kOutput, calls=%fused_computation.4 | convolution fusion | flops 4119592960 | bytes 81199104 | tf_op jit(solution)/shard_map/secf,edf->secd/dot_general | solution.py:193
  887.7 26.5 %copy.210 = f32[8,8,112,1280]{3,2,1,0:T(8,128)} copy(f32[8,8,112,1280]{3,2,0,1:T(8,128)} %add_bitcast_fusion) | data formatting | bytes 73400320 | tf_op jit(solution)/shard_map/add | solution.py:191
  942.0 496.9 %reduce-scatter.9.cloned.1.call-done = f32[320,7168]{1,0:T(8,128)} async-done(((f32[1280,7168]{1,0:T(8,128)}), f32[320,7168]{1,0:T(8,128)}) %reduce-scatter.9.cloned.1.call-update) | async-done | bytes 9175056
  1466.8 30.2 %reduce-scatter.7.cloned.1.call-done = f32[320,512]{1,0:T(8,128)} async-done(((f32[1280,512]{1,0:T(8,128)}), f32[320,512]{1,0:T(8,128)}) %reduce-scatter.7.cloned.1.call-update) | async-done | bytes 655376
  1512.0 30.3 %gather_fusion.1 = f32[3584,1280]{1,0:T(8,128)} fusion(f32[7168,1280]{1,0:T(8,128)} %bitcast.31, s32[4096]{0:T(1024)S(1)} %pad_clamp_fusion), kind=kCustom, calls=%fused_computation.1 | custom fusion | bytes 36714496 | tf_op jit(solution)/shard_map/gather | solution.py:220
  1542.3 19.1 %reshape.292 = f32[512,7,1280]{2,1,0:T(8,128)} reshape(f32[3584,1280]{1,0:T(8,128)} %gather_fusion.1) | data formatting | bytes 36700160 | tf_op jit(solution)/shard_map/reshape | solution.py:220
  1626.4 20.4 %psum.85 = f32[512,7]{1,0:T(8,128)S(1)} all-reduce(f32[512,7]{1,0:T(8,128)} %get-tuple-element.90), channel_id=1, replica_groups=mesh['ep'=8,'hs'=4] {'hs'}, use_global_device_ids=true, to_apply=%region_18.19 | all-reduce | flops 3584 | bytes 28672 | tf_op jit(solution)/shard_map/psum | solution.py:221
  1648.2 37.9 %all-reduce.9.cloned.1.call-done = f32[512,1280]{1,0:T(8,128)} async-done(((f32[512,1280]{1,0:T(8,128)}), f32[512,1280]{1,0:T(8,128)}) %all-reduce.9.cloned.1.call-update) | async-done | bytes 2621456 | tf_op jit(solution)/shard_map/psum | solution.py:221
  1788.0 64.5 %all-reduce.11.cloned.1.call-done = (bf16[1280,320]{0,1:T(8,128)(2,1)}, bf16[1280,320]{0,1:T(8,128)(2,1)}, bf16[1280,320]{0,1:T(8,128)(2,1)}, bf16[1280,320]{0,1...) async-done(((bf16[1280,320]{0,1:T(8,128)(2,1)}, bf16[1280,320]{0,1:T(8,128)(2,1)}, ...) | async-done | bytes 6881296 | tf_op jit(solution)/shard_map/psum | solution.py:287
  (298 shorter events, 409.6 us)
Async XLA Ops:
  7.2 920.3 %copy-start = (bf16[448,1280]{1,0:T(8,128)(2,1)S(1)}, bf16[448,1280]{1,0:T(8,128)(2,1)}, u32[]{:S(2)}) copy-start(bf16[448,1280]{1,0:T(8,128)(2,1)} %param.27) | copy-start | bytes 3440644
  7.2 66.8 %all-gather.6.cloned.1.call-start = ((), (), s32[]{:S(2)}) async-start(), calls=%async_computation.6 | async-start | bytes 4096000 | tf_op jit(solution)/shard_map/all_gather | solution.py:78
  8.0 132.0 %all-gather.8.cloned.1.call-start = ((), (), s32[]{:S(2)}) async-start(), calls=%async_computation.7 | async-start | bytes 4096000 | tf_op jit(solution)/shard_map/all_gather | solution.py:76
  8.7 197.1 %all-gather.10.cloned.1.call-start = ((), (), s32[]{:S(2)}) async-start(), calls=%async_computation.8 | async-start | bytes 4096000 | tf_op jit(solution)/shard_map/all_gather | solution.py:77
  9.4 262.1 %all-gather.12.cloned.1.call-start = ((), (), s32[]{:S(2)}) async-start(), calls=%async_computation.9 | async-start | bytes 4096000 | tf_op jit(solution)/shard_map/all_gather | solution.py:79
  11.0 37.1 %copy-start.68 = (f32[512]{0:T(512)}, f32[512]{0:T(512)S(1)}, u32[]{:S(2)}) copy-start(f32[512]{0:T(512)S(1)} %multiply_reduce_fusion.8) | copy-start | bytes 6148
  11.0 194.8 %copy-start.53 = (f32[512]{0:T(512)}, f32[512]{0:T(512)S(1)}, u32[]{:S(2)}) copy-start(f32[512]{0:T(512)S(1)} %fusion.61) | copy-start | bytes 6148
  55.2 343.1 %copy-start.59 = (s32[3584]{0:T(1024)}, s32[3584]{0:T(1024)S(1)}, u32[]{:S(2)}) copy-start(s32[3584]{0:T(1024)S(1)} %fusion.56) | copy-start | bytes 43012
  277.7 118.8 %copy-start.4 = (bf16[512,1280]{1,0:T(8,128)(2,1)}, bf16[512,1280]{1,0:T(8,128)(2,1)S(1)}, u32[]{:S(2)}) copy-start(bf16[512,1280]{1,0:T(8,128)(2,1)S(1)} %multiply_convert_fusion.3) | copy-start | bytes 3932164
  324.7 203.8 %all-to-all-start = ((bf16[8,896,1280]{2,1,0:T(8,128)(2,1)}), bf16[8,896,1280]{2,1,0:T(8,128)(2,1)}, u32[]{:S(2)}, u32[]{:S(2)}) async-start(bf16[8,896,1280]{2,1,0:T(8,128)(2,1)} %bitcast.177), calls=%async_computation | async-start | bytes 36700160 | tf_op jit(solution)/shard_map/all_to_all | solution.py:129
  331.2 34.8 %all-gather.14.cloned.1.call-start = ((), (), s32[]{:S(2)}) async-start(), calls=%async_computation.10 | async-start | bytes 1638400 | tf_op jit(solution)/shard_map/all_gather | solution.py:163
  397.1 30.5 %copy-start.62 = (f32[512]{0:T(512)}, f32[512]{0:T(512)S(1)}, u32[]{:S(2)}) copy-start(f32[512]{0:T(512)S(1)} %get-tuple-element.137) | copy-start | bytes 6148
  528.5 206.8 %all-to-all-start.2 = ((bf16[8,896,1280]{2,1,0:T(8,128)(2,1)}), bf16[8,896,1280]{2,1,0:T(8,128)(2,1)}, u32[]{:S(2)}, u32[]{:S(2)}) async-start(bf16[8,896,1280]{2,1,0:T(8,128)(2,1)} %bitcast.178), calls=%async_computation.2 | async-start | bytes 36700160 | tf_op jit(solution)/shard_map/all_to_all | solution.py:172
  538.0 900.9 %reduce-scatter.9.cloned.1.call-start = ((), (), s32[]{:S(2)}) async-start(), calls=%async_computation.13 | async-start | bytes 45875200
  914.2 541.8 %all-to-all-start.3 = ((f32[8,896,1280]{2,1,0:T(8,128)}), f32[8,896,1280]{2,1,0:T(8,128)}, u32[]{:S(2)}, u32[]{:S(2)}) async-start(f32[8,896,1280]{2,1,0:T(8,128)} %bitcast.174), calls=%async_computation.3 | async-start | bytes 73400320 | tf_op jit(solution)/shard_map/all_to_all | solution.py:212
  924.5 572.6 %reduce-scatter.7.cloned.1.call-start = ((), (), s32[]{:S(2)}) async-start(), calls=%async_computation.12 | async-start | bytes 3276800
  1455.9 136.3 %all-to-all-start.1 = ((bf16[8,896,320]{1,2,0:T(8,128)(2,1)}), bf16[8,896,320]{1,2,0:T(8,128)(2,1)}, u32[]{:S(2)}, u32[]{:S(2)}) async-start(bf16[8,896,320]{1,2,0:T(8,128)(2,1)} %copy.205), calls=%async_computation.1 | async-start | bytes 9175040 | tf_op jit(solution)/shard_map/all_to_all | solution.py:151
  1461.0 225.1 %all-reduce.9.cloned.1.call-start = ((), (), s32[]{:S(2)}) async-start(), calls=%async_computation.11 | async-start | bytes 5242880 | tf_op jit(solution)/shard_map/psum | solution.py:221
  1579.0 273.5 %all-reduce.11.cloned.1.call-start = ((), (), s32[]{:S(2)}) async-start(), calls=%async_computation.14 | async-start | bytes 13762560 | tf_op jit(solution)/shard_map/psum | solution.py:287
  1626.4 59.7 %copy-start.48 = (bf16[1280,64]{0,1:T(8,128)(2,1)S(1)}, bf16[1280,64]{0,1:T(8,128)(2,1)}, u32[]{:S(2)}) copy-start(bf16[1280,64]{0,1:T(8,128)(2,1)} %param.24) | copy-start | bytes 491524
  1626.4 59.7 %copy-start.58 = (f32[1280]{0:T(1024)S(1)}, f32[1280]{0:T(1024)}, u32[]{:S(2)}) copy-start(f32[1280]{0:T(1024)} %param.23) | copy-start | bytes 15364
  1626.4 59.7 %copy-start.67 = (f32[512]{0:T(512)S(1)}, f32[512]{0:T(512)}, u32[]{:S(2)}) copy-start(f32[512]{0:T(512)} %copy-done.66) | copy-start | bytes 6148
  1648.2 41.5 %copy-start.72 = (f32[512]{0:T(512)S(1)}, f32[512]{0:T(512)}, u32[]{:S(2)}) copy-start(f32[512]{0:T(512)} %copy-done.71) | copy-start | bytes 6148
  1648.2 41.6 %copy-start.16 = (bf16[512,1280]{1,0:T(8,128)(2,1)S(1)}, bf16[512,1280]{1,0:T(8,128)(2,1)}, u32[]{:S(2)}) copy-start(bf16[512,1280]{1,0:T(8,128)(2,1)} %copy.207) | copy-start | bytes 3932164
  (68 other events, 496.0 us)
Sparse Core Ops, SparseCore 0:
  9.6 64.3 all-gather.5
  75.6 64.2 all-gather.7
  141.5 64.2 all-gather.9
  207.2 64.2 all-gather.11
  333.3 32.7 all-gather.13
  837.3 601.5 reduce-scatter.8
  1441.8 55.2 reduce-scatter.6
  1579.1 106.9 all-reduce.8
  1740.3 112.0 all-reduce.10
where the time goes:
time: 1890 us; the launch traced here: 1870 us
  waiting for transfers between devices  1110 us (59%)
  local copies, waits for them, and re-layouts  302 us (16%)
  matrix products  250 us (13%)
  other arithmetic  129 us (7%)
  blocking collectives  32.6 us (2%)
  starting transfers between devices  31.5 us (2%)
    unnamed x11, waiting for transfers between devices  530 us
    all_to_all x1, waiting for transfers between devices, shards(): lax.all_to_all(send_grads.reshape(ep_count, local_experts * slots_used, m...  175 us
    all_to_all x1, waiting for transfers between devices, shards(): lax.all_to_all(send_rows.reshape(ep_count, local_experts * slots_used, mo...  101 us
    unnamed x168, local copies, waits for them, and re-layouts  68.7 us
    psum x1, waiting for transfers between devices, shards(): lax.psum(grad_query_part.astype(jnp.bfloat16), 'ep').astype(jnp.float32)  64.5 us
    all_gather x1, waiting for transfers between devices, shards(): lax.all_gather(attn_query, 'hs', axis=1, tiled=True)  58.6 us
    all_gather x1, waiting for transfers between devices, shards(): lax.all_gather(attn_key, 'hs', axis=1, tiled=True)  54.3 us
    another operation x4, other arithmetic  40.3 us
  transfers between devices with their start and end apart: 13, of which 11 were waited for; matrix products, arithmetic and copies ran while one was open for 24% of the time, Pallas kernels for 0%

commit v1 on v0

v1 whole, which is shorter than its diff:
```python
import math

import jax
import jax.numpy as jnp
from jax import lax
from jax.sharding import Mesh
from jax.sharding import PartitionSpec as P

HEADS = 10
HEAD_DIM = 128
CAP = 112
EPS = 1e-06
EP = ("xy", "core")
bf16 = jnp.bfloat16
f32 = jnp.float32


def dot(a, b):
    return jnp.dot(a, b, preferred_element_type=f32)


def ein(spec, a, b):
    return jnp.einsum(spec, a, b, preferred_element_type=f32)


def rope_tables(rows):
    half = HEAD_DIM // 2
    frequency = 10000.0 ** (-jnp.arange(half, dtype=f32) * 2.0 / HEAD_DIM)
    angles = jnp.arange(rows, dtype=f32)[:, None] * frequency[None, :]
    return jnp.cos(angles)[:, None, :], jnp.sin(angles)[:, None, :]


def rope(v, cosine, sine):
    half = HEAD_DIM // 2
    a, b = v[..., :half], v[..., half:]
    return jnp.concatenate([a * cosine - b * sine, b * cosine + a * sine], axis=-1)


def rope_back(v, cosine, sine):
    half = HEAD_DIM // 2
    a, b = v[..., :half], v[..., half:]
    return jnp.concatenate([a * cosine + b * sine, b * cosine - a * sine], axis=-1)


def shards(
    tokens,
    attn_gain,
    attn_query,
    attn_key,
    attn_value,
    attn_out,
    ffn_gain,
    router,
    shared_gate,
    shared_up,
    shared_down,
    expert_gate,
    expert_up,
    expert_down,
    routes,
    documents,
    out_grad,
):
    rows, width = tokens.shape
    quarter = out_grad.shape[1]
    hs = lax.axis_index("hs")
    hs_count = lax.axis_size("hs")
    odd = (hs % 2) == 1
    ep_count = lax.axis_size("xy") * lax.axis_size("core")
    ep = lax.axis_index("xy") * lax.axis_size("core") + lax.axis_index("core")
    local = expert_gate.shape[0]
    experts = router.shape[1]
    spare = HEAD_DIM * (-(-quarter // HEAD_DIM)) - quarter
    held = quarter + spare
    heads = held // HEAD_DIM
    col0 = hs * quarter

    def outer(w):
        return jnp.where(odd, w[:, :spare], w[:, quarter - spare :])

    pairs = [(i, i ^ 1) for i in range(hs_count)]
    sent = jnp.concatenate([outer(attn_query), outer(attn_key), outer(attn_value)], axis=1)
    got = lax.ppermute(sent, "hs", pairs)

    def widened(w, extra):
        return jnp.where(
            odd, jnp.concatenate([extra, w], axis=1), jnp.concatenate([w, extra], axis=1)
        )

    def own(v):
        return jnp.where(odd, v[:, spare:], v[:, :quarter])

    w_query = widened(attn_query, got[:, :spare])
    w_key = widened(attn_key, got[:, spare : 2 * spare])
    w_value = widened(attn_value, got[:, 2 * spare :])
    out_full = lax.all_gather(attn_out, "hs", axis=1, tiled=True)
    grad_full = lax.all_gather(out_grad, "hs", axis=1, tiled=True)
    grad_all = lax.all_gather(grad_full, EP, axis=0, tiled=True)
    routes_all = lax.all_gather(routes, EP, axis=0, tiled=True)

    x = tokens.astype(f32)
    rms1 = lax.rsqrt(jnp.mean(x * x, axis=-1, keepdims=True) + EPS)
    normed1 = (x * rms1 * attn_gain).astype(bf16)
    cosine, sine = rope_tables(rows)
    shape3 = (rows, heads, HEAD_DIM)
    q = rope(dot(normed1, w_query).reshape(shape3), cosine, sine).astype(bf16)
    k = rope(dot(normed1, w_key).reshape(shape3), cosine, sine).astype(bf16)
    v = dot(normed1, w_value).astype(bf16).reshape(shape3)
    scale = 1.0 / math.sqrt(HEAD_DIM)
    positions = jnp.arange(rows, dtype=jnp.int32)
    doc = documents[0]
    allowed = (positions[:, None] >= positions[None, :]) & (doc[:, None] == doc[None, :])
    scores = jnp.where(allowed[None], ein("qhd,khd->hqk", q, k) * scale, -1e30)
    top = jnp.max(scores, axis=-1, keepdims=True)
    raised = jnp.exp(scores - top)
    probs = raised / jnp.sum(raised, axis=-1, keepdims=True)
    probs_low = probs.astype(bf16)
    attended3 = ein("hqk,khd->qhd", probs_low, v).reshape(rows, held).astype(bf16)
    attended = lax.all_gather(own(attended3), "hs", axis=1, tiled=True)
    residual = x + dot(attended, out_full)
    rms2 = lax.rsqrt(jnp.mean(residual * residual, axis=-1, keepdims=True) + EPS)
    normed2 = (residual * rms2 * ffn_gain).astype(bf16)
    normed_all = lax.all_gather(normed2, EP, axis=0, tiled=True)

    sh_gate = dot(normed2, shared_gate)
    sh_up = dot(normed2, shared_up)
    sh_sig = jax.nn.sigmoid(sh_gate)
    sh_act = sh_gate * sh_sig
    sh_hidden = (sh_act * sh_up).astype(bf16)
    shared_part = dot(sh_hidden, shared_down)
    grad_sh = ein("td,fd->tf", grad_full, shared_down)
    grad_sh_gate = (grad_sh * sh_up * sh_sig * (1 + sh_gate * (1 - sh_sig))).astype(bf16)
    grad_sh_up = (grad_sh * sh_act).astype(bf16)
    grad_shared_down = ein("tf,td->fd", sh_hidden, grad_full)
    grad_shared_gate = ein("td,tf->df", normed2, grad_sh_gate)
    grad_shared_up = ein("td,tf->df", normed2, grad_sh_up)
    shared_back = ein("tf,df->td", grad_sh_gate, shared_gate) + ein(
        "tf,df->td", grad_sh_up, shared_up
    )

    gate_all = jax.nn.softmax(dot(normed_all, router), axis=-1)
    first = ep * local
    weight_all = lax.dynamic_slice_in_dim(gate_all, first, local, 1).reshape(ep_count, rows, local)
    mine = first + jnp.arange(local, dtype=jnp.int32)
    chosen = jnp.any(
        routes_all.reshape(ep_count, rows, -1)[:, :, :, None] == mine[None, None, None, :], axis=2
    )
    below = (positions[:, None] > positions[None, :]).astype(bf16)
    rank = ein("tu,sue->ste", below, chosen.astype(bf16)).astype(jnp.int32)
    slot = jnp.where(chosen, rank, -1).transpose(0, 2, 1)
    pick_f = (slot[:, :, None, :] == jnp.arange(CAP, dtype=jnp.int32)[None, None, :, None]).astype(f32)
    pick = pick_f.astype(bf16).reshape(ep_count, local * CAP, rows)
    slot_weight = jnp.sum(pick_f * weight_all.transpose(0, 2, 1)[:, :, None, :], axis=-1)
    slot_weight = slot_weight.transpose(1, 0, 2).reshape(local, ep_count * CAP, 1)

    def spread(all_rows):
        picked = ein("srt,std->srd", pick, all_rows.reshape(ep_count, rows, width)).astype(bf16)
        return (
            picked.reshape(ep_count, local, CAP, width)
            .transpose(1, 0, 2, 3)
            .reshape(local, ep_count * CAP, width)
        )

    def gathered(slots):
        slots = (
            slots.astype(bf16)
            .reshape(local, ep_count, CAP, -1)
            .transpose(1, 0, 2, 3)
            .reshape(ep_count, local * CAP, -1)
        )
        return ein("srt,srd->std", pick, slots).astype(bf16).reshape(ep_count * rows, -1)

    ex_in = spread(normed_all)
    ex_grad = spread(grad_all)
    ex_gate = ein("erd,edf->erf", ex_in, expert_gate)
    ex_up = ein("erd,edf->erf", ex_in, expert_up)
    sig = jax.nn.sigmoid(ex_gate)
    act = ex_gate * sig
    hidden = (act * ex_up).astype(bf16)
    hidden_w = (hidden.astype(f32) * slot_weight).astype(bf16)
    out_part = gathered(ein("erf,efd->erd", hidden_w, expert_down))
    grad_hidden = ein("erd,efd->erf", ex_grad, expert_down)
    grad_slot_weight = jnp.sum(grad_hidden * hidden.astype(f32), axis=-1)
    grad_hidden = grad_hidden * slot_weight
    grad_ex_gate = (grad_hidden * ex_up * sig * (1 + ex_gate * (1 - sig))).astype(bf16)
    grad_ex_up = (grad_hidden * act).astype(bf16)
    grad_expert_down = ein("erf,erd->efd", hidden_w, ex_grad)
    grad_expert_gate = ein("erd,erf->edf", ex_in, grad_ex_gate)
    grad_expert_up = ein("erd,erf->edf", ex_in, grad_ex_up)
    back = ein("erf,edf->erd", grad_ex_gate, expert_gate) + ein(
        "erf,edf->erd", grad_ex_up, expert_up
    )
    back_part = gathered(back)
    grad_probs_local = jnp.sum(
        pick_f * grad_slot_weight.reshape(local, ep_count, CAP).transpose(1, 0, 2)[..., None], axis=2
    ).transpose(0, 2, 1)
    grad_probs_part = lax.dynamic_update_slice_in_dim(
        jnp.zeros((ep_count * rows, experts), f32), grad_probs_local.reshape(-1, local), first, 1
    ).astype(bf16)
    back_part = jnp.concatenate([back_part, grad_probs_part], axis=1)

    out_rows = lax.psum_scatter(out_part, EP, scatter_dimension=0, tiled=True)
    out_rows = (out_rows.astype(f32) + shared_part).astype(bf16)
    out_quarter = lax.psum_scatter(out_rows, "hs", scatter_dimension=1, tiled=True)

    def quarter_of(a):
        return lax.dynamic_slice_in_dim(a, col0, quarter, 1)

    output = (quarter_of(residual) + out_quarter.astype(f32)).astype(bf16)

    back_rows = lax.psum_scatter(back_part, EP, scatter_dimension=0, tiled=True).astype(f32)
    back_rows = jnp.concatenate([back_rows[:, :width] + shared_back, back_rows[:, width:]], axis=1)
    back_rows = lax.psum(back_rows.astype(bf16), "hs").astype(f32)
    gate_own = jax.nn.softmax(dot(normed2, router), axis=-1)
    grad_probs = back_rows[:, width:]
    grad_logits = (
        gate_own * (grad_probs - jnp.sum(grad_probs * gate_own, axis=-1, keepdims=True))
    ).astype(bf16)
    grad_router = ein("td,te->de", normed2, grad_logits)
    grad_normed2 = back_rows[:, :width] + ein("te,de->td", grad_logits, router)
    grad_ffn_gain = jnp.sum(grad_normed2 * residual * rms2, axis=0)
    u = grad_normed2 * ffn_gain
    grad_residual = (
        grad_full.astype(f32)
        + rms2 * u
        - residual * rms2**3 * jnp.mean(u * residual, axis=-1, keepdims=True)
    )
    grad_low = grad_residual.astype(bf16)
    grad_attn_out = ein("td,tc->dc", attended, quarter_of(grad_low))
    out_held = lax.dynamic_slice_in_dim(out_full, jnp.where(odd, col0 - spare, col0), held, 0)
    grad_attended = ein("tc,dc->td", grad_low, out_held).astype(bf16).reshape(shape3)
    grad_p = ein("qhd,khd->hqk", grad_attended, v)
    grad_v = ein("hqk,qhd->khd", probs_low, grad_attended).astype(bf16)
    grad_s = (probs * (grad_p - jnp.sum(probs * grad_p, axis=-1, keepdims=True))).astype(bf16)
    grad_q = ein("hqk,khd->qhd", grad_s, k) * scale
    grad_k = ein("hqk,qhd->khd", grad_s, q) * scale
    grad_q = own(rope_back(grad_q, cosine, sine).astype(bf16).reshape(rows, held))
    grad_k = own(rope_back(grad_k, cosine, sine).astype(bf16).reshape(rows, held))
    grad_v = own(grad_v.reshape(rows, held))
    normed1_part = (
        ein("tc,dc->td", grad_q, attn_query)
        + ein("tc,dc->td", grad_k, attn_key)
        + ein("tc,dc->td", grad_v, attn_value)
    )
    grad_query = ein("td,tc->dc", normed1, grad_q)
    grad_key = ein("td,tc->dc", normed1, grad_k)
    grad_value = ein("td,tc->dc", normed1, grad_v)
    grad_n1 = lax.psum_scatter(
        normed1_part.astype(bf16), "hs", scatter_dimension=1, tiled=True
    ).astype(f32)
    x_own = quarter_of(x)
    w1 = grad_n1 * lax.dynamic_slice_in_dim(attn_gain, col0, quarter, 0)
    mean1 = lax.psum(jnp.sum(w1 * x_own, axis=-1, keepdims=True), "hs") / width
    grad_tokens = quarter_of(grad_residual) + rms1 * w1 - x_own * rms1**3 * mean1
    gain_own = jnp.sum(grad_n1 * x_own * rms1, axis=0)
    gain_part = lax.dynamic_update_slice_in_dim(jnp.zeros((width,), f32), gain_own, col0, 0)
    grad_attn_gain = lax.psum(gain_part, (*EP, "hs"))

    def over_ep(a):
        return lax.psum(a.astype(bf16), EP).astype(f32)

    return (
        output,
        grad_tokens,
        grad_attn_gain,
        over_ep(grad_query),
        over_ep(grad_key),
        over_ep(grad_value),
        over_ep(grad_attn_out),
        lax.psum(grad_ffn_gain, EP),
        over_ep(grad_router),
        over_ep(grad_shared_gate),
        over_ep(grad_shared_up),
        over_ep(grad_shared_down),
        grad_expert_gate,
        grad_expert_up,
        grad_expert_down,
    )


def solution(mesh):
    ep_count, hs_count = mesh.devices.shape
    cut = Mesh(mesh.devices.reshape(ep_count // 2, 2, hs_count), ("xy", "core", "hs"))
    return jax.shard_map(
        shards,
        mesh=cut,
        in_specs=(
            P(EP, None),
            P(),
            P(None, "hs"),
            P(None, "hs"),
            P(None, "hs"),
            P(None, "hs"),
            P(),
            P(),
            P(None, "hs"),
            P(None, "hs"),
            P("hs", None),
            P(EP, None, "hs"),
            P(EP, None, "hs"),
            P(EP, "hs", None),
            P(EP, None),
            P(EP, None),
            P(EP, "hs"),
        ),
        out_specs=(
            P(EP, "hs"),
            P(EP, "hs"),
            P(),
            P(None, "hs"),
            P(None, "hs"),
            P(None, "hs"),
            P(None, "hs"),
            P(),
            P(),
            P(None, "hs"),
            P(None, "hs"),
            P("hs", None),
            P(EP, None, "hs"),
            P(EP, None, "hs"),
            P(EP, "hs", None),
        ),
        check_vma=False,
    )
```

time: 1890 us -> 949 us (0.50)
  waiting for transfers between devices: 1110 us -> 350 us
  local copies, waits for them, and re-layouts: 302 us -> 127 us
  other arithmetic: 129 us -> 74 us
  matrix products: 250 us -> 296 us
  blocking collectives: 32.6 us -> 74.6 us
  starting transfers between devices: 31.5 us -> 0.9 us
    unnamed x11 -> x13, waiting for transfers between devices: 530 us -> 1.99 us
    all_to_all x4 -> x0, waiting for transfers between devices: 275 us -> none  [the longest x1 175 us: shards(): lax.all_to_all(send_grads.reshape(ep_count, local_experts * slots_used, m...]
    reduce_scatter x0 -> x2, waiting for transfers between devices: none -> 76.8 us  [the longest x1 72.7 us: shards(): out_rows = lax.psum_scatter(out_part, EP, scatter_dimension=0, tiled=True)]
    unnamed x168 -> x128, local copies, waits for them, and re-layouts: 68.7 us -> 17.2 us
    dot_general x38 -> x44, matrix products: 247 us -> 292 us  [the longest x35 269 us: ein(): return jnp.einsum(spec, a, b, preferred_element_type=f32)]
    gather x2 -> x0, local copies, waits for them, and re-layouts: 43.7 us -> none  [the longest x1 30.3 us: shards(): back_rows[dest_rows].reshape(tok_count, topk, model_width)]
    transpose x1 -> x7, local copies, waits for them, and re-layouts: 26.3 us -> 65.6 us  [the longest x2 32.7 us: gathered(): slots = slots.astype(bf16).reshape(local, ep_count, CAP, -1).transpose(1,...]
    another operation x4 -> x2, other arithmetic: 40.3 us -> 4.58 us
  transfers between devices with their start and end apart: 13 -> 12, of which waited for: 11 -> 9; matrix products, arithmetic and copies ran while one was open for 24% -> 30% of each run, Pallas kernels for 0% -> 0%
where the time goes in v1:
time: 949 us; the launch traced here: 938 us
  waiting for transfers between devices  350 us (37%)
  matrix products  296 us (31%)
  local copies, waits for them, and re-layouts  127 us (13%)
  blocking collectives  74.6 us (8%)
  other arithmetic  74 us (8%)
  between operations  15.1 us (2%)
    dot_general x35, matrix products, ein(): return jnp.einsum(spec, a, b, preferred_element_type=f32)  269 us
    reduce_scatter x1, waiting for transfers between devices, shards(): out_rows = lax.psum_scatter(out_part, EP, scatter_dimension=0, tiled=True)  72.7 us
    all_gather x1, waiting for transfers between devices, shards(): out_full = lax.all_gather(attn_out, 'hs', axis=1, tiled=True)  64.7 us
    psum x1, waiting for transfers between devices, shards(): back_rows = lax.psum(back_rows.astype(bf16), 'hs').astype(f32)  63.3 us
    all_gather x1, waiting for transfers between devices, shards(): grad_all = lax.all_gather(grad_full, EP, axis=0, tiled=True)  45.7 us
    psum x1, blocking collectives, shards(): grad_attn_gain = lax.psum(gain_part, (*EP, 'hs'))  43.9 us
    all_gather x1, waiting for transfers between devices, shards(): attended = lax.all_gather(own(attended3), 'hs', axis=1, tiled=True)  42.8 us
    transpose x2, local copies, waits for them, and re-layouts, gathered(): slots = slots.astype(bf16).reshape(local, ep_count, CAP, -1).transpose(1,...  32.7 us
  transfers between devices with their start and end apart: 12, of which 9 were waited for; matrix products, arithmetic and copies ran while one was open for 30% of the time, Pallas kernels for 0%

profile of v1, /device:TPU:9, one launch (start us, length us, event | category | flops | bytes accessed | tf_op | source)
XLA Modules:
  0.0 937.7 jit_solution(41017967007740781)
XLA Ops:
  50.6 42.8 %all-gather.6.cloned.1.call-done = bf16[512,1280]{0,1:T(8,128)(2,1)} async-done(((bf16[512,320]{0,1:T(8,128)(2,1)}), bf16[512,1280]{0,1:T(8,128)(2,1)}) %all-gather.6.cloned.1.call-update) | async-done | bytes 1310736 | tf_op jit(solution)/shard_map/all_gather | solution.py:119
  93.4 64.7 %all-gather.8.cloned.1.call-done = bf16[1280,1280]{0,1:T(8,128)(2,1)} async-done(((bf16[1280,320]{0,1:T(8,128)(2,1)}), bf16[1280,1280]{0,1:T(8,128)(2,1)}) %all-gather.8.cloned.1.call-update) | async-done | bytes 3276816 | tf_op jit(solution)/shard_map/all_gather | solution.py:96
  181.2 45.7 %all-gather.14.cloned.1.call-done = bf16[4096,1280]{0,1:T(8,128)(2,1)} async-done(((bf16[512,1280]{0,1:T(8,128)(2,1)}), bf16[4096,1280]{0,1:T(8,128)(2,1)}) %all-gather.14.cloned.1.call-update) | async-done | bytes 10485776 | tf_op jit(solution)/shard_map/all_gather | solution.py:98
  226.9 14.5 %copy.174 = bf16[4096,1280]{1,0:T(8,128)(2,1)} copy(bf16[4096,1280]{0,1:T(8,128)(2,1)} %all-gather.14.cloned.1.call-done) | data formatting | bytes 20971520 | tf_op jit(solution)/shard_map/all_gather | solution.py:98
  241.4 18.5 %convolution_convert_fusion = bf16[8,896,1280]{2,1,0:T(8,128)(2,1)} fusion(bf16[8,896,512]{2,1,0:T(8,128)(2,1)} %convert_convert_fusion, bf16[8,512,1280]{2,1,0:T(8,128)(2,1)} %bitcast.139), kind=kOutput, calls=%fused_computation.2 | convolution fusion | flops 9404416000 | bytes 36175872 | tf_op jit(solution)/shard_map/srt,std->srd/dot_general | solution.py:23
  260.0 16.4 %copy.175 = bf16[8,8,112,1280]{3,2,1,0:T(8,128)(2,1)} copy(bf16[8,8,112,1280]{3,2,0,1:T(8,128)(2,1)} %bitcast.133) | data formatting | bytes 36700160 | tf_op jit(solution)/shard_map/transpose | solution.py:160
  276.4 16.2 %all-gather.10.cloned.1.call-done = bf16[4096,1280]{1,0:T(8,128)(2,1)} async-done(((bf16[512,1280]{1,0:T(8,128)(2,1)}), bf16[4096,1280]{1,0:T(8,128)(2,1)}) %all-gather.10.cloned.1.call-update) | async-done | bytes 10485776 | tf_op jit(solution)/shard_map/all_gather | solution.py:123
  292.5 18.5 %convolution_convert_fusion.2 = bf16[8,896,1280]{2,1,0:T(8,128)(2,1)} fusion(bf16[8,896,512]{2,1,0:T(8,128)(2,1)} %convert_convert_fusion, bf16[8,512,1280]{2,1,0:T(8,128)(2,1)} %bitcast.136), kind=kOutput, calls=%fused_computation.4 | convolution fusion | flops 9404416000 | bytes 36175872 | tf_op jit(solution)/shard_map/srt,std->srd/dot_general | solution.py:23
  311.0 16.0 %copy.167 = bf16[8,8,112,1280]{3,2,1,0:T(8,128)(2,1)} copy(bf16[8,8,112,1280]{3,2,0,1:T(8,128)(2,1)} %bitcast.135) | data formatting | bytes 36700160 | tf_op jit(solution)/shard_map/transpose | solution.py:160
  353.9 21.1 %fusion.2 = (f32[8,896]{1,0:T(8,128)S(1)}, bf16[8,896,224]{1,2,0:T(8,128)(2,1)}, f32[8,896,224]{1,2,0:T(8,128)}) fusion(f32[8,896,224]{1,2,0:T(8,128)} %fusion.78, f32[8,896,224]{1,2,0:T(8,128)} %fusion.77, bf16[8,896,1280]{2,1,0:T(8,128)(2,1)} %bitcast.130, bf16[8,224,1280]{2,1,0:T(8,128)(2,1)} %param.30), kind=kOutput, calls=%fused_computation.16 | convolution fusion | flops 4124861440 | bytes 45445120 | tf_op jit(solution)/shard_map/erd,efd->erf/dot_general | solution.py:23
  399.5 20.4 %fusion.81 = f32[8,896,1280]{2,1,0:T(8,128)} fusion(bf16[8,896,224]{1,2,0:T(8,128)(2,1)} %get-tuple-element.111, bf16[8,1280,224]{1,2,0:T(8,128)(2,1)} %param.28), kind=kOutput, calls=%fused_computation.176 | convolution fusion | flops 4110417920 | bytes 44498944 | tf_op jit(solution)/shard_map/erf,edf->erd/dot_general | solution.py:23
  419.8 21.0 %add_convert_fusion = bf16[8,896,1280]{2,1,0:T(8,128)(2,1)} fusion(f32[8,896,1280]{2,1,0:T(8,128)} %fusion.81, bf16[8,896,224]{1,2,0:T(8,128)(2,1)} %get-tuple-element.110, bf16[8,1280,224]{1,2,0:T(8,128)(2,1)} %param.29), kind=kOutput, calls=%fused_computation.1 | convolution fusion | flops 4128768000 | bytes 62849024 | tf_op jit(solution)/shard_map/erf,edf->erd/dot_general | solution.py:23
  440.9 16.0 %copy.176 = bf16[8,8,112,1280]{3,2,1,0:T(8,128)(2,1)} copy(bf16[8,8,112,1280]{3,2,0,1:T(8,128)(2,1)} %bitcast.129) | data formatting | bytes 36700160 | tf_op jit(solution)/shard_map/transpose | solution.py:168
  456.9 21.2 %convolution_convert_fusion.3 = bf16[8,512,1280]{2,1,0:T(8,128)(2,1)} fusion(bf16[8,896,512]{2,1,0:T(8,128)(2,1)} %convert_convert_fusion, bf16[8,896,1280]{2,1,0:T(8,128)(2,1)} %bitcast.134), kind=kOutput, calls=%fused_computation.10 | convolution fusion | flops 9400483840 | bytes 36175872 | tf_op jit(solution)/shard_map/srt,srd->std/dot_general | solution.py:23
  495.0 15.7 %convolution_convert_fusion.1 = bf16[8,896,1280]{2,1,0:T(8,128)(2,1)} fusion(bf16[8,224,1280]{2,1,0:T(8,128)(2,1)} %param.30, bf16[8,896,224]{1,2,0:T(8,128)(2,1)} %get-tuple-element.109, f32[8,896]{1,0:T(8,128)S(1)} %mul.513), kind=kOutput, calls=%fused_computation.3 | convolution fusion | flops 4124409856 | bytes 26177536 | tf_op jit(solution)/shard_map/erf,efd->erd/dot_general | solution.py:23
  510.7 16.7 %copy.169 = bf16[8,8,112,1280]{3,2,1,0:T(8,128)(2,1)} copy(bf16[8,8,112,1280]{3,2,0,1:T(8,128)(2,1)} %bitcast.128) | data formatting | bytes 36700160 | tf_op jit(solution)/shard_map/transpose | solution.py:168
  527.4 21.7 %convolution_convert_fusion.4 = bf16[8,512,1280]{2,1,0:T(8,128)(2,1)} fusion(bf16[8,896,512]{2,1,0:T(8,128)(2,1)} %convert_convert_fusion, bf16[8,896,1280]{2,1,0:T(8,128)(2,1)} %bitcast.132), kind=kOutput, calls=%fused_computation.11 | convolution fusion | flops 9400483840 | bytes 36175872 | tf_op jit(solution)/shard_map/srt,srd->std/dot_general | solution.py:23
  593.8 72.7 %reduce-scatter.9.cloned.1.call-done = bf16[512,1280]{0,1:T(8,128)(2,1)} async-done(((bf16[4096,1280]{0,1:T(8,128)(2,1)}), bf16[512,1280]{0,1:T(8,128)(2,1)}) %reduce-scatter.9.cloned.1.call-update) | async-done | bytes 1310736 | tf_op jit(solution)/shard_map/reduce_scatter | solution.py:202
  670.1 63.3 %all-reduce.4.cloned.1.call-done = bf16[512,1344]{1,0:T(8,128)(2,1)} async-done(((bf16[512,1344]{1,0:T(8,128)(2,1)}), bf16[512,1344]{1,0:T(8,128)(2,1)}) %all-reduce.4.cloned.1.call-update) | async-done | bytes 1376272 | tf_op jit(solution)/shard_map/psum | solution.py:213
  759.4 16.0 %fusion.84 = f32[8,1280,224]{1,2,0:T(8,128)} fusion(bf16[8,896,224]{1,2,0:T(8,128)(2,1)} %get-tuple-element.110, bf16[8,896,1280]{2,1,0:T(8,128)(2,1)} %bitcast.126), kind=kOutput, calls=%fused_computation.179 | convolution fusion | flops 4110417920 | bytes 30736384 | tf_op jit(solution)/shard_map/erd,erf->edf/dot_general | solution.py:23
  785.4 16.0 %fusion.83 = f32[8,1280,224]{1,2,0:T(8,128)} fusion(bf16[8,896,224]{1,2,0:T(8,128)(2,1)} %get-tuple-element.111, bf16[8,896,1280]{2,1,0:T(8,128)(2,1)} %bitcast.127), kind=kOutput, calls=%fused_computation.178 | convolution fusion | flops 4110417920 | bytes 30736384 | tf_op jit(solution)/shard_map/erd,erf->edf/dot_general | solution.py:23
  801.4 14.4 %fusion.8 = f32[8,224,1280]{2,1,0:T(8,128)} fusion(bf16[8,896,1280]{2,1,0:T(8,128)(2,1)} %bitcast.131, bf16[8,896,224]{1,2,0:T(8,128)(2,1)S(1)} %copy-done.1, f32[8,896]{1,0:T(8,128)S(1)} %mul.513), kind=kOutput, calls=%fused_computation.39 | convolution fusion | flops 4115234816 | bytes 30765056 | tf_op jit(solution)/shard_map/erf,erd->efd/dot_general | solution.py:23
  846.5 43.9 %psum.86 = f32[1280]{0:T(1024)} all-reduce(f32[1280]{0:T(1024)S(1)} %dynamic_update_slice.7), channel_id=1, replica_groups=mesh['xy'=4,'core'=2,'hs'=4] {'xy','core','hs'}, use_global_device_ids=true, to_apply=%region_23.24 | all-reduce | flops 1280 | bytes 10240 | tf_op jit(solution)/shard_map/psum | solution.py:257
  890.4 27.7 %all-reduce.6.cloned.1.call-done = (bf16[1280,320]{0,1:T(8,128)(2,1)}, bf16[1280,320]{0,1:T(8,128)(2,1)}, bf16[1280,320]{0,1:T(8,128)(2,1)}, bf16[1280,320]{0,1:...) async-done(((bf16[1280,320]{0,1:T(8,128)(2,1)}, bf16[1280,320]{0,1:T(8,128)(2,1)}, ...) | async-done | bytes 6881296 | tf_op jit(solution)/shard_map/psum | solution.py:260
  (258 shorter events, 261.6 us)
Async XLA Ops:
  7.2 565.4 %copy-start = (bf16[448,1280]{1,0:T(8,128)(2,1)S(1)}, bf16[448,1280]{1,0:T(8,128)(2,1)}, u32[]{:S(2)}) copy-start(bf16[448,1280]{1,0:T(8,128)(2,1)} %param.27) | copy-start | bytes 3440644
  7.2 42.8 %all-gather.12.cloned.1.call-start = ((), (), s32[]{:S(2)}) async-start(), calls=%async_computation.8 | async-start | bytes 1638400 | tf_op jit(solution)/shard_map/all_gather | solution.py:97
  8.0 85.4 %all-gather.6.cloned.1.call-start = ((), (), s32[]{:S(2)}) async-start(), calls=%async_computation.4 | async-start | bytes 1638400 | tf_op jit(solution)/shard_map/all_gather | solution.py:119
  9.0 16.5 %copy-start.18 = (bf16[1280,320]{0,1:T(8,128)(2,1)S(1)}, bf16[1280,320]{0,1:T(8,128)(2,1)}, u32[]{:S(2)}) copy-start(bf16[1280,320]{0,1:T(8,128)(2,1)} %param.20) | copy-start | bytes 2457604
  9.0 16.4 %copy-start.52 = (f32[1280]{0:T(1024)S(1)}, f32[1280]{0:T(1024)}, u32[]{:S(2)}) copy-start(f32[1280]{0:T(1024)} %param.18) | copy-start | bytes 15364
  10.4 14.4 %collective-permute-start = (bf16[1280,192]{0,1:T(8,128)(2,1)S(1)}, bf16[1280,192]{0,1:T(8,128)(2,1)S(1)}, u32[]{:S(2)}, u32[]{:S(2)}) collective-permute-start(bf16[1280,192]{0,1:T(8,128)(2,1)S(1)} %pad_maximum_fusion.2), channel_id=1, source_target_pairs={{0,1},{1,0},{2,3},{3,2},{4,5},{5,4},{6,7},{7,6},{8,9},{9,8},{10,11... | collective-permute-start | bytes 1474568 | tf_op jit(solution)/shard_map/ppermute | solution.py:83
  11.4 34.6 %copy-start.44 = (f32[512]{0:T(512)}, f32[512]{0:T(512)S(1)}, u32[]{:S(2)}) copy-start(f32[512]{0:T(512)S(1)} %get-tuple-element.135) | copy-start | bytes 6148
  14.0 24.2 %copy-start.14 = (f32[512,64]{1,0:T(8,128)}, f32[512,64]{1,0:T(8,128)S(1)}, u32[]{:S(2)}) copy-start(f32[512,64]{1,0:T(8,128)S(1)} %get-tuple-element.138) | copy-start | bytes 393220
  49.2 108.9 %all-gather.8.cloned.1.call-start = ((), (), s32[]{:S(2)}) async-start(), calls=%async_computation.5 | async-start | bytes 4096000 | tf_op jit(solution)/shard_map/all_gather | solution.py:96
  49.9 177.0 %all-gather.14.cloned.1.call-start = ((), (), s32[]{:S(2)}) async-start(), calls=%async_computation.9 | async-start | bytes 11796480 | tf_op jit(solution)/shard_map/all_gather | solution.py:98
  50.5 113.5 %copy-start.40 = (f32[1280]{0:T(1024)S(1)}, f32[1280]{0:T(1024)}, u32[]{:S(2)}) copy-start(f32[1280]{0:T(1024)} %param.23) | copy-start | bytes 15364
  50.5 242.0 %all-gather.10.cloned.1.call-start = ((), (), s32[]{:S(2)}) async-start(), calls=%async_computation.6 | async-start | bytes 11796480 | tf_op jit(solution)/shard_map/all_gather | solution.py:123
  165.4 416.1 %reduce-scatter.11.cloned.1.call-start = ((), (), s32[]{:S(2)}) async-start(), calls=%async_computation.10 | async-start | bytes 12976128 | tf_op jit(solution)/shard_map/reduce_scatter | solution.py:211
  353.9 21.2 %copy-start.38 = (bf16[1280,64]{0,1:T(8,128)(2,1)S(1)}, bf16[1280,64]{0,1:T(8,128)(2,1)}, u32[]{:S(2)}) copy-start(bf16[1280,64]{0,1:T(8,128)(2,1)} %param.24) | copy-start | bytes 491524
  494.9 171.6 %reduce-scatter.9.cloned.1.call-start = ((), (), s32[]{:S(2)}) async-start(), calls=%async_computation.7 | async-start | bytes 11796480 | tf_op jit(solution)/shard_map/reduce_scatter | solution.py:202
  563.4 170.0 %all-reduce.4.cloned.1.call-start = ((), (), s32[]{:S(2)}) async-start(), calls=%async_computation.11 | async-start | bytes 2883584 | tf_op jit(solution)/shard_map/psum | solution.py:213
  586.2 243.2 %reduce-scatter.13.cloned.1.call-start = ((), (), s32[]{:S(2)}) async-start(), calls=%async_computation.12 | async-start | bytes 1638400
  591.8 74.8 %copy-start.59 = (bf16[512,448]{0,1:T(8,128)(2,1)S(1)}, bf16[512,448]{0,1:T(8,128)(2,1)}, u32[]{:S(2)}) copy-start(bf16[512,448]{0,1:T(8,128)(2,1)} %get-tuple-element.118) | copy-start | bytes 1376260
  669.8 65.6 %copy-start.41 = (f32[1280]{0:T(1024)S(1)}, f32[1280]{0:T(1024)}, u32[]{:S(2)}) copy-start(f32[1280]{0:T(1024)} %param.23) | copy-start | bytes 15364
  669.8 65.6 %copy-start.43 = (f32[512]{0:T(512)S(1)}, f32[512]{0:T(512)}, u32[]{:S(2)}) copy-start(f32[512]{0:T(512)} %copy-done.42) | copy-start | bytes 6148
  669.9 163.2 %reduce-scatter.15.cloned.1.call-start = ((), (), s32[]{:S(2)}) async-start(), calls=%async_computation.13 | async-start | bytes 1638400
  759.1 159.0 %all-reduce.6.cloned.1.call-start = ((), (), s32[]{:S(2)}) async-start(), calls=%async_computation.14 | async-start | bytes 13762560 | tf_op jit(solution)/shard_map/psum | solution.py:260
  759.4 18.3 %copy-start.28 = (bf16[512,1280]{0,1:T(8,128)(2,1)S(1)}, bf16[512,1280]{0,1:T(8,128)(2,1)}, u32[]{:S(2)}) copy-start(bf16[512,1280]{0,1:T(8,128)(2,1)} %all-gather.6.cloned.1.call-done) | copy-start | bytes 3932164
  815.7 27.3 %copy-start.48 = (f32[512]{0:T(512)S(1)}, f32[512]{0:T(512)}, u32[]{:S(2)}) copy-start(f32[512]{0:T(512)} %get-tuple-element.134) | copy-start | bytes 6148
  (49 other events, 139.6 us)
Sparse Core Ops, SparseCore 0:
  9.6 35.9 all-gather.11
  49.3 44.0 all-gather.5
  95.0 63.1 all-gather.7
  159.8 67.0 all-gather.13
  229.2 63.2 all-gather.9
  495.1 86.3 reduce-scatter.10
  585.0 81.5 reduce-scatter.8
  669.5 63.8 all-reduce.3
  736.3 29.2 reduce-scatter.12
  768.3 29.9 reduce-scatter.14
  803.6 114.4 all-reduce.5

commit v2 on v1

--- a/solution.py
+++ b/solution.py
@@ -1,8 +1,11 @@
+import functools
 import math
 
 import jax
 import jax.numpy as jnp
 from jax import lax
+from jax.experimental import pallas as pl
+from jax.experimental.pallas import tpu as pltpu
 from jax.sharding import Mesh
 from jax.sharding import PartitionSpec as P
 
@@ -40,6 +43,261 @@
     half = HEAD_DIM // 2
     a, b = v[..., :half], v[..., half:]
     return jnp.concatenate([a * cosine + b * sine, b * cosine - a * sine], axis=-1)
+
+
+VMEM_LIMIT = 60 * 1024 * 1024
+PAD = 256
+
+
+def nn(a, b):
+    return lax.dot_general(a, b, (((1,), (0,)), ((), ())), preferred_element_type=f32)
+
+
+def nt(a, b):
+    return lax.dot_general(a, b, (((1,), (1,)), ((), ())), preferred_element_type=f32)
+
+
+def tn(a, b):
+    return lax.dot_general(a, b, (((0,), (0,)), ((), ())), preferred_element_type=f32)
+
+
+def slot_masks(slot_ref, at):
+    local, rows = slot_ref.shape[-2:]
+    number = lax.broadcasted_iota(jnp.int32, (CAP, rows), 0)
+    return [slot_ref[at, e : e + 1, :] == number for e in range(local)]
+
+
+def spread_kernel(weighted, *refs):
+    if weighted:
+        rows_ref, slot_ref, router_ref, x_ref, sw_ref, pick = refs
+    else:
+        rows_ref, slot_ref, x_ref, pick = refs
+    local = slot_ref.shape[1]
+    rows = rows_ref[...]
+    masks = slot_masks(slot_ref, 0)
+    if weighted:
+        logits = nt(router_ref[...], rows)
+        raised = jnp.exp(logits - jnp.max(logits, axis=0, keepdims=True))
+        gates = raised / jnp.sum(raised, axis=0, keepdims=True)
+    for e in range(local):
+        pick[e * CAP : (e + 1) * CAP, :] = masks[e].astype(f32).astype(bf16)
+        if weighted:
+            sw_ref[e] = jnp.sum(
+                jnp.where(masks[e], gates[e : e + 1, :], 0.0), axis=1, keepdims=True
+            )
+    x_ref[...] = nn(pick[...], rows).astype(bf16).reshape(x_ref.shape)
+
+
+def spread(all_rows, slot, router_t=None):
+    s, local, rows = slot.shape
+    width = all_rows.shape[1]
+    weighted = router_t is not None
+    in_specs = [
+        pl.BlockSpec((rows, width), lambda i: (i, 0)),
+        pl.BlockSpec((1, local, rows), lambda i: (i, 0, 0)),
+    ]
+    out_specs = [pl.BlockSpec((1, local, CAP, width), lambda i: (i, 0, 0, 0))]
+    out_shape = [jax.ShapeDtypeStruct((s, local, CAP, width), bf16)]
+    args = [all_rows, slot]
+    if weighted:
+        in_specs.append(pl.BlockSpec(router_t.shape, lambda i: (0, 0)))
+        out_specs.append(pl.BlockSpec((local, CAP, 1), lambda i: (0, i, 0)))
+        out_shape.append(jax.ShapeDtypeStruct((local, s * CAP, 1), f32))
+        args.append(router_t)
+    out = pl.pallas_call(
+        functools.partial(spread_kernel, weighted),
+        grid=(s,),
+        in_specs=in_specs,
+        out_specs=out_specs,
+        out_shape=out_shape,
+        scratch_shapes=[pltpu.VMEM((local * CAP, rows), bf16)],
+        compiler_params=pltpu.CompilerParams(vmem_limit_bytes=VMEM_LIMIT),
+        name="spread",
+    )(*args)
+    return out if weighted else out[0]
+
+
+def padded(ref, out):
+    ff = ref.shape[1]
+    out[:ff, :] = ref[0]
+    out[ff:, :] = jnp.zeros((out.shape[0] - ff, out.shape[1]), out.dtype)
+
+
+def experts_forward_kernel(
+    x_ref, sw_ref, wg_ref, wu_ref, wd_ref, y_ref, gate_ref, up_ref, wg, wu, wd
+):
+    padded(wg_ref, wg)
+    padded(wu_ref, wu)
+    padded(wd_ref, wd)
+    rows, width = gate_ref.shape[1], x_ref.shape[3]
+    x = x_ref[...].reshape(rows, width)
+    gate = nt(x, wg[...])
+    up = nt(x, wu[...])
+    gate_ref[0] = gate
+    up_ref[0] = up
+    act = gate / (1.0 + jnp.exp(-gate))
+    hidden = (act * up).astype(bf16).astype(f32)
+    hidden_w = (hidden * sw_ref[0]).astype(bf16)
+    y_ref[...] = nn(hidden_w, wd[...]).astype(bf16).reshape(y_ref.shape)
+
+
+def experts_backward_kernel(
+    groups,
+    x_ref,
+    gx_ref,
+    gate_ref,
+    up_ref,
+    sw_ref,
+    wg_ref,
+    wu_ref,
+    wd_ref,
+    dx_ref,
+    dg_ref,
+    du_ref,
+    dd_ref,
+    gsw_ref,
+    wg,
+    wu,
+    wd,
+):
+    padded(wg_ref, wg)
+    padded(wu_ref, wu)
+    padded(wd_ref, wd)
+    rows, width = gate_ref.shape[1], x_ref.shape[3]
+    ff = wg_ref.shape[1]
+    x = x_ref[...].reshape(rows, width)
+    gx = gx_ref[...].reshape(rows, width)
+    gate, up, sw = gate_ref[0], up_ref[0], sw_ref[0]
+    sig = 1.0 / (1.0 + jnp.exp(-gate))
+    act = gate * sig
+    hidden = (act * up).astype(bf16).astype(f32)
+    gh = nt(gx, wd[...])
+    gsw_ref[0] = jnp.sum(gh * hidden, axis=-1, keepdims=True)
+    gh = gh * sw
+    gg = (gh * up * sig * (1.0 + gate * (1.0 - sig))).astype(bf16)
+    gu = (gh * act).astype(bf16)
+    sums = (
+        (dd_ref, tn((hidden * sw).astype(bf16), gx)[:ff]),
+        (dg_ref, tn(gg, x)[:ff]),
+        (du_ref, tn(gu, x)[:ff]),
+    )
+    if groups == 1:
+        for ref, value in sums:
+            ref[0] = value
+    else:
+
+        @pl.when(pl.program_id(1) == 0)
+        def _():
+            for ref, value in sums:
+                ref[0] = value
+
+        @pl.when(pl.program_id(1) > 0)
+        def _():
+            for ref, value in sums:
+                ref[0] += value
+
+    dx_ref[...] = (nn(gg, wg[...]) + nn(gu, wu[...])).astype(bf16).reshape(dx_ref.shape)
+
+
+def expert_specs(s, width):
+    group = min(s, 8)
+    slots = pl.BlockSpec((group, 1, CAP, width), lambda i, j: (j, i, 0, 0))
+    lines = lambda columns: pl.BlockSpec((1, group * CAP, columns), lambda i, j: (i, j, 0))
+    per = lambda *shape: pl.BlockSpec((1, *shape), lambda i, j: (i, 0, 0))
+    return s // group, slots, lines, per
+
+
+def experts_forward(x, sw, wg, wu, wd):
+    s, local, cap, width = x.shape
+    ff = wg.shape[1]
+    rows = s * cap
+    groups, slots, lines, per = expert_specs(s, width)
+    middle = jax.ShapeDtypeStruct((local, rows, PAD), f32)
+    return pl.pallas_call(
+        experts_forward_kernel,
+        grid=(local, groups),
+        in_specs=[slots, lines(1)] + [per(ff, width)] * 3,
+        out_specs=[slots, lines(PAD), lines(PAD)],
+        out_shape=[jax.ShapeDtypeStruct(x.shape, bf16), middle, middle],
+        scratch_shapes=[pltpu.VMEM((PAD, width), bf16)] * 3,
+        compiler_params=pltpu.CompilerParams(vmem_limit_bytes=VMEM_LIMIT),
+        name="experts_forward",
+    )(x, sw, wg, wu, wd)
+
+
+def experts_backward(x, gx, gate, up, sw, wg, wu, wd):
+    s, local, cap, width = x.shape
+    ff = wg.shape[1]
+    rows = s * cap
+    groups, slots, lines, per = expert_specs(s, width)
+    return pl.pallas_call(
+        functools.partial(experts_backward_kernel, groups),
+        grid=(local, groups),
+        in_specs=[slots, slots, lines(PAD), lines(PAD), lines(1)]
+        + [per(ff, width)] * 3,
+        out_specs=[slots] + [per(ff, width)] * 3 + [lines(1)],
+        out_shape=[jax.ShapeDtypeStruct(x.shape, bf16)]
+        + [jax.ShapeDtypeStruct((local, ff, width), f32)] * 3
+        + [jax.ShapeDtypeStruct((local, rows, 1), f32)],
+        scratch_shapes=[pltpu.VMEM((PAD, width), bf16)] * 3,
+        compiler_params=pltpu.CompilerParams(vmem_limit_bytes=VMEM_LIMIT),
+        name="experts_backward",
+    )(x, gx, gate, up, sw, wg, wu, wd)
+
+
+def collect_kernel(y_ref, slot_ref, out_ref, pick):
+    local = slot_ref.shape[1]
+    masks = slot_masks(slot_ref, 0)
+    for e in range(local):
+        pick[e * CAP : (e + 1) * CAP, :] = masks[e].astype(f32).astype(bf16)
+    out_ref[0] = tn(pick[...], y_ref[...].reshape(pick.shape[0], -1)).astype(bf16)
+
+
+def collect_back_kernel(experts, y_ref, slot_ref, gsw_ref, first_ref, out_ref, pick):
+    local, rows = slot_ref.shape[1:]
+    first = first_ref[0]
+    masks = slot_masks(slot_ref, 0)
+    number = lax.broadcasted_iota(jnp.int32, (experts, rows), 0)
+    probs = jnp.zeros((experts, rows), f32)
+    for e in range(local):
+        pick[e * CAP : (e + 1) * CAP, :] = masks[e].astype(f32).astype(bf16)
+        line = jnp.sum(jnp.where(masks[e], gsw_ref[e], 0.0), axis=0, keepdims=True)
+        probs = jnp.where(number == first + e, line, probs)
+    out_ref[0, :rows] = tn(pick[...], y_ref[...].reshape(pick.shape[0], -1)).astype(bf16)
+    half = experts // 2
+    out_ref[0, rows:] = jnp.zeros((half, out_ref.shape[2]), bf16)
+    out_ref[0, rows:, :rows] = probs[:half].astype(bf16)
+    out_ref[0, rows:, rows : 2 * rows] = probs[half:].astype(bf16)
+
+
+def collect(y, slot, gsw=None, first=None, experts=0):
+    s, local, cap, width = y.shape
+    rows = slot.shape[2]
+    in_specs = [
+        pl.BlockSpec((1, local, cap, width), lambda i: (i, 0, 0, 0)),
+        pl.BlockSpec((1, local, rows), lambda i: (i, 0, 0)),
+    ]
+    args = [y, slot]
+    kernel = collect_kernel
+    tall = rows
+    if gsw is not None:
+        in_specs += [
+            pl.BlockSpec((local, cap, 1), lambda i: (0, i, 0)),
+            pl.BlockSpec(memory_space=pltpu.SMEM),
+        ]
+        args += [gsw, first.reshape(1)]
+        kernel = functools.partial(collect_back_kernel, experts)
+        tall = rows + experts // 2
+    return pl.pallas_call(
+        kernel,
+        grid=(s,),
+        in_specs=in_specs,
+        out_specs=pl.BlockSpec((1, tall, width), lambda i: (i, 0, 0)),
+        out_shape=jax.ShapeDtypeStruct((s, tall, width), bf16),
+        scratch_shapes=[pltpu.VMEM((local * cap, rows), bf16)],
+        compiler_params=pltpu.CompilerParams(vmem_limit_bytes=VMEM_LIMIT),
+        name="collect",
+    )(*args)
 
 
 def shards(
@@ -138,9 +396,7 @@
         "tf,df->td", grad_sh_up, shared_up
     )
 
-    gate_all = jax.nn.softmax(dot(normed_all, router), axis=-1)
     first = ep * local
-    weight_all = lax.dynamic_slice_in_dim(gate_all, first, local, 1).reshape(ep_count, rows, local)
     mine = first + jnp.arange(local, dtype=jnp.int32)
     chosen = jnp.any(
         routes_all.reshape(ep_count, rows, -1)[:, :, :, None] == mine[None, None, None, :], axis=2
@@ -148,56 +404,19 @@
     below = (positions[:, None] > positions[None, :]).astype(bf16)
     rank = ein("tu,sue->ste", below, chosen.astype(bf16)).astype(jnp.int32)
     slot = jnp.where(chosen, rank, -1).transpose(0, 2, 1)
-    pick_f = (slot[:, :, None, :] == jnp.arange(CAP, dtype=jnp.int32)[None, None, :, None]).astype(f32)
-    pick = pick_f.astype(bf16).reshape(ep_count, local * CAP, rows)
-    slot_weight = jnp.sum(pick_f * weight_all.transpose(0, 2, 1)[:, :, None, :], axis=-1)
-    slot_weight = slot_weight.transpose(1, 0, 2).reshape(local, ep_count * CAP, 1)
-
-    def spread(all_rows):
-        picked = ein("srt,std->srd", pick, all_rows.reshape(ep_count, rows, width)).astype(bf16)
-        return (
-            picked.reshape(ep_count, local, CAP, width)
-            .transpose(1, 0, 2, 3)
-            .reshape(local, ep_count * CAP, width)
-        )
-
-    def gathered(slots):
-        slots = (
-            slots.astype(bf16)
-            .reshape(local, ep_count, CAP, -1)
-            .transpose(1, 0, 2, 3)
-            .reshape(ep_count, local * CAP, -1)
-        )
-        return ein("srt,srd->std", pick, slots).astype(bf16).reshape(ep_count * rows, -1)
-
-    ex_in = spread(normed_all)
-    ex_grad = spread(grad_all)
-    ex_gate = ein("erd,edf->erf", ex_in, expert_gate)
-    ex_up = ein("erd,edf->erf", ex_in, expert_up)
-    sig = jax.nn.sigmoid(ex_gate)
-    act = ex_gate * sig
-    hidden = (act * ex_up).astype(bf16)
-    hidden_w = (hidden.astype(f32) * slot_weight).astype(bf16)
-    out_part = gathered(ein("erf,efd->erd", hidden_w, expert_down))
-    grad_hidden = ein("erd,efd->erf", ex_grad, expert_down)
-    grad_slot_weight = jnp.sum(grad_hidden * hidden.astype(f32), axis=-1)
-    grad_hidden = grad_hidden * slot_weight
-    grad_ex_gate = (grad_hidden * ex_up * sig * (1 + ex_gate * (1 - sig))).astype(bf16)
-    grad_ex_up = (grad_hidden * act).astype(bf16)
-    grad_expert_down = ein("erf,erd->efd", hidden_w, ex_grad)
-    grad_expert_gate = ein("erd,erf->edf", ex_in, grad_ex_gate)
-    grad_expert_up = ein("erd,erf->edf", ex_in, grad_ex_up)
-    back = ein("erf,edf->erd", grad_ex_gate, expert_gate) + ein(
-        "erf,edf->erd", grad_ex_up, expert_up
-    )
-    back_part = gathered(back)
-    grad_probs_local = jnp.sum(
-        pick_f * grad_slot_weight.reshape(local, ep_count, CAP).transpose(1, 0, 2)[..., None], axis=2
-    ).transpose(0, 2, 1)
-    grad_probs_part = lax.dynamic_update_slice_in_dim(
-        jnp.zeros((ep_count * rows, experts), f32), grad_probs_local.reshape(-1, local), first, 1
-    ).astype(bf16)
-    back_part = jnp.concatenate([back_part, grad_probs_part], axis=1)
+    router_t = jnp.roll(router.T, -first, axis=0)
+
+    gate_t, up_t = expert_gate.swapaxes(1, 2), expert_up.swapaxes(1, 2)
+    ex_grad = spread(grad_all, slot)
+    ex_in, slot_weight = spread(normed_all, slot, router_t)
+    ex_out, ex_gate, ex_up = experts_forward(ex_in, slot_weight, gate_t, up_t, expert_down)
+    out_part = collect(ex_out, slot).reshape(ep_count * rows, width)
+    ex_back, grad_gate_t, grad_up_t, grad_expert_down, grad_slot_weight = experts_backward(
+        ex_in, ex_grad, ex_gate, ex_up, slot_weight, gate_t, up_t, expert_down
+    )
+    grad_expert_gate, grad_expert_up = grad_gate_t.swapaxes(1, 2), grad_up_t.swapaxes(1, 2)
+    back_part = collect(ex_back, slot, grad_slot_weight, first, experts)
+    back_part = back_part.reshape(-1, width)
 
     out_rows = lax.psum_scatter(out_part, EP, scatter_dimension=0, tiled=True)
     out_rows = (out_rows.astype(f32) + shared_part).astype(bf16)
@@ -209,15 +428,17 @@
     output = (quarter_of(residual) + out_quarter.astype(f32)).astype(bf16)
 
     back_rows = lax.psum_scatter(back_part, EP, scatter_dimension=0, tiled=True).astype(f32)
-    back_rows = jnp.concatenate([back_rows[:, :width] + shared_back, back_rows[:, width:]], axis=1)
+    back_rows = jnp.concatenate([back_rows[:rows] + shared_back, back_rows[rows:]], axis=0)
     back_rows = lax.psum(back_rows.astype(bf16), "hs").astype(f32)
     gate_own = jax.nn.softmax(dot(normed2, router), axis=-1)
-    grad_probs = back_rows[:, width:]
+    grad_probs = jnp.concatenate(
+        [back_rows[rows:, :rows], back_rows[rows:, rows : 2 * rows]], axis=0
+    ).T
     grad_logits = (
         gate_own * (grad_probs - jnp.sum(grad_probs * gate_own, axis=-1, keepdims=True))
     ).astype(bf16)
     grad_router = ein("td,te->de", normed2, grad_logits)
-    grad_normed2 = back_rows[:, :width] + ein("te,de->td", grad_logits, router)
+    grad_normed2 = back_rows[:rows] + ein("te,de->td", grad_logits, router)
     grad_ffn_gain = jnp.sum(grad_normed2 * residual * rms2, axis=0)
     u = grad_normed2 * ffn_gain
     grad_residual = (

time: 949 us -> 857 us (0.903)
  matrix products: 296 us -> 57.9 us
  Pallas kernels: 0 us -> 151 us
  waiting for transfers between devices: 350 us -> 461 us
  local copies, waits for them, and re-layouts: 127 us -> 44.4 us
  other arithmetic: 74 us -> 41.1 us
    dot_general x35 -> x22, matrix products: 269 us -> 35.3 us  [ein(): return jnp.einsum(spec, a, b, preferred_element_type=f32)]
    pallas_call x0 -> x6, Pallas kernels: none -> 151 us  [the longest x1 46.9 us: experts_backward(): pl.pallas_call(functools.partial(experts_backward_kernel, groups), grid=(...]
    transpose x7 -> x0, local copies, waits for them, and re-layouts: 65.6 us -> none  [the longest x2 32.7 us: gathered(): slots = slots.astype(bf16).reshape(local, ep_count, CAP, -1).transpose(1,...]
    reduce_scatter x1, waiting for transfers between devices: 4.04 us -> 41.1 us  [shards(): lax.psum_scatter(back_part, EP, scatter_dimension=0, tiled=True).astype(f32)]
    psum x1, waiting for transfers between devices: 27.7 us -> 61.5 us  [over_ep(): return lax.psum(a.astype(bf16), EP).astype(f32)]
    all_gather x1, waiting for transfers between devices: 16.2 us -> 49.2 us  [shards(): normed_all = lax.all_gather(normed2, EP, axis=0, tiled=True)]
    convert_element_type x2 -> x1, other arithmetic: 15.4 us -> 0.04 us  [shards(): grad_logits = (gate_own * (grad_probs - jnp.sum(grad_probs * gate_own, ax...]
    all_gather x1 -> x0, local copies, waits for them, and re-layouts: 14.5 us -> none  [shards(): grad_all = lax.all_gather(grad_full, EP, axis=0, tiled=True)]
  transfers between devices with their start and end apart: 12 -> 12, of which waited for: 9 -> 10; matrix products, arithmetic and copies ran while one was open for 30% -> 14% of each run, Pallas kernels for 0% -> 4%
where the time goes in v2:
time: 857 us; the launch traced here: 846 us
  waiting for transfers between devices  461 us (54%)
  Pallas kernels  151 us (18%)
  blocking collectives  74.7 us (9%)
  matrix products  57.9 us (7%)
  local copies, waits for them, and re-layouts  44.4 us (5%)
  other arithmetic  41.1 us (5%)
  between operations  14.7 us (2%)
    reduce_scatter x1, waiting for transfers between devices, shards(): out_rows = lax.psum_scatter(out_part, EP, scatter_dimension=0, tiled=True)  80.1 us
    all_gather x1, waiting for transfers between devices, shards(): out_full = lax.all_gather(attn_out, 'hs', axis=1, tiled=True)  64.7 us
    psum x1, waiting for transfers between devices, shards(): back_rows = lax.psum(back_rows.astype(bf16), 'hs').astype(f32)  62.4 us
    psum x1, waiting for transfers between devices, over_ep(): return lax.psum(a.astype(bf16), EP).astype(f32)  61.5 us
    all_gather x1, waiting for transfers between devices, shards(): normed_all = lax.all_gather(normed2, EP, axis=0, tiled=True)  49.2 us
    all_gather x1, waiting for transfers between devices, shards(): grad_all = lax.all_gather(grad_full, EP, axis=0, tiled=True)  47.8 us
    pallas_call x1, Pallas kernels, experts_backward(): pl.pallas_call(functools.partial(experts_backward_kernel, groups), grid=(...  46.9 us
    psum x1, blocking collectives, shards(): grad_attn_gain = lax.psum(gain_part, (*EP, 'hs'))  43 us
  transfers between devices with their start and end apart: 12, of which 10 were waited for; matrix products, arithmetic and copies ran while one was open for 14% of the time, Pallas kernels for 4%

profile of v2, /device:TPU:9, one launch (start us, length us, event | category | flops | bytes accessed | tf_op | source)
XLA Modules:
  0.0 845.9 jit_solution(11921366817121736259)
XLA Ops:
  13.5 10.2 %collective-permute-done = bf16[1280,192]{0,1:T(8,128)(2,1)S(1)} collective-permute-done((bf16[1280,192]{0,1:T(8,128)(2,1)}, bf16[1280,192]{0,1:T(8,128)(2,1)S(1)}, u32[]{:S(2)}, u32[]{:S(2)}) %collective-permute-start) | collective-permute-done | bytes 491552 | tf_op jit(solution)/shard_map/ppermute | solution.py:341
  41.7 4.6 fusion.69
  53.5 39.1 %all-gather.6.cloned.1.call-done = bf16[512,1280]{0,1:T(8,128)(2,1)} async-done(((bf16[512,320]{0,1:T(8,128)(2,1)}), bf16[512,1280]{0,1:T(8,128)(2,1)}) %all-gather.6.cloned.1.call-update) | async-done | bytes 1310736 | tf_op jit(solution)/shard_map/all_gather | solution.py:377
  92.7 64.7 %all-gather.8.cloned.1.call-done = bf16[1280,1280]{0,1:T(8,128)(2,1)} async-done(((bf16[1280,320]{0,1:T(8,128)(2,1)}), bf16[1280,1280]{0,1:T(8,128)(2,1)}) %all-gather.8.cloned.1.call-update) | async-done | bytes 3276816 | tf_op jit(solution)/shard_map/all_gather | solution.py:354
  157.4 4.4 multiply_reduce_fusion.3
  164.7 10.3 %all_gather.21 = s32[4096,7]{0,1:T(8,128)S(1)} all-gather(s32[512,7]{0,1:T(8,128)S(1)} %copy-done.42), channel_id=1, replica_groups=mesh['xy'=4,'core'=2,'hs'=4] {'xy','core'}, dimensions={0}, use_global_device_ids=true | all-gather | bytes 129024 | tf_op jit(solution)/shard_map/all_gather | solution.py:357
  176.9 47.8 %all-gather.14.cloned.1.call-done.refs_0_ = bf16[4096,1280]{1,0:T(8,128)(2,1)} async-done(((bf16[512,1280]{1,0:T(8,128)(2,1)}), bf16[4096,1280]{1,0:T(8,128)(2,1)}) %all-gather.14.cloned.1.call-update) | async-done | bytes 10485776 | tf_op jit(solution)/shard_map/all_gather | solution.py:356
  224.7 16.4 %spread.3.gx_ref = bf16[8,8,112,1280]{3,2,1,0:T(8,128)(2,1)} custom-call(bf16[4096,1280]{1,0:T(8,128)(2,1)} %all-gather.14.cloned.1.call-done.refs_0_, s32[8,8,512]{2,1,0:T(8,128)} %fusion.13.refs_1_.slot_ref), custom_call_target="tpu_custom_call" | custom-call | tf_op jit(solution)/shard_map/spread/pallas_call | solution.py:107
  241.1 49.2 %all-gather.10.cloned.1.call-done.refs_0_ = bf16[4096,1280]{1,0:T(8,128)(2,1)} async-done(((bf16[512,1280]{1,0:T(8,128)(2,1)}), bf16[4096,1280]{1,0:T(8,128)(2,1)}) %all-gather.10.cloned.1.call-update) | async-done | bytes 10485776 | tf_op jit(solution)/shard_map/all_gather | solution.py:381
  290.3 20.1 %spread.2 = (bf16[8,8,112,1280]{3,2,1,0:T(8,128)(2,1)}, f32[8,896,1]{2,1,0:T(8,128)}) custom-call(bf16[4096,1280]{1,0:T(8,128)(2,1)} %all-gather.10.cloned.1.call-done.refs_0_, s32[8,8,512]{2,1,0:T(8,128)} %fusion.13.refs_1_.slot_ref, bf16[64,1280]{1,0:T(8,128)(2,1)} %fusion.53.refs_2_), custom_call_target="tpu_custom_call" | custom-call | tf_op jit(solution)/shard_map/spread/pallas_call | solution.py:107
  310.4 30.5 %experts_forward.1 = (bf16[8,8,112,1280]{3,2,1,0:T(8,128)(2,1)}, f32[8,896,256]{2,1,0:T(8,128)}, f32[8,896,256]{2,1,0:T(8,128)}) custom-call(bf16[8,8,112,1280]{3,2,1,0:T(8,128)(2,1)} %get-tuple-element.25.x_ref, f32[8,896,1]{2,1,0:T(8,128)} %get-tuple-element.26.sw_ref, bf16[8,224,1280]{2,1,0:T(8,128)(2,1)} %bitcast.85, bf16[8,224,1280]{2,1,0:T(8,128)(2,1)} %bitcast.87, ...), custom_call_target="tpu_custom_call" | custom-call | tf_op jit(solution)/shard_map/experts_forward/pallas_call | solution.py:216
  340.9 46.9 %experts_backward.1 = (bf16[8,8,112,1280]{3,2,1,0:T(8,128)(2,1)}, f32[8,224,1280]{2,1,0:T(8,128)}, f32[8,224,1280]{2,1,0:T(8,128)}, f32[8,224,1280]{2,1,0:T(8,128)}, f32[8,896,1]{2,1,0:T(8,128)}) custom-call(bf16[8,8,112,1280]{3,2,1,0:T(8,128)(2,1)} %get-tuple-element.25.x_ref, bf16[8,8,112,1280]{3,2,1,0:T(8,128)(2,1)} %spread.3.gx_ref, ...), custom_call_target="tpu_custom_call" | custom-call | tf_op jit(solution)/shard_map/experts_backward/pallas_call | solution.py:233
  387.8 18.6 %collect.3 = bf16[8,544,1280]{2,1,0:T(8,128)(2,1)} custom-call(bf16[8,8,112,1280]{3,2,1,0:T(8,128)(2,1)} %get-tuple-element.30.y_ref, s32[8,8,512]{2,1,0:T(8,128)} %fusion.13.refs_1_.slot_ref, f32[8,896,1]{2,1,0:T(8,128)} %get-tuple-element.31.gsw_ref, s32[1]{0:T(128)} %bitcast.14.first_ref), custom_call_target="tpu_custom_call" | custom-call | tf_op jit(solution)/shard_map/collect/pallas_call | solution.py:291
  406.7 19.0 %collect.2 = bf16[8,512,1280]{2,1,0:T(8,128)(2,1)} custom-call(bf16[8,8,112,1280]{3,2,1,0:T(8,128)(2,1)} %get-tuple-element.27.y_ref, s32[8,8,512]{2,1,0:T(8,128)} %fusion.13.refs_1_.slot_ref), custom_call_target="tpu_custom_call" | custom-call | tf_op jit(solution)/shard_map/collect/pallas_call | solution.py:291
  425.6 14.4 %copy.108 = bf16[4096,1280]{0,1:T(8,128)(2,1)} copy(bf16[4096,1280]{1,0:T(8,128)(2,1)} %bitcast.84) | data formatting | bytes 20971520 | tf_op jit(solution)/shard_map/reshape | solution.py:413
  449.8 41.1 %reduce-scatter.11.cloned.1.call-done = bf16[544,1280]{1,0:T(8,128)(2,1)} async-done(((bf16[4352,1280]{1,0:T(8,128)(2,1)}), bf16[544,1280]{1,0:T(8,128)(2,1)}) %reduce-scatter.11.cloned.1.call-update) | async-done | bytes 1392656 | tf_op jit(solution)/shard_map/reduce_scatter | solution.py:430
  490.9 3.5 fusion.2
  496.2 80.1 %reduce-scatter.9.cloned.1.call-done = bf16[512,1280]{0,1:T(8,128)(2,1)} async-done(((bf16[4096,1280]{0,1:T(8,128)(2,1)}), bf16[512,1280]{0,1:T(8,128)(2,1)}) %reduce-scatter.9.cloned.1.call-update) | async-done | bytes 1310736 | tf_op jit(solution)/shard_map/reduce_scatter | solution.py:421
  579.7 62.4 %all-reduce.4.cloned.1.call-done = bf16[544,1280]{1,0:T(8,128)(2,1)} async-done(((bf16[544,1280]{1,0:T(8,128)(2,1)}), bf16[544,1280]{1,0:T(8,128)(2,1)}) %all-reduce.4.cloned.1.call-update) | async-done | bytes 1392656 | tf_op jit(solution)/shard_map/psum | solution.py:432
  687.1 12.7 %psum.91 = f32[1280]{0:T(1024)} all-reduce(f32[1280]{0:T(1024)S(1)} %get-tuple-element.95), channel_id=1, replica_groups=mesh['xy'=4,'core'=2,'hs'=4] {'xy','core'}, use_global_device_ids=true, to_apply=%region_24.25 | all-reduce | flops 1280 | bytes 10240 | tf_op jit(solution)/shard_map/psum | solution.py:491
  703.4 3.8 reduce-scatter.15.cloned.1.call-done
  710.2 8.7 %psum.85 = f32[512,1]{0,1:T(1,128)S(1)} all-reduce(f32[512,1]{0,1:T(1,128)S(1)} %bitcast.104), channel_id=1, replica_groups=mesh['xy'=4,'core'=2,'hs'=4] {'hs'}, use_global_device_ids=true, to_apply=%region_16.17 | all-reduce | flops 512 | bytes 4096 | tf_op jit(solution)/shard_map/psum | solution.py:474
  722.8 43.0 %psum.86 = f32[1280]{0:T(1024)} all-reduce(f32[1280]{0:T(1024)S(1)} %dynamic_update_slice.3), channel_id=1, replica_groups=mesh['xy'=4,'core'=2,'hs'=4] {'xy','core','hs'}, use_global_device_ids=true, to_apply=%region_18.19 | all-reduce | flops 1280 | bytes 10240 | tf_op jit(solution)/shard_map/psum | solution.py:478
  765.8 61.5 %all-reduce.6.cloned.1.call-done = (bf16[1280,320]{0,1:T(8,128)(2,1)}, bf16[1280,320]{0,1:T(8,128)(2,1)}, bf16[1280,320]{0,1:T(8,128)(2,1)}, bf16[1280,320]{0,1:...) async-done(((bf16[1280,320]{0,1:T(8,128)(2,1)}, bf16[1280,320]{0,1:T(8,128)(2,1)}, ...) | async-done | bytes 6881296 | tf_op jit(solution)/shard_map/psum | solution.py:481
  (214 shorter events, 118.2 us)
Async XLA Ops:
  7.2 437.3 %copy-start = (bf16[448,1280]{1,0:T(8,128)(2,1)S(1)}, bf16[448,1280]{1,0:T(8,128)(2,1)}, u32[]{:S(2)}) copy-start(bf16[448,1280]{1,0:T(8,128)(2,1)} %param.27) | copy-start | bytes 3440644
  7.2 3.7 copy-start.43
  7.2 43.8 %all-gather.12.cloned.1.call-start = ((), (), s32[]{:S(2)}) async-start(), calls=%async_computation.8 | async-start | bytes 1638400 | tf_op jit(solution)/shard_map/all_gather | solution.py:355
  9.6 14.8 %copy-start.44 = (f32[1280]{0:T(1024)S(1)}, f32[1280]{0:T(1024)}, u32[]{:S(2)}) copy-start(f32[1280]{0:T(1024)} %param.18) | copy-start | bytes 15364
  10.5 13.2 %collective-permute-start = (bf16[1280,192]{0,1:T(8,128)(2,1)}, bf16[1280,192]{0,1:T(8,128)(2,1)S(1)}, u32[]{:S(2)}, u32[]{:S(2)}) collective-permute-start(bf16[1280,192]{0,1:T(8,128)(2,1)} %pad_maximum_fusion.1), channel_id=1, source_target_pairs={{0,1},{1,0},{2,3},{3,2},{4,5},{5,4},{6,7},{7,6},{8,9},{9,8},{10,11... | collective-permute-start | bytes 1474568 | tf_op jit(solution)/shard_map/ppermute | solution.py:341
  10.5 82.2 %all-gather.6.cloned.1.call-start = ((), (), s32[]{:S(2)}) async-start(), calls=%async_computation.4 | async-start | bytes 1638400 | tf_op jit(solution)/shard_map/all_gather | solution.py:377
  41.7 4.6 copy-start.40
  50.2 107.2 %all-gather.8.cloned.1.call-start = ((), (), s32[]{:S(2)}) async-start(), calls=%async_computation.5 | async-start | bytes 4096000 | tf_op jit(solution)/shard_map/all_gather | solution.py:354
  50.9 173.7 %all-gather.14.cloned.1.call-start = ((), (), s32[]{:S(2)}) async-start(), calls=%async_computation.9 | async-start | bytes 11796480 | tf_op jit(solution)/shard_map/all_gather | solution.py:356
  53.5 109.8 %copy-start.41 = (f32[1280]{0:T(1024)S(1)}, f32[1280]{0:T(1024)}, u32[]{:S(2)}) copy-start(f32[1280]{0:T(1024)} %param.23) | copy-start | bytes 15364
  53.5 236.8 %all-gather.10.cloned.1.call-start = ((), (), s32[]{:S(2)}) async-start(), calls=%async_computation.6 | async-start | bytes 11796480 | tf_op jit(solution)/shard_map/all_gather | solution.py:381
  163.2 12.9 %copy-start.19 = (bf16[1280,64]{0,1:T(8,128)(2,1)S(1)}, bf16[1280,64]{0,1:T(8,128)(2,1)}, u32[]{:S(2)}) copy-start(bf16[1280,64]{0,1:T(8,128)(2,1)} %param.24) | copy-start | bytes 491524
  164.6 326.3 %reduce-scatter.11.cloned.1.call-start = ((), (), s32[]{:S(2)}) async-start(), calls=%async_computation.10 | async-start | bytes 12533760 | tf_op jit(solution)/shard_map/reduce_scatter | solution.py:430
  406.4 169.9 %reduce-scatter.9.cloned.1.call-start = ((), (), s32[]{:S(2)}) async-start(), calls=%async_computation.7 | async-start | bytes 11796480 | tf_op jit(solution)/shard_map/reduce_scatter | solution.py:421
  440.0 202.1 %all-reduce.4.cloned.1.call-start = ((), (), s32[]{:S(2)}) async-start(), calls=%async_computation.11 | async-start | bytes 2785280 | tf_op jit(solution)/shard_map/psum | solution.py:432
  494.4 82.0 %copy-start.49 = (bf16[512,448]{0,1:T(8,128)(2,1)S(1)}, bf16[512,448]{0,1:T(8,128)(2,1)}, u32[]{:S(2)}) copy-start(bf16[512,448]{0,1:T(8,128)(2,1)} %get-tuple-element.115) | copy-start | bytes 1376260
  495.6 204.2 %reduce-scatter.13.cloned.1.call-start = ((), (), s32[]{:S(2)}) async-start(), calls=%async_computation.12 | async-start | bytes 1638400
  579.7 127.6 %reduce-scatter.15.cloned.1.call-start = ((), (), s32[]{:S(2)}) async-start(), calls=%async_computation.13 | async-start | bytes 1638400
  646.5 5.2 copy-start.46
  660.1 4.3 copy-start.13
  669.5 157.8 %all-reduce.6.cloned.1.call-start = ((), (), s32[]{:S(2)}) async-start(), calls=%async_computation.14 | async-start | bytes 13762560 | tf_op jit(solution)/shard_map/psum | solution.py:481
  675.1 3.7 copy-start.6
  675.1 3.7 copy-start.22
  827.3 3.8 copy-start.34
  (40 other events, 79.5 us)
Sparse Core Ops, SparseCore 0:
  10.6 35.5 all-gather.11
  50.3 42.2 all-gather.5
  94.2 63.1 all-gather.7
  159.7 64.9 all-gather.13
  227.0 63.2 all-gather.9
  406.5 84.2 reduce-scatter.10
  494.8 81.5 reduce-scatter.8
  579.5 62.6 all-reduce.3
  645.1 29.1 reduce-scatter.12
  677.2 29.9 reduce-scatter.14
  713.1 114.1 all-reduce.5

commit v3 on v2

--- a/solution.py
+++ b/solution.py
@@ -73,7 +73,7 @@
     else:
         rows_ref, slot_ref, x_ref, pick = refs
     local = slot_ref.shape[1]
-    rows = rows_ref[...]
+    rows = rows_ref[...] if weighted else rows_ref[0]
     masks = slot_masks(slot_ref, 0)
     if weighted:
         logits = nt(router_ref[...], rows)
@@ -85,15 +85,21 @@
             sw_ref[e] = jnp.sum(
                 jnp.where(masks[e], gates[e : e + 1, :], 0.0), axis=1, keepdims=True
             )
-    x_ref[...] = nn(pick[...], rows).astype(bf16).reshape(x_ref.shape)
+    product = nn if weighted else nt
+    x_ref[...] = product(pick[...], rows).astype(bf16).reshape(x_ref.shape)
 
 
 def spread(all_rows, slot, router_t=None):
     s, local, rows = slot.shape
-    width = all_rows.shape[1]
     weighted = router_t is not None
+    if weighted:
+        width = all_rows.shape[1]
+        block = pl.BlockSpec((rows, width), lambda i: (i, 0))
+    else:
+        width = all_rows.shape[1]
+        block = pl.BlockSpec((1, width, rows), lambda i: (i, 0, 0))
     in_specs = [
-        pl.BlockSpec((rows, width), lambda i: (i, 0)),
+        block,
         pl.BlockSpec((1, local, rows), lambda i: (i, 0, 0)),
     ]
     out_specs = [pl.BlockSpec((1, local, CAP, width), lambda i: (i, 0, 0, 0))]
@@ -264,10 +270,8 @@
         line = jnp.sum(jnp.where(masks[e], gsw_ref[e], 0.0), axis=0, keepdims=True)
         probs = jnp.where(number == first + e, line, probs)
     out_ref[0, :rows] = tn(pick[...], y_ref[...].reshape(pick.shape[0], -1)).astype(bf16)
-    half = experts // 2
-    out_ref[0, rows:] = jnp.zeros((half, out_ref.shape[2]), bf16)
-    out_ref[0, rows:, :rows] = probs[:half].astype(bf16)
-    out_ref[0, rows:, rows : 2 * rows] = probs[half:].astype(bf16)
+    out_ref[0, rows:] = jnp.zeros((experts, out_ref.shape[2]), bf16)
+    out_ref[0, rows:, :rows] = probs.astype(bf16)
 
 
 def collect(y, slot, gsw=None, first=None, experts=0):
@@ -287,7 +291,7 @@
         ]
         args += [gsw, first.reshape(1)]
         kernel = functools.partial(collect_back_kernel, experts)
-        tall = rows + experts // 2
+        tall = rows + experts
     return pl.pallas_call(
         kernel,
         grid=(s,),
@@ -298,6 +302,390 @@
         compiler_params=pltpu.CompilerParams(vmem_limit_bytes=VMEM_LIMIT),
         name="collect",
     )(*args)
+
+
+MESH = pl.DeviceIdType.MESH
+EXTRA = 64
+
+
+def places():
+    chip, core, z = lax.axis_index("xy"), lax.axis_index("core"), lax.axis_index("hs")
+    x, y = chip % 2, chip // 2
+    return chip, core, z, y * 2 + (1 - x), (1 - y) * 2 + x, (1 - y) * 2 + (1 - x)
+
+
+def greet(peers):
+    barrier = pltpu.get_barrier_semaphore()
+    for peer in peers:
+        pl.semaphore_signal(barrier, inc=1, device_id=peer, device_id_type=MESH)
+    pl.semaphore_wait(barrier, len(peers))
+
+
+def remote(src, dst, send, recv, peer):
+    return pltpu.make_async_remote_copy(
+        src_ref=src, dst_ref=dst, send_sem=send, recv_sem=recv, device_id=peer, device_id_type=MESH
+    )
+
+
+def gather_spread_kernel(
+    own_ref, slots_ref, router_ref, x_ref, sw_ref, slot_ref, held, pick, xbuf, send, recv, copied
+):
+    chip, core, z, cx, cy, cd = places()
+    other = 1 - core
+    x_peer, y_peer, c_peer = (cx, core, z), (cy, core, z), (chip, other, z)
+    tall = held.shape[1]
+    half = tall // 2
+    local, rows = slot_ref.shape[1:]
+    me = chip * 2 + core
+    top, low = pl.ds(0, half), pl.ds(half, half)
+
+    def at(c, k):
+        return c * 2 + k
+
+    def move(number, src_slot, part, peer):
+        return remote(
+            held.at[src_slot, part], held.at[src_slot, part], send.at[number], recv.at[number], peer
+        )
+
+    whole = pl.ds(0, tall)
+    greet([x_peer, y_peer, c_peer])
+    held[me, :rows] = own_ref[...]
+    held[me, rows:] = jnp.zeros((EXTRA, own_ref.shape[1]), bf16)
+    held[me, rows:, :rows] = slots_ref[...]
+    x_top, x_low = move(0, me, top, x_peer), move(1, me, low, x_peer)
+    y_low, y_top = move(2, me, low, y_peer), move(3, me, top, y_peer)
+    to_core = move(4, me, whole, c_peer)
+    relay_top, relay_low = move(5, at(cx, core), top, y_peer), move(6, at(cy, core), low, x_peer)
+    pass_x, pass_y = move(7, at(cx, core), whole, c_peer), move(8, at(cy, core), whole, c_peer)
+    pass_d = move(9, at(cd, core), whole, c_peer)
+    for copy in (x_top, y_low, x_low, y_top, to_core):
+        copy.start()
+
+    def arrived(number, slot, part):
+        move(number, slot, part, c_peer).wait_recv()
+
+    number = lax.broadcasted_iota(jnp.int32, (CAP, rows), 0)
+    first = me * local
+    line = lax.broadcasted_iota(jnp.int32, (local, EXTRA), 0)
+    column = lax.broadcasted_iota(jnp.int32, (local, EXTRA), 1)
+    chosen = (column == line + first).astype(f32).astype(bf16)
+
+    def out_copy(t, src):
+        return pltpu.make_async_copy(xbuf.at[t % 2], x_ref.at[src], copied.at[t % 2])
+
+    def step(t, carry):
+        @pl.when(t == 1)
+        def _():
+            arrived(4, at(chip, other), whole)
+
+        @pl.when(t == 2)
+        def _():
+            arrived(0, at(cx, core), top)
+            relay_top.start()
+            arrived(2, at(cy, core), low)
+            relay_low.start()
+            arrived(1, at(cx, core), low)
+            pass_x.start()
+
+        @pl.when(t == 3)
+        def _():
+            arrived(3, at(cy, core), top)
+            pass_y.start()
+            arrived(7, at(cx, other), whole)
+
+        @pl.when(t == 5)
+        def _():
+            arrived(8, at(cy, other), whole)
+
+        @pl.when(t == 6)
+        def _():
+            arrived(5, at(cd, core), top)
+            arrived(6, at(cd, core), low)
+            pass_d.start()
+
+        @pl.when(t == 7)
+        def _():
+            arrived(9, at(cd, other), whole)
+
+        x, y = (chip % 2 + (t // 2) % 2) % 2, (chip // 2 + t // 4) % 2
+        src = (y * 2 + x) * 2 + (core + t % 2) % 2
+        slots = nn(chosen, held[src, rows:, :rows]).astype(jnp.int32)
+        slot_ref[src] = slots
+        logits = nt(router_ref[...], held[src, :rows])
+        raised = jnp.exp(logits - jnp.max(logits, axis=0, keepdims=True))
+        gates = raised / jnp.sum(raised, axis=0, keepdims=True)
+        for e in range(local):
+            mask = slots[e : e + 1, :] == number
+            pick[e * CAP : (e + 1) * CAP, :] = mask.astype(f32).astype(bf16)
+            sw_ref[e, pl.ds(pl.multiple_of(src * CAP, 8), CAP), :] = jnp.sum(
+                jnp.where(mask, gates[e : e + 1, :], 0.0), axis=1, keepdims=True
+            )
+
+        @pl.when(t >= 2)
+        def _():
+            out_copy(t, src).wait()
+
+        xbuf[t % 2] = nn(pick[...], held[src, :rows]).astype(bf16).reshape(xbuf.shape[1:])
+        out_copy(t, src).start()
+        return carry
+
+    lax.fori_loop(0, 8, step, 0)
+    out_copy(0, me).wait()
+    out_copy(1, me).wait()
+    for copy in (x_top, x_low, y_low, y_top, to_core, relay_top, relay_low, pass_x, pass_y, pass_d):
+        copy.wait_send()
+
+
+def gather_spread(own, slots, router_t, local, ep_count):
+    rows, width = own.shape
+    tall = rows + EXTRA
+    vmem = pl.BlockSpec(memory_space=pltpu.VMEM)
+    return pl.pallas_call(
+        gather_spread_kernel,
+        in_specs=[vmem, vmem, vmem],
+        out_specs=[pl.BlockSpec(memory_space=pl.ANY), vmem, vmem],
+        out_shape=[
+            jax.ShapeDtypeStruct((ep_count, local, CAP, width), bf16),
+            jax.ShapeDtypeStruct((local, ep_count * CAP, 1), f32),
+            jax.ShapeDtypeStruct((ep_count, local, rows), jnp.int32),
+        ],
+        scratch_shapes=[
+            pltpu.VMEM((ep_count, tall, width), bf16),
+            pltpu.VMEM((local * CAP, rows), bf16),
+            pltpu.VMEM((2, local, CAP, width), bf16),
+            pltpu.SemaphoreType.DMA((10,)),
+            pltpu.SemaphoreType.DMA((10,)),
+            pltpu.SemaphoreType.DMA((2,)),
+        ],
+        compiler_params=pltpu.CompilerParams(
+            vmem_limit_bytes=VMEM_LIMIT, collective_id=0, has_side_effects=True
+        ),
+        name="gather_spread",
+    )(own, slots, router_t)
+
+
+def line_gather_kernel(own_ref, out_ref, held, send, recv):
+    chip, core, z, _, _, _ = places()
+    peers = [(chip, core, (z + i) % 4) for i in (1, 2, 3)]
+    greet(peers)
+    copies = [
+        remote(own_ref, held.at[i], send.at[i], recv.at[i], peer) for i, peer in enumerate(peers)
+    ]
+    for copy in (copies[1], copies[0], copies[2]):
+        copy.start()
+    out_ref[z] = own_ref[...]
+    for i in range(3):
+        copies[i].wait_recv()
+        out_ref[(z + 3 - i) % 4] = held[i]
+    for copy in copies:
+        copy.wait_send()
+
+
+def line_gather(own, collective_id):
+    vmem = pl.BlockSpec(memory_space=pltpu.VMEM)
+    return pl.pallas_call(
+        line_gather_kernel,
+        in_specs=[vmem],
+        out_specs=vmem,
+        out_shape=jax.ShapeDtypeStruct((4, *own.shape), own.dtype),
+        scratch_shapes=[
+            pltpu.VMEM((3, *own.shape), own.dtype),
+            pltpu.SemaphoreType.DMA((3,)),
+            pltpu.SemaphoreType.DMA((3,)),
+        ],
+        compiler_params=pltpu.CompilerParams(
+            vmem_limit_bytes=VMEM_LIMIT, collective_id=collective_id, has_side_effects=True
+        ),
+        name="line_gather",
+    )(own)
+
+
+def collect_sum_kernel(
+    y_ref,
+    slot_ref,
+    gsw_ref,
+    mine_ref,
+    out_ref,
+    pick,
+    ybuf,
+    stage,
+    given,
+    sums,
+    relay,
+    land,
+    zland,
+    total,
+    copied,
+    core_send,
+    core_recv,
+    send,
+    recv,
+    zsend,
+    zrecv,
+):
+    chip, core, z, cx, cy, cd = places()
+    other = 1 - core
+    x_peer, y_peer, c_peer = (cx, core, z), (cy, core, z), (chip, other, z)
+    z_peers = [(chip, core, (z + i) % 4) for i in (1, 2, 3)]
+    local, rows = slot_ref.shape[1:]
+    tall = out_ref.shape[0]
+    half, part = tall // 2, tall // 4
+    me = chip * 2 + core
+    top, low = pl.ds(0, half), pl.ds(half, half)
+    number = lax.broadcasted_iota(jnp.int32, (CAP, rows), 0)
+    row = lax.broadcasted_iota(jnp.int32, (EXTRA, rows), 0)
+
+    greet([x_peer, y_peer, c_peer, *z_peers])
+
+    def sequence(t):
+        p = t // 2
+        x, y = (chip % 2 + 1 + p // 2) % 2, (chip // 2 + 1 + p % 2) % 2
+        return (y * 2 + x) * 2 + (core + 1 + t % 2) % 2
+
+    def in_copy(t):
+        return pltpu.make_async_copy(y_ref.at[sequence(t)], ybuf.at[t % 2], copied.at[t % 2])
+
+    def to_core(p):
+        return remote(stage.at[p], given.at[p], core_send.at[p], core_recv.at[p], c_peer)
+
+    far_top = remote(sums.at[0, top], relay.at[0], send.at[0], recv.at[0], x_peer)
+    far_low = remote(sums.at[0, low], relay.at[1], send.at[1], recv.at[1], y_peer)
+    x_top = remote(sums.at[1, top], land.at[0, top], send.at[2], recv.at[2], x_peer)
+    x_low = remote(sums.at[1, low], land.at[0, low], send.at[3], recv.at[3], x_peer)
+    y_low = remote(sums.at[2, low], land.at[1, low], send.at[4], recv.at[4], y_peer)
+    y_top = remote(sums.at[2, top], land.at[1, top], send.at[5], recv.at[5], y_peer)
+
+    in_copy(0).start()
+
+    def step(t, carry):
+        @pl.when(t < 7)
+        def _():
+            in_copy(t + 1).start()
+
+        p, s = t // 2, sequence(t)
+        probs = jnp.zeros((EXTRA, rows), f32)
+        for e in range(local):
+            mask = slot_ref[s, e : e + 1, :] == number
+            pick[e * CAP : (e + 1) * CAP, :] = mask.astype(f32).astype(bf16)
+            column = gsw_ref[e, pl.ds(pl.multiple_of(s * CAP, 8), CAP), :]
+            line = jnp.sum(jnp.where(mask, column, 0.0), axis=0, keepdims=True)
+            probs = jnp.where(row == me * local + e, line, probs)
+        in_copy(t).wait()
+        back = tn(pick[...], ybuf[t % 2].reshape(local * CAP, -1))
+
+        @pl.when(t % 2 == 0)
+        def _():
+            stage[p, :rows] = back.astype(bf16)
+            stage[p, rows:] = jnp.zeros((tall - rows, back.shape[1]), bf16)
+            stage[p, rows:, :rows] = probs.astype(bf16)
+            to_core(p).start()
+
+        @pl.when(t % 2 == 1)
+        def _():
+            to_core(p).wait_recv()
+            sums[p, :rows] = (back + given[p, :rows].astype(f32)).astype(bf16)
+            sums[p, rows:] = given[p, rows:]
+            sums[p, rows:, :rows] = (probs + given[p, rows:, :rows].astype(f32)).astype(bf16)
+
+        @pl.when(t == 1)
+        def _():
+            far_top.start()
+            far_low.start()
+
+        @pl.when(t == 3)
+        def _():
+            x_top.start()
+
+        @pl.when(t == 5)
+        def _():
+            y_low.start()
+
+        return carry
+
+    lax.fori_loop(0, 8, step, 0)
+    far_low.wait_recv()
+    sums[1, half:] = (sums[1, half:].astype(f32) + relay[1].astype(f32)).astype(bf16)
+    x_low.start()
+    far_top.wait_recv()
+    sums[2, :half] = (sums[2, :half].astype(f32) + relay[0].astype(f32)).astype(bf16)
+    y_top.start()
+
+    def add_up(at):
+        return (
+            sums[3, at].astype(f32) + land[0, at].astype(f32) + land[1, at].astype(f32)
+        )
+
+    x_top.wait_recv()
+    y_top.wait_recv()
+    total[:half] = (add_up(slice(0, half)) + mine_ref[:half]).astype(bf16)
+    x_low.wait_recv()
+    y_low.wait_recv()
+    total[half:rows] = (add_up(slice(half, rows)) + mine_ref[half:]).astype(bf16)
+    total[rows:] = add_up(slice(rows, tall)).astype(bf16)
+
+    def block(q):
+        return pl.ds(pl.multiple_of(q * part, 16), part)
+
+    scatter = [
+        remote(total.at[block((z + i) % 4)], zland.at[i - 1], zsend.at[i - 1], zrecv.at[i - 1], z_peers[i - 1])
+        for i in (1, 2, 3)
+    ]
+    spread_ = [
+        remote(out_ref.at[block(z)], out_ref.at[block(z)], zsend.at[2 + i], zrecv.at[2 + i], z_peers[i - 1])
+        for i in (1, 2, 3)
+    ]
+    for i in (1, 0, 2):
+        scatter[i].start()
+    done = total[block(z)].astype(f32)
+    for i in range(3):
+        scatter[i].wait_recv()
+        done = done + zland[i].astype(f32)
+    out_ref[block(z)] = done.astype(bf16)
+    for i in (1, 0, 2):
+        spread_[i].start()
+    for i in (1, 2, 3):
+        theirs = block((z + 4 - i) % 4)
+        remote(out_ref.at[theirs], out_ref.at[theirs], zsend.at[2 + i], zrecv.at[2 + i], z_peers[i - 1]).wait_recv()
+    for copy in (far_top, far_low, x_top, x_low, y_low, y_top, *scatter, *spread_):
+        copy.wait_send()
+    for p in range(4):
+        to_core(p).wait_send()
+
+
+def collect_sum(y, slot, gsw, mine):
+    s, local, cap, width = y.shape
+    rows = slot.shape[2]
+    tall = rows + EXTRA
+    half = tall // 2
+    vmem = pl.BlockSpec(memory_space=pltpu.VMEM)
+    return pl.pallas_call(
+        collect_sum_kernel,
+        in_specs=[pl.BlockSpec(memory_space=pl.ANY), vmem, vmem, vmem],
+        out_specs=vmem,
+        out_shape=jax.ShapeDtypeStruct((tall, width), bf16),
+        scratch_shapes=[
+            pltpu.VMEM((local * cap, rows), bf16),
+            pltpu.VMEM((2, local, cap, width), bf16),
+            pltpu.VMEM((4, tall, width), bf16),
+            pltpu.VMEM((4, tall, width), bf16),
+            pltpu.VMEM((4, tall, width), bf16),
+            pltpu.VMEM((2, half, width), bf16),
+            pltpu.VMEM((2, tall, width), bf16),
+            pltpu.VMEM((3, tall // 4, width), bf16),
+            pltpu.VMEM((tall, width), bf16),
+            pltpu.SemaphoreType.DMA((2,)),
+            pltpu.SemaphoreType.DMA((4,)),
+            pltpu.SemaphoreType.DMA((4,)),
+            pltpu.SemaphoreType.DMA((6,)),
+            pltpu.SemaphoreType.DMA((6,)),
+            pltpu.SemaphoreType.DMA((6,)),
+            pltpu.SemaphoreType.DMA((6,)),
+        ],
+        compiler_params=pltpu.CompilerParams(
+            vmem_limit_bytes=VMEM_LIMIT, collective_id=2, has_side_effects=True
+        ),
+        name="collect_sum",
+    )(y, slot, gsw, mine)
 
 
 def shards(
@@ -351,10 +739,17 @@
     w_query = widened(attn_query, got[:, :spare])
     w_key = widened(attn_key, got[:, spare : 2 * spare])
     w_value = widened(attn_value, got[:, 2 * spare :])
+    small = ep_count == 8 and hs_count == 4
     out_full = lax.all_gather(attn_out, "hs", axis=1, tiled=True)
-    grad_full = lax.all_gather(out_grad, "hs", axis=1, tiled=True)
-    grad_all = lax.all_gather(grad_full, EP, axis=0, tiled=True)
-    routes_all = lax.all_gather(routes, EP, axis=0, tiled=True)
+    grad_all_t = lax.all_gather(out_grad.T, (*EP, "hs"), axis=0, tiled=True)
+    grad_all_t = grad_all_t.reshape(ep_count, width, rows)
+    grad_full = lax.dynamic_index_in_dim(grad_all_t, ep, 0, keepdims=False).T
+    positions = jnp.arange(rows, dtype=jnp.int32)
+    below = (positions[:, None] > positions[None, :]).astype(bf16)
+    chosen = jnp.any(
+        routes[:, :, None] == jnp.arange(experts, dtype=jnp.int32)[None, None, :], axis=1
+    )
+    own_slots = jnp.where(chosen, dot(below, chosen.astype(bf16)), -1.0).T.astype(bf16)
 
     x = tokens.astype(f32)
     rms1 = lax.rsqrt(jnp.mean(x * x, axis=-1, keepdims=True) + EPS)
@@ -365,7 +760,6 @@
     k = rope(dot(normed1, w_key).reshape(shape3), cosine, sine).astype(bf16)
     v = dot(normed1, w_value).astype(bf16).reshape(shape3)
     scale = 1.0 / math.sqrt(HEAD_DIM)
-    positions = jnp.arange(rows, dtype=jnp.int32)
     doc = documents[0]
     allowed = (positions[:, None] >= positions[None, :]) & (doc[:, None] == doc[None, :])
     scores = jnp.where(allowed[None], ein("qhd,khd->hqk", q, k) * scale, -1e30)
@@ -373,12 +767,15 @@
     raised = jnp.exp(scores - top)
     probs = raised / jnp.sum(raised, axis=-1, keepdims=True)
     probs_low = probs.astype(bf16)
-    attended3 = ein("hqk,khd->qhd", probs_low, v).reshape(rows, held).astype(bf16)
-    attended = lax.all_gather(own(attended3), "hs", axis=1, tiled=True)
-    residual = x + dot(attended, out_full)
+    attended3 = ein("khd,hqk->hdq", v, probs_low).astype(bf16).reshape(held, rows)
+    attended3 = jnp.where(odd, attended3[spare:], attended3[:quarter])
+    if small:
+        attended_t = line_gather(attended3, 1).reshape(width, rows)
+    else:
+        attended_t = lax.all_gather(attended3, "hs", axis=0, tiled=True)
+    residual = x + ein("ct,cd->td", attended_t, out_full)
     rms2 = lax.rsqrt(jnp.mean(residual * residual, axis=-1, keepdims=True) + EPS)
     normed2 = (residual * rms2 * ffn_gain).astype(bf16)
-    normed_all = lax.all_gather(normed2, EP, axis=0, tiled=True)
 
     sh_gate = dot(normed2, shared_gate)
     sh_up = dot(normed2, shared_up)
@@ -397,26 +794,23 @@
     )
 
     first = ep * local
-    mine = first + jnp.arange(local, dtype=jnp.int32)
-    chosen = jnp.any(
-        routes_all.reshape(ep_count, rows, -1)[:, :, :, None] == mine[None, None, None, :], axis=2
-    )
-    below = (positions[:, None] > positions[None, :]).astype(bf16)
-    rank = ein("tu,sue->ste", below, chosen.astype(bf16)).astype(jnp.int32)
-    slot = jnp.where(chosen, rank, -1).transpose(0, 2, 1)
     router_t = jnp.roll(router.T, -first, axis=0)
-
+    if small:
+        ex_in, slot_weight, slot = gather_spread(normed2, own_slots, router_t, local, ep_count)
+    else:
+        slot = lax.dynamic_slice_in_dim(
+            lax.all_gather(own_slots, EP, axis=0), first, local, 1
+        ).astype(jnp.int32)
+        normed_all = lax.all_gather(normed2, EP, axis=0, tiled=True)
+        ex_in, slot_weight = spread(normed_all, slot, router_t)
     gate_t, up_t = expert_gate.swapaxes(1, 2), expert_up.swapaxes(1, 2)
-    ex_grad = spread(grad_all, slot)
-    ex_in, slot_weight = spread(normed_all, slot, router_t)
+    ex_grad = spread(grad_all_t, slot)
     ex_out, ex_gate, ex_up = experts_forward(ex_in, slot_weight, gate_t, up_t, expert_down)
     out_part = collect(ex_out, slot).reshape(ep_count * rows, width)
     ex_back, grad_gate_t, grad_up_t, grad_expert_down, grad_slot_weight = experts_backward(
         ex_in, ex_grad, ex_gate, ex_up, slot_weight, gate_t, up_t, expert_down
     )
     grad_expert_gate, grad_expert_up = grad_gate_t.swapaxes(1, 2), grad_up_t.swapaxes(1, 2)
-    back_part = collect(ex_back, slot, grad_slot_weight, first, experts)
-    back_part = back_part.reshape(-1, width)
 
     out_rows = lax.psum_scatter(out_part, EP, scatter_dimension=0, tiled=True)
     out_rows = (out_rows.astype(f32) + shared_part).astype(bf16)
@@ -427,13 +821,15 @@
 
     output = (quarter_of(residual) + out_quarter.astype(f32)).astype(bf16)
 
-    back_rows = lax.psum_scatter(back_part, EP, scatter_dimension=0, tiled=True).astype(f32)
-    back_rows = jnp.concatenate([back_rows[:rows] + shared_back, back_rows[rows:]], axis=0)
-    back_rows = lax.psum(back_rows.astype(bf16), "hs").astype(f32)
+    if small:
+        back_rows = collect_sum(ex_back, slot, grad_slot_weight, shared_back).astype(f32)
+    else:
+        back_part = collect(ex_back, slot, grad_slot_weight, first, experts).reshape(-1, width)
+        back_rows = lax.psum_scatter(back_part, EP, scatter_dimension=0, tiled=True).astype(f32)
+        back_rows = jnp.concatenate([back_rows[:rows] + shared_back, back_rows[rows:]], axis=0)
+        back_rows = lax.psum(back_rows.astype(bf16), "hs").astype(f32)
     gate_own = jax.nn.softmax(dot(normed2, router), axis=-1)
-    grad_probs = jnp.concatenate(
-        [back_rows[rows:, :rows], back_rows[rows:, rows : 2 * rows]], axis=0
-    ).T
+    grad_probs = back_rows[rows:, :rows].T
     grad_logits = (
         gate_own * (grad_probs - jnp.sum(grad_probs * gate_own, axis=-1, keepdims=True))
     ).astype(bf16)
@@ -447,7 +843,7 @@
         - residual * rms2**3 * jnp.mean(u * residual, axis=-1, keepdims=True)
     )
     grad_low = grad_residual.astype(bf16)
-    grad_attn_out = ein("td,tc->dc", attended, quarter_of(grad_low))
+    grad_attn_out = dot(attended_t, quarter_of(grad_low))
     out_held = lax.dynamic_slice_in_dim(out_full, jnp.where(odd, col0 - spare, col0), held, 0)
     grad_attended = ein("tc,dc->td", grad_low, out_held).astype(bf16).reshape(shape3)
     grad_p = ein("qhd,khd->hqk", grad_attended, v)

time: 857 us -> 714 us (0.83)
  waiting for transfers between devices: 461 us -> 99.9 us
  Pallas kernels: 151 us -> 374 us
  blocking collectives: 74.7 us -> 63.1 us
    pallas_call x0 -> x3, Pallas kernels: none -> 259 us  [the longest x1 126 us: collect_sum(): pl.pallas_call(collect_sum_kernel, in_specs=[pl.BlockSpec(memory_space=pl...]
    all_gather x4 -> x1, waiting for transfers between devices: 136 us -> 0.01 us  [shards(): grad_all_t = lax.all_gather(out_grad.T, (*EP, 'hs'), axis=0, tiled=True)]
    reduce_scatter x1, waiting for transfers between devices: 80.1 us -> 0.02 us  [shards(): out_rows = lax.psum_scatter(out_part, EP, scatter_dimension=0, tiled=True)]
    all_gather x1, waiting for transfers between devices: 64.7 us -> 0.02 us  [shards(): out_full = lax.all_gather(attn_out, 'hs', axis=1, tiled=True)]
    psum x1 -> x0, waiting for transfers between devices: 62.4 us -> none  [shards(): back_rows = lax.psum(back_rows.astype(bf16), 'hs').astype(f32)]
    reduce_scatter x1 -> x0, waiting for transfers between devices: 41.1 us -> none  [shards(): lax.psum_scatter(back_part, EP, scatter_dimension=0, tiled=True).astype(f32)]
    psum x1, waiting for transfers between devices: 61.5 us -> 84.8 us  [over_ep(): return lax.psum(a.astype(bf16), EP).astype(f32)]
    pallas_call x2 -> x1, Pallas kernels: 37.5 us -> 17.7 us  [collect(): pl.pallas_call(kernel, grid=(s,), in_specs=in_specs, out_specs=pl.BlockSp...]
  transfers between devices with their start and end apart: 12 -> 7, of which waited for: 10 -> 2; matrix products, arithmetic and copies ran while one was open for 14% -> 18% of each run, Pallas kernels for 4% -> 53%
where the time goes in v3:
time: 714 us; the launch traced here: 700 us
  Pallas kernels  374 us (52%)
  waiting for transfers between devices  99.9 us (14%)
  blocking collectives  63.1 us (9%)
  matrix products  61.6 us (9%)
  local copies, waits for them, and re-layouts  46.1 us (6%)
  other arithmetic  40.2 us (6%)
  between operations  14.8 us (2%)
    pallas_call x1, Pallas kernels, collect_sum(): pl.pallas_call(collect_sum_kernel, in_specs=[pl.BlockSpec(memory_space=pl...  126 us
    psum x1, waiting for transfers between devices, over_ep(): return lax.psum(a.astype(bf16), EP).astype(f32)  84.8 us
    pallas_call x1, Pallas kernels, gather_spread(): pl.pallas_call(gather_spread_kernel, in_specs=[vmem, vmem, vmem], out_spe...  84.7 us
    pallas_call x1, Pallas kernels, experts_backward(): pl.pallas_call(functools.partial(experts_backward_kernel, groups), grid=(...  49.9 us
    pallas_call x1, Pallas kernels, line_gather(): pl.pallas_call(line_gather_kernel, in_specs=[vmem], out_specs=vmem, out_s...  47.4 us
    psum x1, blocking collectives, shards(): grad_attn_gain = lax.psum(gain_part, (*EP, 'hs'))  41.2 us
    dot_general x21, matrix products, ein(): return jnp.einsum(spec, a, b, preferred_element_type=f32)  37.3 us
    pallas_call x1, Pallas kernels, experts_forward(): pl.pallas_call(experts_forward_kernel, grid=(local, groups), in_specs=[sl...  30.6 us
  transfers between devices with their start and end apart: 7, of which 2 were waited for; matrix products, arithmetic and copies ran while one was open for 18% of the time, Pallas kernels for 53%

profile of v3, /device:TPU:9, one launch (start us, length us, event | category | flops | bytes accessed | tf_op | source)
XLA Modules:
  0.0 700.1 jit_solution(2218718847026762580)
XLA Ops:
  16.6 13.6 %collective-permute-done = bf16[1280,192]{0,1:T(8,128)(2,1)S(1)} collective-permute-done((bf16[1280,192]{0,1:T(8,128)(2,1)}, bf16[1280,192]{0,1:T(8,128)(2,1)S(1)}, u32[]{:S(2)}, u32[]{:S(2)}) %collective-permute-start) | collective-permute-done | bytes 491552 | tf_op jit(solution)/shard_map/ppermute | solution.py:729
  45.1 3.1 subtract_convert_fusion.3
  48.3 4.6 fusion.70
  56.5 47.4 %line_gather.1 = bf16[4,320,512]{2,1,0:T(8,128)(2,1)} custom-call(bf16[320,512]{1,0:T(8,128)(2,1)} %slice_select_fusion.3.own_ref), custom_call_target="tpu_custom_call" | custom-call | tf_op jit(solution)/shard_map/line_gather/pallas_call | solution.py:486
  103.9 4.4 multiply_reduce_fusion.3
  111.2 84.7 %gather_spread.1 = (bf16[8,8,112,1280]{3,2,1,0:T(8,128)(2,1)}, f32[8,896,1]{2,1,0:T(8,128)}, s32[8,8,512]{2,1,0:T(8,128)}) custom-call(bf16[512,1280]{1,0:T(8,128)(2,1)} %multiply_convert_fusion.1.own_ref, bf16[64,512]{1,0:T(8,128)(2,1)} %fusion.15.slots_ref, bf16[64,1280]{1,0:T(8,128)(2,1)} %fusion.54.router_ref), custom_call_target="tpu_custom_call" | custom-call | tf_op jit(solution)/shard_map/gather_spread/pallas_call | solution.py:443
  195.9 30.6 %experts_forward.1 = (bf16[8,8,112,1280]{3,2,1,0:T(8,128)(2,1)}, f32[8,896,256]{2,1,0:T(8,128)}, f32[8,896,256]{2,1,0:T(8,128)}) custom-call(bf16[8,8,112,1280]{3,2,1,0:T(8,128)(2,1)} %get-tuple-element.26.x_ref, f32[8,896,1]{2,1,0:T(8,128)} %get-tuple-element.27.sw_ref, bf16[8,224,1280]{2,1,0:T(8,128)(2,1)} %bitcast.93, bf16[8,224,1280]{2,1,0:T(8,128)(2,1)} %bitcast.95, ...), custom_call_target="tpu_custom_call" | custom-call | tf_op jit(solution)/shard_map/experts_forward/pallas_call | solution.py:222
  226.4 17.7 %collect.1 = bf16[8,512,1280]{2,1,0:T(8,128)(2,1)} custom-call(bf16[8,8,112,1280]{3,2,1,0:T(8,128)(2,1)} %get-tuple-element.28.y_ref, s32[8,8,512]{2,1,0:T(8,128)} %get-tuple-element.29.slot_ref.refs_1_), custom_call_target="tpu_custom_call" | custom-call | tf_op jit(solution)/shard_map/collect/pallas_call | solution.py:295
  244.1 14.3 %copy.106 = bf16[4096,1280]{0,1:T(8,128)(2,1)} copy(bf16[4096,1280]{1,0:T(8,128)(2,1)} %bitcast.92) | data formatting | bytes 20971520 | tf_op jit(solution)/shard_map/reshape | solution.py:809
  260.3 3.1 fusion.72
  265.1 17.1 %spread.1.gx_ref = bf16[8,8,112,1280]{3,2,1,0:T(8,128)(2,1)} custom-call(bf16[8,1280,512]{2,1,0:T(8,128)(2,1)} %bitcast.97, s32[8,8,512]{2,1,0:T(8,128)} %get-tuple-element.29.slot_ref.refs_1_), custom_call_target="tpu_custom_call" | custom-call | tf_op jit(solution)/shard_map/spread/pallas_call | solution.py:113
  282.2 2.5 constant_dynamic-slice_fusion
  287.1 49.9 %experts_backward.1 = (bf16[8,8,112,1280]{3,2,1,0:T(8,128)(2,1)}, f32[8,224,1280]{2,1,0:T(8,128)}, f32[8,224,1280]{2,1,0:T(8,128)}, f32[8,224,1280]{2,1,0:T(8,128)}, f32[8,896,1]{2,1,0:T(8,128)}) custom-call(bf16[8,8,112,1280]{3,2,1,0:T(8,128)(2,1)} %get-tuple-element.26.x_ref, bf16[8,8,112,1280]{3,2,1,0:T(8,128)(2,1)} %spread.1.gx_ref, ...), custom_call_target="tpu_custom_call" | custom-call | tf_op jit(solution)/shard_map/experts_backward/pallas_call | solution.py:239
  337.0 3.8 multiply_convert_fusion.3
  344.9 126.5 %collect_sum.1 = bf16[576,1280]{1,0:T(8,128)(2,1)} custom-call(bf16[8,8,112,1280]{3,2,1,0:T(8,128)(2,1)} %get-tuple-element.32.y_ref, s32[8,8,512]{2,1,0:T(8,128)} %get-tuple-element.29.slot_ref.refs_1_, f32[8,896,1]{2,1,0:T(8,128)} %get-tuple-element.33.gsw_ref, f32[512,1280]{1,0:T(8,128)} %convolution_add_fusion.3.mine_ref), custom_call_target="tpu_custom_call" | custom-call | tf_op jit(solution)/shard_map/collect_sum/pallas_call | solution.py:661
  477.8 2.9 convolution_convert_fusion.9
  500.0 3.4 fusion.4
  505.5 3.1 convolution_convert_fusion.6
  508.6 2.7 convolution_convert_fusion.5
  523.1 13.1 %psum.83 = f32[1280]{0:T(1024)} all-reduce(f32[1280]{0:T(1024)S(1)} %get-tuple-element.97), channel_id=1, replica_groups=mesh['xy'=4,'core'=2,'hs'=4] {'xy','core'}, use_global_device_ids=true, to_apply=%region_22.23 | all-reduce | flops 1280 | bytes 10240 | tf_op jit(solution)/shard_map/psum | solution.py:887
  539.2 8.8 %psum.77 = f32[512,1]{0,1:T(1,128)S(1)} all-reduce(f32[512,1]{0,1:T(1,128)S(1)} %bitcast.116), channel_id=1, replica_groups=mesh['xy'=4,'core'=2,'hs'=4] {'hs'}, use_global_device_ids=true, to_apply=%region_14.15 | all-reduce | flops 512 | bytes 4096 | tf_op jit(solution)/shard_map/psum | solution.py:870
  551.6 41.2 %psum.78 = f32[1280]{0:T(1024)} all-reduce(f32[1280]{0:T(1024)S(1)} %dynamic_update_slice.3), channel_id=1, replica_groups=mesh['xy'=4,'core'=2,'hs'=4] {'xy','core','hs'}, use_global_device_ids=true, to_apply=%region_16.17 | all-reduce | flops 1280 | bytes 10240 | tf_op jit(solution)/shard_map/psum | solution.py:874
  596.4 84.8 %all-reduce.3.cloned.1.call-done = (bf16[1280,320]{0,1:T(8,128)(2,1)}, bf16[1280,320]{0,1:T(8,128)(2,1)}, bf16[1280,320]{0,1:T(8,128)(2,1)}, bf16[1280,320]{0,1:...) async-done(((bf16[1280,320]{0,1:T(8,128)(2,1)}, bf16[1280,320]{0,1:T(8,128)(2,1)}, ...) | async-done | bytes 6881296 | tf_op jit(solution)/shard_map/psum | solution.py:877
  681.2 2.5 convert_element_type.165
  (186 shorter events, 99.3 us)
Async XLA Ops:
  7.2 329.8 %copy-start = (bf16[448,1280]{1,0:T(8,128)(2,1)S(1)}, bf16[448,1280]{1,0:T(8,128)(2,1)}, u32[]{:S(2)}) copy-start(bf16[448,1280]{1,0:T(8,128)(2,1)} %param.27) | copy-start | bytes 3440644
  7.2 4.6 copy-start.41
  7.2 4.8 copy-start.6
  7.2 96.7 %all-gather.3.cloned.1.call-start = ((), (), s32[]{:S(2)}) async-start(), calls=%async_computation.3 | async-start | bytes 4096000 | tf_op jit(solution)/shard_map/all_gather | solution.py:743
  8.0 257.2 %all-gather.5.cloned.1.call-start = ((), (), s32[]{:S(2)}) async-start(), calls=%async_computation.5 | async-start | bytes 10813440 | tf_op jit(solution)/shard_map/all_gather | solution.py:744
  8.0 5.3 copy-start.32
  8.7 491.3 %reduce-scatter.8.cloned.1.call-start = ((), (), s32[]{:S(2)}) async-start(), calls=%async_computation.4 | async-start | bytes 11796480 | tf_op jit(solution)/shard_map/reduce_scatter | solution.py:815
  8.8 5.3 copy-start.42
  11.0 20.0 %copy-start.43 = (f32[1280]{0:T(1024)S(1)}, f32[1280]{0:T(1024)}, u32[]{:S(2)}) copy-start(f32[1280]{0:T(1024)} %param.18) | copy-start | bytes 15364
  11.8 18.4 %collective-permute-start = (bf16[1280,192]{0,1:T(8,128)(2,1)}, bf16[1280,192]{0,1:T(8,128)(2,1)S(1)}, u32[]{:S(2)}, u32[]{:S(2)}) collective-permute-start(bf16[1280,192]{0,1:T(8,128)(2,1)} %pad_maximum_fusion), channel_id=1, source_target_pairs={{0,1},{1,0},{2,3},{3,2},{4,5},{5,4},{6,7},{7,6},{8,9},{9,8},{10,11... | collective-permute-start | bytes 1474568 | tf_op jit(solution)/shard_map/ppermute | solution.py:729
  48.3 4.6 copy-start.39
  103.9 5.9 copy-start.40
  258.5 277.8 %reduce-scatter.12.cloned.1.call-start = ((), (), s32[]{:S(2)}) async-start(), calls=%async_computation.7 | async-start | bytes 1638400
  260.3 3.1 copy-start.21
  337.0 3.9 copy-start.26
  477.8 3.6 copy-start.14
  477.8 3.0 copy-start.11
  499.7 93.1 %reduce-scatter.10.cloned.1.call-start = ((), (), s32[]{:S(2)}) async-start(), calls=%async_computation.6 | async-start | bytes 1638400
  503.4 177.8 %all-reduce.3.cloned.1.call-start = ((), (), s32[]{:S(2)}) async-start(), calls=%async_computation.8 | async-start | bytes 13762560 | tf_op jit(solution)/shard_map/psum | solution.py:877
  503.5 5.1 copy-start.7
  681.2 3.8 copy-start.30
  683.7 2.6 copy-start.29
  685.0 2.6 copy-start.38
  685.0 3.3 copy-start.25
  (30 other events, 46.4 us)
Sparse Core Ops, SparseCore 0:
  9.6 76.2 all-gather.2
  88.8 113.6 all-gather.4
  258.6 79.2 reduce-scatter.7
  499.8 29.5 reduce-scatter.11
  532.1 30.2 reduce-scatter.9
  567.6 113.5 all-reduce.2

commit v4 on v3

--- a/solution.py
+++ b/solution.py
@@ -5,6 +5,7 @@
 import jax.numpy as jnp
 from jax import lax
 from jax.experimental import pallas as pl
+from jax.experimental.layout import Layout, with_layout_constraint
 from jax.experimental.pallas import tpu as pltpu
 from jax.sharding import Mesh
 from jax.sharding import PartitionSpec as P
@@ -29,20 +30,20 @@
 def rope_tables(rows):
     half = HEAD_DIM // 2
     frequency = 10000.0 ** (-jnp.arange(half, dtype=f32) * 2.0 / HEAD_DIM)
-    angles = jnp.arange(rows, dtype=f32)[:, None] * frequency[None, :]
-    return jnp.cos(angles)[:, None, :], jnp.sin(angles)[:, None, :]
+    angles = frequency[:, None] * jnp.arange(rows, dtype=f32)[None, :]
+    return jnp.cos(angles), jnp.sin(angles)
 
 
 def rope(v, cosine, sine):
     half = HEAD_DIM // 2
-    a, b = v[..., :half], v[..., half:]
-    return jnp.concatenate([a * cosine - b * sine, b * cosine + a * sine], axis=-1)
+    a, b = v[:, :half], v[:, half:]
+    return jnp.concatenate([a * cosine - b * sine, b * cosine + a * sine], axis=1)
 
 
 def rope_back(v, cosine, sine):
     half = HEAD_DIM // 2
-    a, b = v[..., :half], v[..., half:]
-    return jnp.concatenate([a * cosine + b * sine, b * cosine - a * sine], axis=-1)
+    a, b = v[:, :half], v[:, half:]
+    return jnp.concatenate([a * cosine + b * sine, b * cosine - a * sine], axis=1)
 
 
 VMEM_LIMIT = 60 * 1024 * 1024
@@ -59,6 +60,10 @@
 
 def tn(a, b):
     return lax.dot_general(a, b, (((0,), (0,)), ((), ())), preferred_element_type=f32)
+
+
+def takes(microseconds):
+    return pl.CostEstimate(flops=0, transcendentals=0, bytes_accessed=microseconds * 3_000_000)
 
 
 def slot_masks(slot_ref, at):
@@ -118,6 +123,7 @@
         out_shape=out_shape,
         scratch_shapes=[pltpu.VMEM((local * CAP, rows), bf16)],
         compiler_params=pltpu.CompilerParams(vmem_limit_bytes=VMEM_LIMIT),
+        cost_estimate=takes(17),
         name="spread",
     )(*args)
     return out if weighted else out[0]
@@ -227,6 +233,7 @@
         out_shape=[jax.ShapeDtypeStruct(x.shape, bf16), middle, middle],
         scratch_shapes=[pltpu.VMEM((PAD, width), bf16)] * 3,
         compiler_params=pltpu.CompilerParams(vmem_limit_bytes=VMEM_LIMIT),
+        cost_estimate=takes(31),
         name="experts_forward",
     )(x, sw, wg, wu, wd)
 
@@ -247,6 +254,7 @@
         + [jax.ShapeDtypeStruct((local, rows, 1), f32)],
         scratch_shapes=[pltpu.VMEM((PAD, width), bf16)] * 3,
         compiler_params=pltpu.CompilerParams(vmem_limit_bytes=VMEM_LIMIT),
+        cost_estimate=takes(47),
         name="experts_backward",
     )(x, gx, gate, up, sw, wg, wu, wd)
 
@@ -300,6 +308,7 @@
         out_shape=jax.ShapeDtypeStruct((s, tall, width), bf16),
         scratch_shapes=[pltpu.VMEM((local * cap, rows), bf16)],
         compiler_params=pltpu.CompilerParams(vmem_limit_bytes=VMEM_LIMIT),
+        cost_estimate=takes(17),
         name="collect",
     )(*args)
 
@@ -325,6 +334,81 @@
     return pltpu.make_async_remote_copy(
         src_ref=src, dst_ref=dst, send_sem=send, recv_sem=recv, device_id=peer, device_id_type=MESH
     )
+
+
+def block(q, size):
+    return pl.ds(pl.multiple_of(q * size, 16), size)
+
+
+def weight_sum(grads, given, half, land, out_ref, csend, crecv, send, recv):
+    chip, core, z, cx, cy, cd = places()
+    other = 1 - core
+    c_peer = (chip, other, z)
+    chips = (cx, cy, cd)
+    count = grads.shape[0] // 2
+    piece = count // 4
+
+    to_core = remote(grads.at[block(other, count)], given, csend.at[0], crecv.at[0], c_peer)
+    scatter = [
+        remote(half.at[block(c, piece)], land.at[i], send.at[i], recv.at[i], (c, core, z))
+        for i, c in enumerate(chips)
+    ]
+
+    def share():
+        to_core.wait_recv()
+        half[...] = (grads[block(core, count)].astype(f32) + given[...].astype(f32)).astype(bf16)
+        for i in (2, 0, 1):
+            scatter[i].start()
+
+    def place(c, k):
+        return pl.ds(pl.multiple_of(k * count + c * piece, 16), piece)
+
+    def give(number, c, k, sems, peer):
+        return remote(out_ref.at[place(c, k)], out_ref.at[place(c, k)], *sems(number), peer)
+
+    def chip_sems(i):
+        return send.at[3 + i], recv.at[3 + i]
+
+    def core_sems(i):
+        return csend.at[1 + i], crecv.at[1 + i]
+
+    gather = [give(i, chip, core, chip_sems, (c, core, z)) for i, c in enumerate(chips)]
+    over = [give(i, c, core, core_sems, c_peer) for i, c in enumerate((*chips, chip))]
+
+    def give_back():
+        done = half[block(chip, piece)].astype(f32)
+        for i in range(3):
+            scatter[i].wait_recv()
+            done = done + land[i].astype(f32)
+        out_ref[place(chip, core)] = done.astype(bf16)
+        for i in (2, 0, 1):
+            gather[i].start()
+        over[3].start()
+
+    def end():
+        for i, c in enumerate(chips):
+            give(i, c, core, chip_sems, (c, core, z)).wait_recv()
+            over[i].start()
+        for i, c in enumerate((*chips, chip)):
+            give(i, c, other, core_sems, c_peer).wait_recv()
+        for copy in (to_core, *scatter, *gather, *over):
+            copy.wait_send()
+
+    return to_core.start, share, give_back, end
+
+
+def weight_sum_scratch(tall, width):
+    dma = pltpu.SemaphoreType.DMA
+    return [
+        pltpu.VMEM((tall, width), bf16),
+        pltpu.VMEM((tall // 2, width), bf16),
+        pltpu.VMEM((tall // 2, width), bf16),
+        pltpu.VMEM((3, tall // 8, width), bf16),
+        dma((5,)),
+        dma((5,)),
+        dma((6,)),
+        dma((6,)),
+    ]
 
 
 def gather_spread_kernel(
@@ -460,6 +544,7 @@
         compiler_params=pltpu.CompilerParams(
             vmem_limit_bytes=VMEM_LIMIT, collective_id=0, has_side_effects=True
         ),
+        cost_estimate=takes(62),
         name="gather_spread",
     )(own, slots, router_t)
 
@@ -496,6 +581,7 @@
         compiler_params=pltpu.CompilerParams(
             vmem_limit_bytes=VMEM_LIMIT, collective_id=collective_id, has_side_effects=True
         ),
+        cost_estimate=takes(30),
         name="line_gather",
     )(own)
 
@@ -505,7 +591,11 @@
     slot_ref,
     gsw_ref,
     mine_ref,
+    shared_gate_ref,
+    shared_up_ref,
+    shared_down_ref,
     out_ref,
+    sum_ref,
     pick,
     ybuf,
     stage,
@@ -522,6 +612,8 @@
     recv,
     zsend,
     zrecv,
+    grads,
+    *more,
 ):
     chip, core, z, cx, cy, cd = places()
     other = 1 - core
@@ -535,7 +627,7 @@
     number = lax.broadcasted_iota(jnp.int32, (CAP, rows), 0)
     row = lax.broadcasted_iota(jnp.int32, (EXTRA, rows), 0)
 
-    greet([x_peer, y_peer, c_peer, *z_peers])
+    greet([x_peer, y_peer, c_peer, (cd, core, z), *z_peers])
 
     def sequence(t):
         p = t // 2
@@ -556,6 +648,13 @@
     y_top = remote(sums.at[2, top], land.at[1, top], send.at[5], recv.at[5], y_peer)
 
     in_copy(0).start()
+    start, share, give_back, end = weight_sum(grads, *more[:3], sum_ref, *more[3:])
+    at = 0
+    for ref in (shared_gate_ref, shared_up_ref, shared_down_ref):
+        grads[at : at + ref.shape[0]] = ref[...]
+        at += ref.shape[0]
+    grads[at:] = jnp.zeros((grads.shape[0] - at, grads.shape[1]), bf16)
+    start()
 
     def step(t, carry):
         @pl.when(t < 7)
@@ -609,6 +708,7 @@
     far_top.wait_recv()
     sums[2, :half] = (sums[2, :half].astype(f32) + relay[0].astype(f32)).astype(bf16)
     y_top.start()
+    share()
 
     def add_up(at):
         return (
@@ -623,28 +723,27 @@
     total[half:rows] = (add_up(slice(half, rows)) + mine_ref[half:]).astype(bf16)
     total[rows:] = add_up(slice(rows, tall)).astype(bf16)
 
-    def block(q):
-        return pl.ds(pl.multiple_of(q * part, 16), part)
-
     scatter = [
-        remote(total.at[block((z + i) % 4)], zland.at[i - 1], zsend.at[i - 1], zrecv.at[i - 1], z_peers[i - 1])
+        remote(total.at[block((z + i) % 4, part)], zland.at[i - 1], zsend.at[i - 1], zrecv.at[i - 1], z_peers[i - 1])
         for i in (1, 2, 3)
     ]
     spread_ = [
-        remote(out_ref.at[block(z)], out_ref.at[block(z)], zsend.at[2 + i], zrecv.at[2 + i], z_peers[i - 1])
+        remote(out_ref.at[block(z, part)], out_ref.at[block(z, part)], zsend.at[2 + i], zrecv.at[2 + i], z_peers[i - 1])
         for i in (1, 2, 3)
     ]
     for i in (1, 0, 2):
         scatter[i].start()
-    done = total[block(z)].astype(f32)
+    give_back()
+    done = total[block(z, part)].astype(f32)
     for i in range(3):
         scatter[i].wait_recv()
         done = done + zland[i].astype(f32)
-    out_ref[block(z)] = done.astype(bf16)
+    out_ref[block(z, part)] = done.astype(bf16)
     for i in (1, 0, 2):
         spread_[i].start()
+    end()
     for i in (1, 2, 3):
-        theirs = block((z + 4 - i) % 4)
+        theirs = block((z + 4 - i) % 4, part)
         remote(out_ref.at[theirs], out_ref.at[theirs], zsend.at[2 + i], zrecv.at[2 + i], z_peers[i - 1]).wait_recv()
     for copy in (far_top, far_low, x_top, x_low, y_low, y_top, *scatter, *spread_):
         copy.wait_send()
@@ -652,17 +751,21 @@
         to_core(p).wait_send()
 
 
-def collect_sum(y, slot, gsw, mine):
+def collect_sum(y, slot, gsw, mine, *shared):
     s, local, cap, width = y.shape
     rows = slot.shape[2]
     tall = rows + EXTRA
     half = tall // 2
+    weights = 128 * (-(-sum(a.shape[0] for a in shared) // 128))
     vmem = pl.BlockSpec(memory_space=pltpu.VMEM)
     return pl.pallas_call(
         collect_sum_kernel,
-        in_specs=[pl.BlockSpec(memory_space=pl.ANY), vmem, vmem, vmem],
-        out_specs=vmem,
-        out_shape=jax.ShapeDtypeStruct((tall, width), bf16),
+        in_specs=[pl.BlockSpec(memory_space=pl.ANY)] + [vmem] * 6,
+        out_specs=[vmem, vmem],
+        out_shape=[
+            jax.ShapeDtypeStruct((tall, width), bf16),
+            jax.ShapeDtypeStruct((weights, width), bf16),
+        ],
         scratch_shapes=[
             pltpu.VMEM((local * cap, rows), bf16),
             pltpu.VMEM((2, local, cap, width), bf16),
@@ -680,12 +783,158 @@
             pltpu.SemaphoreType.DMA((6,)),
             pltpu.SemaphoreType.DMA((6,)),
             pltpu.SemaphoreType.DMA((6,)),
+            *weight_sum_scratch(weights, width),
         ],
         compiler_params=pltpu.CompilerParams(
             vmem_limit_bytes=VMEM_LIMIT, collective_id=2, has_side_effects=True
         ),
+        cost_estimate=takes(131),
         name="collect_sum",
-    )(y, slot, gsw, mine)
+    )(y, slot, gsw, mine, *shared)
+
+
+def finish_kernel(
+    dq_ref,
+    dk_ref,
+    dv_ref,
+    low_ref,
+    wq_ref,
+    wk_ref,
+    wv_ref,
+    normed_ref,
+    attended_ref,
+    x_ref,
+    gain_ref,
+    rms_ref,
+    back_ref,
+    router_ref,
+    ffn_ref,
+    tokens_ref,
+    sum_ref,
+    part,
+    low_part,
+    zland,
+    mine,
+    theirs,
+    zsend,
+    zrecv,
+    lsend,
+    lrecv,
+    grads,
+    given,
+    half,
+    land,
+    csend,
+    crecv,
+    send,
+    recv,
+):
+    chip, core, z, cx, cy, cd = places()
+    other = 1 - core
+    c_peer = (chip, other, z)
+    chips = (cx, cy, cd)
+    z_peers = [(chip, core, (z + i) % 4) for i in (1, 2, 3)]
+    quarter, rows = dq_ref.shape
+    width = x_ref.shape[0]
+    tall = grads.shape[0]
+    experts = router_ref.shape[0]
+
+    greet([c_peer, *[(c, core, z) for c in chips], *z_peers])
+
+    part[...] = tn(wq_ref[...], dq_ref[...])
+    part[...] += tn(wk_ref[...], dk_ref[...])
+    part[...] += tn(wv_ref[...], dv_ref[...])
+    low_part[...] = part[...].astype(bf16)
+    to_z = [
+        remote(
+            low_part.at[block((z + i) % 4, quarter)],
+            zland.at[i - 1],
+            zsend.at[i - 1],
+            zrecv.at[i - 1],
+            z_peers[i - 1],
+        )
+        for i in (1, 2, 3)
+    ]
+    few_to_z = [
+        remote(mine, theirs.at[i], lsend.at[i], lrecv.at[i], peer) for i, peer in enumerate(z_peers)
+    ]
+    along = part[...] * x_ref[...].astype(f32)
+    mine[...] = jnp.zeros(mine.shape, f32)
+    mine[0:1, :rows] = jnp.sum(along * gain_ref[...], axis=0, keepdims=True)
+    mine[:, rows:] = nt(jnp.ones((8, rows), bf16), (along * rms_ref[...]).astype(bf16))
+    for copy in few_to_z:
+        copy.start()
+    for i in (1, 0, 2):
+        to_z[i].start()
+
+    normed = normed_ref[...]
+    for i, ref in enumerate((dq_ref, dk_ref, dv_ref)):
+        grads[i * quarter : (i + 1) * quarter] = nn(ref[...], normed).astype(bf16)
+    grads[3 * quarter : 4 * quarter] = nt(low_ref[...], attended_ref[...]).astype(bf16)
+    at = 4 * quarter
+    grads[at : at + experts] = router_ref[...].astype(bf16)
+    for copy in few_to_z:
+        copy.wait_recv()
+    few = mine[...] + theirs[0] + theirs[1] + theirs[2]
+    grads[at + experts :] = jnp.zeros((tall - at - experts, width), bf16)
+    line = lax.broadcasted_iota(jnp.int32, (16, width), 0)
+    gains = jnp.where(line == 0, few[0:1, rows:], jnp.where(line == 1, ffn_ref[...], 0.0))
+    grads[at + experts : at + experts + 16] = gains.astype(bf16)
+
+    start, share, give_back, end = weight_sum(
+        grads, given, half, land, sum_ref, csend, crecv, send, recv
+    )
+    start()
+    share()
+
+    own = block(z, quarter)
+    total = part[own]
+    for i in range(3):
+        to_z[i].wait_recv()
+        total = total + zland[i].astype(f32)
+    rms = rms_ref[...]
+    x = x_ref[own].astype(f32)
+    mean = few[0:1, :rows] * (1.0 / width)
+    tokens_ref[...] = back_ref[...] + rms * gain_ref[own] * total - x * (rms * rms * rms * mean)
+
+    give_back()
+    end()
+    for copy in (*to_z, *few_to_z):
+        copy.wait_send()
+
+
+def finish(*args):
+    quarter, rows = args[0].shape
+    width = args[9].shape[0]
+    tall = 4 * quarter + 128
+    vmem = pl.BlockSpec(memory_space=pltpu.VMEM)
+    dma = pltpu.SemaphoreType.DMA
+    return pl.pallas_call(
+        finish_kernel,
+        in_specs=[vmem] * len(args),
+        out_specs=[vmem, vmem],
+        out_shape=[
+            jax.ShapeDtypeStruct((quarter, rows), f32),
+            jax.ShapeDtypeStruct((tall, width), bf16),
+        ],
+        scratch_shapes=[
+            pltpu.VMEM((width, rows), f32),
+            pltpu.VMEM((width, rows), bf16),
+            pltpu.VMEM((3, quarter, rows), bf16),
+            pltpu.VMEM((8, rows + width), f32),
+            pltpu.VMEM((3, 8, rows + width), f32),
+            dma((3,)),
+            dma((3,)),
+            dma((3,)),
+            dma((3,)),
+            *weight_sum_scratch(tall, width),
+        ],
+        compiler_params=pltpu.CompilerParams(
+            vmem_limit_bytes=VMEM_LIMIT, collective_id=3, has_side_effects=True
+        ),
+        cost_estimate=takes(70),
+        name="finish",
+    )(*args)
 
 
 def shards(
@@ -721,24 +970,26 @@
     heads = held // HEAD_DIM
     col0 = hs * quarter
 
+    query_t, key_t, value_t = attn_query.T, attn_key.T, attn_value.T
+
     def outer(w):
-        return jnp.where(odd, w[:, :spare], w[:, quarter - spare :])
+        return jnp.where(odd, w[:spare], w[quarter - spare :])
 
     pairs = [(i, i ^ 1) for i in range(hs_count)]
-    sent = jnp.concatenate([outer(attn_query), outer(attn_key), outer(attn_value)], axis=1)
+    sent = jnp.concatenate([outer(query_t), outer(key_t), outer(value_t)], axis=0)
     got = lax.ppermute(sent, "hs", pairs)
 
     def widened(w, extra):
         return jnp.where(
-            odd, jnp.concatenate([extra, w], axis=1), jnp.concatenate([w, extra], axis=1)
+            odd, jnp.concatenate([extra, w], axis=0), jnp.concatenate([w, extra], axis=0)
         )
 
     def own(v):
-        return jnp.where(odd, v[:, spare:], v[:, :quarter])
-
-    w_query = widened(attn_query, got[:, :spare])
-    w_key = widened(attn_key, got[:, spare : 2 * spare])
-    w_value = widened(attn_value, got[:, 2 * spare :])
+        return jnp.where(odd, v[spare:], v[:quarter])
+
+    w_query = widened(query_t, got[:spare])
+    w_key = widened(key_t, got[spare : 2 * spare])
+    w_value = widened(value_t, got[2 * spare :])
     small = ep_count == 8 and hs_count == 4
     out_full = lax.all_gather(attn_out, "hs", axis=1, tiled=True)
     grad_all_t = lax.all_gather(out_grad.T, (*EP, "hs"), axis=0, tiled=True)
@@ -755,20 +1006,19 @@
     rms1 = lax.rsqrt(jnp.mean(x * x, axis=-1, keepdims=True) + EPS)
     normed1 = (x * rms1 * attn_gain).astype(bf16)
     cosine, sine = rope_tables(rows)
-    shape3 = (rows, heads, HEAD_DIM)
-    q = rope(dot(normed1, w_query).reshape(shape3), cosine, sine).astype(bf16)
-    k = rope(dot(normed1, w_key).reshape(shape3), cosine, sine).astype(bf16)
-    v = dot(normed1, w_value).astype(bf16).reshape(shape3)
+    shape3 = (heads, HEAD_DIM, rows)
+    q = rope(ein("cd,td->ct", w_query, normed1).reshape(shape3), cosine, sine).astype(bf16)
+    k = rope(ein("cd,td->ct", w_key, normed1).reshape(shape3), cosine, sine).astype(bf16)
+    v = ein("cd,td->ct", w_value, normed1).astype(bf16).reshape(shape3)
     scale = 1.0 / math.sqrt(HEAD_DIM)
     doc = documents[0]
     allowed = (positions[:, None] >= positions[None, :]) & (doc[:, None] == doc[None, :])
-    scores = jnp.where(allowed[None], ein("qhd,khd->hqk", q, k) * scale, -1e30)
+    scores = jnp.where(allowed[None], ein("hdq,hdk->hqk", q, k) * scale, -1e30)
     top = jnp.max(scores, axis=-1, keepdims=True)
     raised = jnp.exp(scores - top)
     probs = raised / jnp.sum(raised, axis=-1, keepdims=True)
     probs_low = probs.astype(bf16)
-    attended3 = ein("khd,hqk->hdq", v, probs_low).astype(bf16).reshape(held, rows)
-    attended3 = jnp.where(odd, attended3[spare:], attended3[:quarter])
+    attended3 = own(ein("hdk,hqk->hdq", v, probs_low).astype(bf16).reshape(held, rows))
     if small:
         attended_t = line_gather(attended3, 1).reshape(width, rows)
     else:
@@ -787,11 +1037,13 @@
     grad_sh_gate = (grad_sh * sh_up * sh_sig * (1 + sh_gate * (1 - sh_sig))).astype(bf16)
     grad_sh_up = (grad_sh * sh_act).astype(bf16)
     grad_shared_down = ein("tf,td->fd", sh_hidden, grad_full)
-    grad_shared_gate = ein("td,tf->df", normed2, grad_sh_gate)
-    grad_shared_up = ein("td,tf->df", normed2, grad_sh_up)
+    grad_shared_gate = ein("tf,td->fd", grad_sh_gate, normed2)
+    grad_shared_up = ein("tf,td->fd", grad_sh_up, normed2)
     shared_back = ein("tf,df->td", grad_sh_gate, shared_gate) + ein(
         "tf,df->td", grad_sh_up, shared_up
     )
+
+    shared_grads = [a.astype(bf16) for a in (grad_shared_gate, grad_shared_up, grad_shared_down)]
 
     first = ep * local
     router_t = jnp.roll(router.T, -first, axis=0)
@@ -812,7 +1064,10 @@
     )
     grad_expert_gate, grad_expert_up = grad_gate_t.swapaxes(1, 2), grad_up_t.swapaxes(1, 2)
 
+    rows_major = Layout(major_to_minor=(0, 1))
+    out_part = with_layout_constraint(out_part, rows_major)
     out_rows = lax.psum_scatter(out_part, EP, scatter_dimension=0, tiled=True)
+    out_rows = with_layout_constraint(out_rows, rows_major)
     out_rows = (out_rows.astype(f32) + shared_part).astype(bf16)
     out_quarter = lax.psum_scatter(out_rows, "hs", scatter_dimension=1, tiled=True)
 
@@ -822,18 +1077,24 @@
     output = (quarter_of(residual) + out_quarter.astype(f32)).astype(bf16)
 
     if small:
-        back_rows = collect_sum(ex_back, slot, grad_slot_weight, shared_back).astype(f32)
+        back_rows, shared_sums = collect_sum(
+            ex_back, slot, grad_slot_weight, shared_back, *shared_grads
+        )
+        back_rows, shared_sums = back_rows.astype(f32), shared_sums.astype(f32)
+        hidden_units = shared_down.shape[0]
+        shared_sums = [shared_sums[i * hidden_units : (i + 1) * hidden_units] for i in range(3)]
     else:
         back_part = collect(ex_back, slot, grad_slot_weight, first, experts).reshape(-1, width)
         back_rows = lax.psum_scatter(back_part, EP, scatter_dimension=0, tiled=True).astype(f32)
         back_rows = jnp.concatenate([back_rows[:rows] + shared_back, back_rows[rows:]], axis=0)
         back_rows = lax.psum(back_rows.astype(bf16), "hs").astype(f32)
+        shared_sums = [lax.psum(a, EP).astype(f32) for a in shared_grads]
     gate_own = jax.nn.softmax(dot(normed2, router), axis=-1)
     grad_probs = back_rows[rows:, :rows].T
     grad_logits = (
         gate_own * (grad_probs - jnp.sum(grad_probs * gate_own, axis=-1, keepdims=True))
     ).astype(bf16)
-    grad_router = ein("td,te->de", normed2, grad_logits)
+    grad_router = ein("te,td->ed", grad_logits, normed2)
     grad_normed2 = back_rows[:rows] + ein("te,de->td", grad_logits, router)
     grad_ffn_gain = jnp.sum(grad_normed2 * residual * rms2, axis=0)
     u = grad_normed2 * ffn_gain
@@ -843,52 +1104,80 @@
         - residual * rms2**3 * jnp.mean(u * residual, axis=-1, keepdims=True)
     )
     grad_low = grad_residual.astype(bf16)
-    grad_attn_out = dot(attended_t, quarter_of(grad_low))
     out_held = lax.dynamic_slice_in_dim(out_full, jnp.where(odd, col0 - spare, col0), held, 0)
-    grad_attended = ein("tc,dc->td", grad_low, out_held).astype(bf16).reshape(shape3)
-    grad_p = ein("qhd,khd->hqk", grad_attended, v)
-    grad_v = ein("hqk,qhd->khd", probs_low, grad_attended).astype(bf16)
+    grad_attended = ein("cd,td->ct", out_held, grad_low).astype(bf16).reshape(shape3)
+    grad_p = ein("hdq,hdk->hqk", grad_attended, v)
+    grad_v = ein("hdq,hqk->hdk", grad_attended, probs_low).astype(bf16)
     grad_s = (probs * (grad_p - jnp.sum(probs * grad_p, axis=-1, keepdims=True))).astype(bf16)
-    grad_q = ein("hqk,khd->qhd", grad_s, k) * scale
-    grad_k = ein("hqk,qhd->khd", grad_s, q) * scale
-    grad_q = own(rope_back(grad_q, cosine, sine).astype(bf16).reshape(rows, held))
-    grad_k = own(rope_back(grad_k, cosine, sine).astype(bf16).reshape(rows, held))
-    grad_v = own(grad_v.reshape(rows, held))
-    normed1_part = (
-        ein("tc,dc->td", grad_q, attn_query)
-        + ein("tc,dc->td", grad_k, attn_key)
-        + ein("tc,dc->td", grad_v, attn_value)
-    )
-    grad_query = ein("td,tc->dc", normed1, grad_q)
-    grad_key = ein("td,tc->dc", normed1, grad_k)
-    grad_value = ein("td,tc->dc", normed1, grad_v)
-    grad_n1 = lax.psum_scatter(
-        normed1_part.astype(bf16), "hs", scatter_dimension=1, tiled=True
-    ).astype(f32)
-    x_own = quarter_of(x)
-    w1 = grad_n1 * lax.dynamic_slice_in_dim(attn_gain, col0, quarter, 0)
-    mean1 = lax.psum(jnp.sum(w1 * x_own, axis=-1, keepdims=True), "hs") / width
-    grad_tokens = quarter_of(grad_residual) + rms1 * w1 - x_own * rms1**3 * mean1
-    gain_own = jnp.sum(grad_n1 * x_own * rms1, axis=0)
-    gain_part = lax.dynamic_update_slice_in_dim(jnp.zeros((width,), f32), gain_own, col0, 0)
-    grad_attn_gain = lax.psum(gain_part, (*EP, "hs"))
+    grad_q = ein("hdk,hqk->hdq", k, grad_s) * scale
+    grad_k = ein("hdq,hqk->hdk", q, grad_s) * scale
+    grad_q = own(rope_back(grad_q, cosine, sine).astype(bf16).reshape(held, rows))
+    grad_k = own(rope_back(grad_k, cosine, sine).astype(bf16).reshape(held, rows))
+    grad_v = own(grad_v.reshape(held, rows))
+    low_own = quarter_of(grad_low).T
+    back_own = quarter_of(grad_residual).T
 
     def over_ep(a):
         return lax.psum(a.astype(bf16), EP).astype(f32)
 
+    if small:
+        grad_tokens, sums = finish(
+            grad_q,
+            grad_k,
+            grad_v,
+            low_own,
+            query_t,
+            key_t,
+            value_t,
+            normed1,
+            attended_t,
+            tokens.T,
+            attn_gain[:, None],
+            rms1.T,
+            back_own,
+            grad_router,
+            grad_ffn_gain[None, :],
+        )
+        sums = sums.astype(f32)
+        heads_sums = [sums[i * quarter : (i + 1) * quarter].T for i in range(4)]
+        rest = sums[4 * quarter :]
+        grad_router, grad_attn_gain, grad_ffn_gain = rest[:experts].T, rest[experts], rest[experts + 1]
+    else:
+        heads_sums = [
+            over_ep(dot(grad_q, normed1).T),
+            over_ep(dot(grad_k, normed1).T),
+            over_ep(dot(grad_v, normed1).T),
+            over_ep(ein("ct,dt->dc", low_own, attended_t)),
+        ]
+        part = (
+            ein("cd,ct->dt", query_t, grad_q)
+            + ein("cd,ct->dt", key_t, grad_k)
+            + ein("cd,ct->dt", value_t, grad_v)
+        )
+        grad_n1 = lax.psum_scatter(
+            part.astype(bf16), "hs", scatter_dimension=0, tiled=True
+        ).astype(f32)
+        x_own = quarter_of(x).T
+        w1 = grad_n1 * lax.dynamic_slice_in_dim(attn_gain, col0, quarter, 0)[:, None]
+        mean1 = lax.psum(jnp.sum(w1 * x_own, axis=0, keepdims=True), "hs") / width
+        rms_t = rms1.T
+        grad_tokens = back_own + rms_t * w1 - x_own * rms_t**3 * mean1
+        gain_own = jnp.sum(grad_n1 * x_own * rms_t, axis=1)
+        gain_part = lax.dynamic_update_slice_in_dim(jnp.zeros((width,), f32), gain_own, col0, 0)
+        grad_attn_gain = lax.psum(gain_part, (*EP, "hs"))
+        grad_ffn_gain = lax.psum(grad_ffn_gain, EP)
+        grad_router = over_ep(grad_router.T)
+
     return (
         output,
-        grad_tokens,
+        grad_tokens.T,
         grad_attn_gain,
-        over_ep(grad_query),
-        over_ep(grad_key),
-        over_ep(grad_value),
-        over_ep(grad_attn_out),
-        lax.psum(grad_ffn_gain, EP),
-        over_ep(grad_router),
-        over_ep(grad_shared_gate),
-        over_ep(grad_shared_up),
-        over_ep(grad_shared_down),
+        *heads_sums,
+        grad_ffn_gain,
+        grad_router,
+        shared_sums[0].T,
+        shared_sums[1].T,
+        shared_sums[2],
         grad_expert_gate,
         grad_expert_up,
         grad_expert_down,

time: 714 us -> 639 us (0.89)
  Pallas kernels: 374 us -> 459 us
  waiting for transfers between devices: 99.9 us -> 29.1 us
  blocking collectives: 63.1 us -> 0 us
  matrix products: 61.6 us -> 54 us
  other arithmetic: 40.2 us -> 32.8 us
    psum x1 -> x0, waiting for transfers between devices: 84.8 us -> none  [over_ep(): return lax.psum(a.astype(bf16), EP).astype(f32)]
    pallas_call x0 -> x1, Pallas kernels: none -> 83.2 us  [finish(): pl.pallas_call(finish_kernel, in_specs=[vmem] * len(args), out_specs=[vme...]
    psum x3 -> x0, blocking collectives: 63.1 us -> none  [the longest x1 41.2 us: shards(): grad_attn_gain = lax.psum(gain_part, (*EP, 'hs'))]
    reshape x1 -> x0, local copies, waits for them, and re-layouts: 14.3 us -> none  [shards(): out_part = collect(ex_out, slot).reshape(ep_count * rows, width)]
    reduce_scatter x0 -> x1, waiting for transfers between devices: none -> 14.2 us  [shards(): lax.psum_scatter(out_rows, 'hs', scatter_dimension=1, tiled=True)]
    dot_general x9 -> x5, matrix products: 19.7 us -> 9.43 us  [dot(): return jnp.dot(a, b, preferred_element_type=f32)]
    convert_element_type x11 -> x4, other arithmetic: 16.6 us -> 8.16 us  [the longest x2 5.25 us: shards(): back_rows, shared_sums = (back_rows.astype(f32), shared_sums.astype(f32))]
    unnamed x102 -> x78, local copies, waits for them, and re-layouts: 21 us -> 13.1 us
  transfers between devices with their start and end apart: 7 -> 5, of which waited for: 2 -> 2; matrix products, arithmetic and copies ran while one was open for 18% -> 17% of each run, Pallas kernels for 53% -> 60%
where the time goes in v4:
time: 639 us; the launch traced here: 629 us
  Pallas kernels  459 us (72%)
  matrix products  54 us (8%)
  local copies, waits for them, and re-layouts  39.4 us (6%)
  other arithmetic  32.8 us (5%)
  waiting for transfers between devices  29.1 us (5%)
  between operations  14.5 us (2%)
    pallas_call x1, Pallas kernels, collect_sum(): pl.pallas_call(collect_sum_kernel, in_specs=[pl.BlockSpec(memory_space=pl...  130 us
    pallas_call x1, Pallas kernels, gather_spread(): pl.pallas_call(gather_spread_kernel, in_specs=[vmem, vmem, vmem], out_spe...  88.8 us
    pallas_call x1, Pallas kernels, finish(): pl.pallas_call(finish_kernel, in_specs=[vmem] * len(args), out_specs=[vme...  83.2 us
    pallas_call x1, Pallas kernels, experts_backward(): pl.pallas_call(functools.partial(experts_backward_kernel, groups), grid=(...  48.2 us
    pallas_call x1, Pallas kernels, line_gather(): pl.pallas_call(line_gather_kernel, in_specs=[vmem], out_specs=vmem, out_s...  43.3 us
    dot_general x18, matrix products, ein(): return jnp.einsum(spec, a, b, preferred_element_type=f32)  39.9 us
    pallas_call x1, Pallas kernels, experts_forward(): pl.pallas_call(experts_forward_kernel, grid=(local, groups), in_specs=[sl...  31 us
    pallas_call x1, Pallas kernels, collect(): pl.pallas_call(kernel, grid=(s,), in_specs=in_specs, out_specs=pl.BlockSp...  17.4 us
  transfers between devices with their start and end apart: 5, of which 2 were waited for; matrix products, arithmetic and copies ran while one was open for 17% of the time, Pallas kernels for 60%

profile of v4, /device:TPU:9, one launch (start us, length us, event | category | flops | bytes accessed | tf_op | source)
XLA Modules:
  0.0 628.6 jit_solution(8818395497509856785)
XLA Ops:
  19.5 13.5 %collective-permute-done = bf16[192,1280]{1,0:T(8,128)(2,1)S(1)} collective-permute-done((bf16[192,1280]{1,0:T(8,128)(2,1)}, bf16[192,1280]{1,0:T(8,128)(2,1)S(1)}, u32[]{:S(2)}, u32[]{:S(2)}) %collective-permute-start) | collective-permute-done | bytes 491552 | tf_op jit(solution)/shard_map/ppermute | solution.py:980
  46.6 3.5 convolution_convert_fusion.6
  51.6 4.6 fusion.63
  59.3 43.3 %line_gather.1 = bf16[4,320,512]{2,1,0:T(8,128)(2,1)} custom-call(bf16[320,512]{1,0:T(8,128)(2,1)} %slice_select_fusion.3.own_ref), custom_call_target="tpu_custom_call" | custom-call | bytes 90000000 | tf_op jit(solution)/shard_map/line_gather/pallas_call | solution.py:571
  102.7 4.5 multiply_reduce_fusion.3
  110.4 88.8 %gather_spread.1 = (bf16[8,8,112,1280]{3,2,1,0:T(8,128)(2,1)}, f32[8,896,1]{2,1,0:T(8,128)}, s32[8,8,512]{2,1,0:T(8,128)}) custom-call(bf16[512,1280]{1,0:T(8,128)(2,1)} %copy.93.own_ref, bf16[64,512]{1,0:T(8,128)(2,1)} %fusion.13.slots_ref, bf16[64,1280]{1,0:T(8,128)(2,1)} %fusion.48.router_ref), custom_call_target="tpu_custom_call" | custom-call | bytes 186000000 | tf_op jit(solution)/shard_map/gather_spread/pallas_call | solution.py:527
  199.2 31.0 %experts_forward.1 = (bf16[8,8,112,1280]{3,2,1,0:T(8,128)(2,1)}, f32[8,896,256]{2,1,0:T(8,128)}, f32[8,896,256]{2,1,0:T(8,128)}) custom-call(bf16[8,8,112,1280]{3,2,1,0:T(8,128)(2,1)} %get-tuple-element.30.x_ref, f32[8,896,1]{2,1,0:T(8,128)} %get-tuple-element.31.sw_ref, bf16[8,224,1280]{2,1,0:T(8,128)(2,1)} %bitcast.105, bf16[8,224,1280]{2,1,0:T(8,128)(2,1)} %bitcast.107, ...), custom_call_target="tpu_custom_call" | custom-call | bytes 93000000 | tf_op jit(solution)/shard_map/experts_forward/pallas_call | solution.py:228
  230.2 17.4 %collect.1 = bf16[8,512,1280]{2,1,0:T(8,128)(2,1)} custom-call(bf16[8,8,112,1280]{3,2,1,0:T(8,128)(2,1)} %get-tuple-element.32.y_ref, s32[8,8,512]{2,1,0:T(8,128)} %get-tuple-element.33.slot_ref.refs_1_), custom_call_target="tpu_custom_call" | custom-call | bytes 51000000 | tf_op jit(solution)/shard_map/collect/pallas_call | solution.py:303
  252.0 3.1 fusion.66
  256.7 17.0 %spread.1.gx_ref = bf16[8,8,112,1280]{3,2,1,0:T(8,128)(2,1)} custom-call(bf16[8,1280,512]{2,1,0:T(8,128)(2,1)} %bitcast.109, s32[8,8,512]{2,1,0:T(8,128)} %get-tuple-element.33.slot_ref.refs_1_), custom_call_target="tpu_custom_call" | custom-call | bytes 51000000 | tf_op jit(solution)/shard_map/spread/pallas_call | solution.py:118
  273.7 48.2 %experts_backward.1 = (bf16[8,8,112,1280]{3,2,1,0:T(8,128)(2,1)}, f32[8,224,1280]{2,1,0:T(8,128)}, f32[8,224,1280]{2,1,0:T(8,128)}, f32[8,224,1280]{2,1,0:T(8,128)}, f32[8,896,1]{2,1,0:T(8,128)}) custom-call(bf16[8,8,112,1280]{3,2,1,0:T(8,128)(2,1)} %get-tuple-element.30.x_ref, bf16[8,8,112,1280]{3,2,1,0:T(8,128)(2,1)} %spread.1.gx_ref, ...), custom_call_target="tpu_custom_call" | custom-call | bytes 141000000 | tf_op jit(solution)/shard_map/experts_backward/pallas_call | solution.py:246
  321.9 3.0 multiply_convert_fusion.2
  324.9 3.3 convolution_convert_fusion.shared_down_ref
  335.5 129.8 %collect_sum.1 = (bf16[576,1280]{1,0:T(8,128)(2,1)}, bf16[1408,1280]{1,0:T(8,128)(2,1)}) custom-call(bf16[8,8,112,1280]{3,2,1,0:T(8,128)(2,1)} %get-tuple-element.36.y_ref, s32[8,8,512]{2,1,0:T(8,128)} %get-tuple-element.33.slot_ref.refs_1_, f32[8,896,1]{2,1,0:T(8,128)} %get-tuple-element.37.gsw_ref, f32[512,1280]{1,0:T(8,128)} %convolution_add_fusion.1.mine_ref, ...), custom_call_target="tpu_custom_call" | custom-call | bytes 393000000 | tf_op jit(solution)/shard_map/collect_sum/pallas_call | solution.py:761
  465.3 2.9 slice.188
  468.3 3.5 convert_element_type.123
  478.6 3.6 fusion.58
  482.2 2.9 convolution_convert_fusion.4
  492.5 3.4 fusion.1
  496.0 3.0 add_convert_fusion
  505.1 3.4 convolution_convert_fusion.3
  514.3 14.2 %reduce-scatter.5.cloned.1.call-done = bf16[512,320]{0,1:T(8,128)(2,1)} async-done(((bf16[512,1280]{0,1:T(8,128)(2,1)}), bf16[512,320]{0,1:T(8,128)(2,1)}) %reduce-scatter.5.cloned.1.call-update) | async-done | bytes 327696 | tf_op jit(solution)/shard_map/reduce_scatter | solution.py:1072
  530.9 83.2 %finish.1 = (f32[320,512]{1,0:T(8,128)}, bf16[1408,1280]{1,0:T(8,128)(2,1)}) custom-call(bf16[320,512]{1,0:T(8,128)(2,1)} %slice_select_fusion.2.dq_ref, bf16[320,512]{1,0:T(8,128)(2,1)} %get-tuple-element.93.dk_ref, bf16[320,512]{1,0:T(8,128)(2,1)} %get-tuple-element.92.dv_ref, bf16[320,512]{1,0:T(8,128)(2,1)} %dynamic-slice_bitcast_fusion.1.low_ref, ...), custom_call_target="tpu_custom_call" | custom-call | bytes 210000000 | tf_op jit(solution)/shard_map/finish/pallas_call | solution.py:912
  618.1 2.9 slice_bitcast_fusion.2
  (149 shorter events, 80.1 us)
Async XLA Ops:
  7.2 314.7 %copy-start = (bf16[448,1280]{1,0:T(8,128)(2,1)S(1)}, bf16[448,1280]{1,0:T(8,128)(2,1)}, u32[]{:S(2)}) copy-start(bf16[448,1280]{1,0:T(8,128)(2,1)} %param.27) | copy-start | bytes 3440644
  7.2 95.5 %all-gather.3.cloned.1.call-start = ((), (), s32[]{:S(2)}) async-start(), calls=%async_computation.2 | async-start | bytes 4096000 | tf_op jit(solution)/shard_map/all_gather | solution.py:994
  7.9 248.8 %all-gather.5.cloned.1.call-start = ((), (), s32[]{:S(2)}) async-start(), calls=%async_computation.5 | async-start | bytes 10813440 | tf_op jit(solution)/shard_map/all_gather | solution.py:995
  8.7 481.2 %reduce-scatter.3.cloned.1.call-start = ((), (), s32[]{:S(2)}) async-start(), calls=%async_computation.3 | async-start | bytes 11796480 | tf_op jit(solution)/shard_map/reduce_scatter | solution.py:1069
  9.8 4.6 copy-start.28
  12.6 20.3 %collective-permute-start = (bf16[192,1280]{1,0:T(8,128)(2,1)}, bf16[192,1280]{1,0:T(8,128)(2,1)S(1)}, u32[]{:S(2)}, u32[]{:S(2)}) collective-permute-start(bf16[192,1280]{1,0:T(8,128)(2,1)} %pad_maximum_fusion), channel_id=1, source_target_pairs={{0,1},{1,0},{2,3},{3,2},{4,5},{5,4},{6,7},{7,6},{8,9},{9,8},{10,11... | collective-permute-start | bytes 1474568 | tf_op jit(solution)/shard_map/ppermute | solution.py:980
  12.6 3.9 copy-start.29
  12.6 6.5 %copy-start.26 = (f32[1280]{0:T(1024)S(1)}, f32[1280]{0:T(1024)}, u32[]{:S(2)}) copy-start(f32[1280]{0:T(1024)} %param.18) | copy-start | bytes 15364
  14.3 88.4 %copy-start.1 = (bf16[512,1280]{0,1:T(8,128)(2,1)}, bf16[512,1280]{0,1:T(8,128)(2,1)S(1)}, u32[]{:S(2)}) copy-start(bf16[512,1280]{0,1:T(8,128)(2,1)S(1)} %copy.85) | copy-start | bytes 3932164
  14.9 18.9 %copy-start.27 = (f32[512]{0:T(512)}, f32[512]{0:T(512)S(1)}, u32[]{:S(2)}) copy-start(f32[512]{0:T(512)S(1)} %add_rsqrt_fusion.1) | copy-start | bytes 6148
  15.8 18.0 %copy-start.14 = (bf16[1280,320]{0,1:T(8,128)(2,1)S(1)}, bf16[1280,320]{0,1:T(8,128)(2,1)}, u32[]{:S(2)}) copy-start(bf16[1280,320]{0,1:T(8,128)(2,1)} %param.20) | copy-start | bytes 2457604
  19.1 31.0 %copy-start.11 = (f32[64,512]{0,1:T(8,128)}, f32[64,512]{0,1:T(8,128)S(1)}, u32[]{:S(2)}) copy-start(f32[64,512]{0,1:T(8,128)S(1)} %get-tuple-element.81) | copy-start | bytes 393220
  19.4 15.0 %copy-start.5 = (bf16[512,1280]{0,1:T(8,128)(2,1)}, bf16[512,1280]{0,1:T(8,128)(2,1)S(1)}, u32[]{:S(2)}) copy-start(bf16[512,1280]{0,1:T(8,128)(2,1)S(1)} %fusion.4) | copy-start | bytes 3932164
  46.6 3.5 copy-start.7
  46.6 3.5 copy-start.8
  46.6 3.5 copy-start.9
  46.6 3.5 copy-start.12
  51.6 4.6 copy-start.30
  102.7 6.0 copy-start.25
  247.6 3.6 copy-start.23
  247.7 280.8 %reduce-scatter.5.cloned.1.call-start = ((), (), s32[]{:S(2)}) async-start(), calls=%async_computation.4 | async-start | bytes 1638400 | tf_op jit(solution)/shard_map/reduce_scatter | solution.py:1072
  482.2 3.6 copy-start.13
  504.3 7.5 %slice-start = ((s8[7208960]{0:T(1024)(128)(4,1)}), s8[4194304]{0:T(1024)(128)(4,1)S(1)}, s32[]{:S(2)}) async-start(s8[7208960]{0:T(1024)(128)(4,1)} %bitcast.103), calls=%async_computation.6 | async-start | bytes 8388608
  505.1 6.7 %slice-start.1 = ((s8[7208960]{0:T(1024)(128)(4,1)}), s8[3014656]{0:T(1024)(128)(4,1)S(1)}, s32[]{:S(2)}) async-start(s8[7208960]{0:T(1024)(128)(4,1)} %bitcast.103), calls=%async_computation.7 | async-start | bytes 6029312
  (17 other events, 34.9 us)
Sparse Core Ops, SparseCore 0:
  9.6 74.2 all-gather.2
  86.7 116.9 all-gather.4
  247.8 79.2 reduce-scatter.2
  496.1 32.3 reduce-scatter.4
